TPU v7x, 512 devices: a whole 4x4x16 slice. The times are simulated.
512 devices in a mesh: dp: 32 (over y, z_lo), ctx: 16 (over x, z_hi, core).
Axes of the slice: x: 4, y: 4, z: 16 (z_hi: 2, z_lo: 8; z = z_hi * 8 + z_lo), core: 2. Of those that a mesh axis runs over, the one named last changes fastest.
Arguments:
- projected: bfloat16 [65536, 2048], P(('dp', 'ctx')), may hold values from -6 to 6
- destination: int32 [16, 4096], P('ctx'), may hold values from 0 to 4095, as said below
- lengths: int32 [32, 3], P('dp'), may hold values from 1 to 1088, 1730 in all within a row
- grad_out: bfloat16 [65536, 512], P(('dp', 'ctx')), may hold values from -6 to 6
Outputs:
- layer_output: bfloat16 [65536, 512], P(('dp', 'ctx'))
- grad_projected: bfloat16 [65536, 2048], P(('dp', 'ctx'))
Inputs may be any that keep to these rules, and one draw needn't show every extreme that they name: `destination`: row c maps the loader rows of ctx index c: entry i * 128 + r is m when row r of loader dp index i becomes row m % 128 of owner dp index m // 128. Each row is a permutation of 0 to 4095. From each loader device at most 8 rows go to one owner device, and exactly 8 to one of them. Row g holds the lengths of the 3 users of group g in packing order; they sum to 1730, and the longest is exactly 1088.
All inputs are finite; a program needn't handle non-finite values.
Results may differ from a plain program's by a relative error of at most 0.0085.
Values may be sent and summed in bfloat16 or wider, within the bound.
No kernel may reach another device: no remote copies, remote signals or barrier semaphores. Data moves between devices by JAX's collectives and lax.ppermute only.
A program may use at most 64 MiB of HBM per device.

v0:
```python
import jax
import jax.numpy as jnp
from jax import lax
from jax.sharding import PartitionSpec as P

HEAD_DIM = 128
BLOCK = 128
USERS = 3


EPSILON = 1e-06


def from_behind(array, axis, by):
    peers = lax.axis_size(axis)
    return lax.ppermute(array, axis, [(i, (i + by) % peers) for i in range(peers)])


def user_layout(positions, lengths_row):
    padded = (lengths_row + BLOCK - 1) // BLOCK * BLOCK
    starts = jnp.cumsum(padded) - padded
    ends = starts + lengths_row
    inside = (positions[:, None] >= starts[None, :]) & (positions[:, None] < ends[None, :])
    active = jnp.any(inside, axis=1)
    user_ids = jnp.sum(jnp.where(inside, jnp.arange(USERS, dtype=jnp.int32)[None, :], 0), axis=1)
    return (user_ids, active)


def pair_mask(query_pos, query_user, query_live, key_pos, key_user, key_live):
    allowed = (query_user[:, None] == key_user[None, :]) & query_live[:, None] & key_live[None, :]
    allowed = allowed & (key_pos[None, :] <= query_pos[:, None])
    return allowed.astype(jnp.float32)


def body(projected, destination, lengths, grad_out):
    dp_count = lax.axis_size("dp")
    ctx_count = lax.axis_size("ctx")
    dp_index = lax.axis_index("dp")
    ctx_index = lax.axis_index("ctx")
    row_count = projected.shape[0]
    features = projected.shape[1]
    model_width = grad_out.shape[1]
    head_count = model_width // HEAD_DIM
    capacity = 2 * row_count // dp_count
    score_scale = HEAD_DIM ** (-0.5)
    mapping = destination[0]
    my_targets = lax.dynamic_slice_in_dim(mapping, dp_index * row_count, row_count)
    owners = my_targets // row_count
    picked = (owners[:, None] == jnp.arange(dp_count, dtype=jnp.int32)[None, :]).astype(jnp.int32)
    out_slots = jnp.sum(jnp.cumsum(picked, axis=0) * picked, axis=1) - 1
    outgoing = (
        jnp.zeros((dp_count, capacity, features), jnp.bfloat16).at[owners, out_slots].set(projected)
    )
    arrived = lax.all_to_all(outgoing, "dp", split_axis=0, concat_axis=0, tiled=True)
    mapping_grid = mapping.reshape(dp_count, row_count)
    landing = mapping_grid // row_count == dp_index
    in_slots = jnp.cumsum(landing.astype(jnp.int32), axis=1) - 1
    landing_rows = jnp.where(landing, mapping_grid % row_count, row_count).reshape(-1)
    senders = jnp.broadcast_to(
        jnp.arange(dp_count, dtype=jnp.int32)[:, None], (dp_count, row_count)
    ).reshape(-1)
    from_sender = jnp.zeros((row_count,), jnp.int32).at[landing_rows].set(senders, mode="drop")
    from_slot = (
        jnp.zeros((row_count,), jnp.int32).at[landing_rows].set(in_slots.reshape(-1), mode="drop")
    )
    owned_rows = arrived[from_sender, from_slot]

    def split_heads(matrix):
        return matrix.reshape(matrix.shape[0], head_count, HEAD_DIM)

    gating = owned_rows[:, 0:model_width]
    values = owned_rows[:, model_width : 2 * model_width]
    queries = split_heads(owned_rows[:, 2 * model_width : 3 * model_width])
    key_rows = owned_rows[:, 3 * model_width : 4 * model_width]
    lengths_row = lengths[0]
    my_pos = ctx_index * row_count + jnp.arange(row_count, dtype=jnp.int32)
    my_user, my_live = user_layout(my_pos, lengths_row)
    empty_rows = jnp.zeros((row_count, head_count, HEAD_DIM), jnp.float32)
    piece_keys = lax.all_gather(key_rows, "ctx", axis=0, tiled=True)
    piece_values = lax.all_gather(values, "ctx", axis=0, tiled=True)
    piece_rows = piece_keys.shape[0]
    key_pos = jnp.arange(piece_rows, dtype=jnp.int32)
    key_user, key_live = user_layout(key_pos, lengths_row)
    allowed = pair_mask(my_pos, my_user, my_live, key_pos, key_user, key_live)
    scores = (
        jnp.einsum(
            "qhd,khd->hqk", queries, split_heads(piece_keys), preferred_element_type=jnp.float32
        )
        * score_scale
    )
    weights = (jax.nn.silu(scores) * allowed[None]).astype(jnp.bfloat16)
    mixed_sum = jnp.einsum(
        "hqk,khd->qhd", weights, split_heads(piece_values), preferred_element_type=jnp.float32
    )
    center = mixed_sum - jnp.mean(mixed_sum, axis=-1, keepdims=True)
    inverse = lax.rsqrt(jnp.mean(center * center, axis=-1, keepdims=True) + EPSILON)
    normed = center * inverse
    gating_heads = split_heads(gating).astype(jnp.float32)
    layer_output = (normed * gating_heads).astype(jnp.bfloat16).reshape(row_count, model_width)
    upstream = split_heads(grad_out).astype(jnp.float32)
    grad_gating = upstream * normed
    grad_normed = upstream * gating_heads
    grad_mixed = (
        (
            grad_normed
            - jnp.mean(grad_normed, axis=-1, keepdims=True)
            - normed * jnp.mean(grad_normed * normed, axis=-1, keepdims=True)
        )
        * inverse
    ).astype(jnp.bfloat16)
    my_keys = split_heads(key_rows)
    my_values = split_heads(values)

    def pair_terms(panel_queries, panel_grads, query_pos):
        query_user, query_live = user_layout(query_pos, lengths_row)
        allowed = pair_mask(query_pos, query_user, query_live, my_pos, my_user, my_live)
        scores = (
            jnp.einsum("qhd,khd->hqk", panel_queries, my_keys, preferred_element_type=jnp.float32)
            * score_scale
        )
        weights = (jax.nn.silu(scores) * allowed[None]).astype(jnp.bfloat16)
        grad_weights = jnp.einsum(
            "qhd,khd->hqk", panel_grads, my_values, preferred_element_type=jnp.float32
        )
        sigmoid_part = jax.nn.sigmoid(scores)
        grad_scores = (
            grad_weights * allowed[None] * sigmoid_part * (1.0 + scores * (1.0 - sigmoid_part))
        ).astype(jnp.bfloat16)
        term_q = jnp.einsum(
            "hqk,khd->qhd", grad_scores, my_keys, preferred_element_type=jnp.float32
        )
        term_k = jnp.einsum(
            "hqk,qhd->khd", grad_scores, panel_queries, preferred_element_type=jnp.float32
        )
        term_v = jnp.einsum(
            "hqk,qhd->khd", weights, panel_grads, preferred_element_type=jnp.float32
        )
        return (term_q, term_k, term_v)

    def pass_on(grad_acc):
        return from_behind(grad_acc.astype(jnp.bfloat16), "ctx", 1).astype(grad_acc.dtype)

    def contribute(rotation, panels, grad_acc, acc_keys, acc_values):
        source = (ctx_index - rotation) % ctx_count
        query_pos = source * row_count + jnp.arange(row_count, dtype=jnp.int32)
        term_q, term_k, term_v = pair_terms(panels[0], panels[1], query_pos)
        return (pass_on(grad_acc + term_q), acc_keys + term_k, acc_values + term_v)

    def cycle_turn(rotation, cycle_state):
        panels, grad_acc, acc_keys, acc_values = cycle_state
        grad_acc, acc_keys, acc_values = contribute(
            rotation, panels, grad_acc, acc_keys, acc_values
        )
        panels = from_behind(panels, "ctx", 1)
        return (panels, grad_acc, acc_keys, acc_values)

    start_panels = jnp.stack([queries, grad_mixed])
    cycle_state = lax.fori_loop(
        0, ctx_count - 1, cycle_turn, (start_panels, empty_rows, empty_rows, empty_rows)
    )
    grad_queries, grad_keys, grad_values = contribute(ctx_count - 1, *cycle_state)
    grad_local = jnp.concatenate(
        [
            grad_gating.reshape(row_count, model_width),
            grad_values.reshape(row_count, model_width),
            (grad_queries * score_scale).reshape(row_count, model_width),
            (grad_keys * score_scale).reshape(row_count, model_width),
        ],
        axis=1,
    ).astype(jnp.bfloat16)
    returning = (
        jnp.zeros((dp_count, capacity, features), jnp.bfloat16)
        .at[from_sender, from_slot]
        .set(grad_local)
    )
    returned = lax.all_to_all(returning, "dp", split_axis=0, concat_axis=0, tiled=True)
    grad_projected = returned[owners, out_slots]
    return (layer_output, grad_projected)


def solution(mesh):
    in_specs = (P(("dp", "ctx"), None), P("ctx", None), P("dp", None), P(("dp", "ctx"), None))
    out_specs = (P(("dp", "ctx"), None), P(("dp", "ctx"), None))
    return jax.shard_map(body, mesh=mesh, in_specs=in_specs, out_specs=out_specs, check_vma=False)
```

profile of v0, /device:TPU:38, one launch (start us, length us, event | category | flops | bytes accessed | tf_op | source)
XLA Modules:
  0.0 734.6 jit_solution(16223004948521338735)
XLA Ops:
  10.1 23.6 %scatter_fusion = bf16[32,8,2048]{2,1,0:T(8,128)(2,1)} fusion(bf16[32,8,2048]{2,1,0:T(8,128)(2,1)} %broadcast.1029.clone, s32[128]{0:T(128)S(1)} %fusion.54, bf16[128,2048]{1,0:T(8,128)(2,1)} %param.6), kind=kCustom, calls=%fused_computation.2 | custom fusion | bytes 1573888 | tf_op jit(solution)/shard_map/scatter | solution.py:52
  33.7 15.6 %all-to-all-start = ((bf16[32,8,2048]{2,1,0:T(8,128)(2,1)}), bf16[32,8,2048]{2,1,0:T(8,128)(2,1)S(1)}, u32[]{:S(2)}, u32[]{:S(2)}) async-start(bf16[32,8,2048]{2,1,0:T(8,128)(2,1)} %scatter_fusion), calls=%async_computation | async-start | bytes 2097152 | tf_op jit(solution)/shard_map/all_to_all | solution.py:54
  49.8 15.5 %scatter_custom_fusion.2 = s32[128]{0:T(128)S(1)} fusion(s32[4096]{0:T(1024)S(1)} %bitcast.228, s32[4096]{0:T(1024)S(1)} %add_bitcast_fusion, s32[]{:T(128)} %constant.264.clone.1), kind=kCustom, calls=%fused_computation.159 | custom fusion | bytes 516 | tf_op jit(solution)/shard_map/scatter | solution.py:64
  65.3 15.5 %scatter_custom_fusion.1 = s32[128]{0:T(128)S(1)} fusion(s32[4096]{0:T(1024)S(1)} %bitcast.229, s32[4096]{0:T(1024)S(1)} %iota_bitcast_fusion, s32[]{:T(128)} %constant.264.clone.1), kind=kCustom, calls=%fused_computation.161 | custom fusion | bytes 516 | tf_op jit(solution)/shard_map/scatter | solution.py:62
  80.8 20.1 %all-to-all-done = bf16[32,8,2048]{2,1,0:T(8,128)(2,1)S(1)} async-done(((bf16[32,8,2048]{2,1,0:T(8,128)(2,1)}), bf16[32,8,2048]{2,1,0:T(8,128)(2,1)S(1)}, u32[]{:S(2)}, u32[]{:S(2)}) %all-to-all-start) | async-done | bytes 1048608 | tf_op jit(solution)/shard_map/all_to_all | solution.py:54
  111.4 73.1 %all-gather.3.cloned.1.call-done = bf16[2048,512]{1,0:T(8,128)(2,1)} async-done(((bf16[128,512]{1,0:T(8,128)(2,1)}), bf16[2048,512]{1,0:T(8,128)(2,1)}) %all-gather.3.cloned.1.call-update) | async-done | bytes 2097168 | tf_op jit(solution)/shard_map/all_gather | solution.py:80
  187.4 83.9 %all-gather.5.cloned.1.call-done = bf16[2048,512]{1,0:T(8,128)(2,1)} async-done(((bf16[128,512]{1,0:T(8,128)(2,1)}), bf16[2048,512]{1,0:T(8,128)(2,1)}) %all-gather.5.cloned.1.call-update) | async-done | bytes 2097168 | tf_op jit(solution)/shard_map/all_gather | solution.py:79
  282.3 323.3 %while.25 = (s32[]{:T(128)}, bf16[2,128,4,128]{3,1,2,0:T(8,128)(2,1)S(1)}, f32[128,4,128]{2,0,1:T(8,128)S(1)}, f32[128,4,128]{2,0,1:T(8,128)S(1)}, f32[128,4,128...) while((s32[]{:T(128)}, ...), condition=%wide.region_19.20_spmd.clone, body=%wide.region_15.19_spmd.clone.sunk | while | flops 85625200 | bytes 6231682 | solution.py:158
  293.3 11.1 %collective-permute-done.1 = bf16[128,4,128]{2,0,1:T(8,128)(2,1)S(1)} collective-permute-done((bf16[128,4,128]{2,0,1:T(8,128)(2,1)S(1)}, bf16[128,4,128]{2,0,1:T(8,128)(2,1)S(1)}, u32[]{:S(2)}, u32[]{:S(2)}) %collective-permute-start.1) | collective-permute-done | bytes 131104 | tf_op jit(solution)/shard_map/while/body/eval_jaxpr/ppermute | solution.py:16
  311.7 11.9 %collective-permute-done.1 = bf16[128,4,128]{2,0,1:T(8,128)(2,1)S(1)} collective-permute-done((bf16[128,4,128]{2,0,1:T(8,128)(2,1)S(1)}, bf16[128,4,128]{2,0,1:T(8,128)(2,1)S(1)}, u32[]{:S(2)}, u32[]{:S(2)}) %collective-permute-start.1) | collective-permute-done | bytes 131104 | tf_op jit(solution)/shard_map/while/body/eval_jaxpr/ppermute | solution.py:16
  368.0 11.4 %collective-permute-start.1 = (bf16[128,4,128]{2,0,1:T(8,128)(2,1)S(1)}, bf16[128,4,128]{2,0,1:T(8,128)(2,1)S(1)}, u32[]{:S(2)}, u32[]{:S(2)}) collective-permute-start(bf16[128,4,128]{2,0,1:T(8,128)(2,1)S(1)} %fusion.114), channel_id=1, source_target_pairs={{0,1},{1,2},{2,3},{3,4},{4,5},{5,6},{6,7},{7,8},{8,9},{9,10},{10,1... | collective-permute-start | bytes 393224 | tf_op jit(solution)/shard_map/while/body/eval_jaxpr/ppermute | solution.py:16
  411.3 11.4 %collective-permute-start.1 = (bf16[128,4,128]{2,0,1:T(8,128)(2,1)S(1)}, bf16[128,4,128]{2,0,1:T(8,128)(2,1)S(1)}, u32[]{:S(2)}, u32[]{:S(2)}) collective-permute-start(bf16[128,4,128]{2,0,1:T(8,128)(2,1)S(1)} %fusion.114), channel_id=1, source_target_pairs={{0,1},{1,2},{2,3},{3,4},{4,5},{5,6},{6,7},{7,8},{8,9},{9,10},{10,1... | collective-permute-start | bytes 393224 | tf_op jit(solution)/shard_map/while/body/eval_jaxpr/ppermute | solution.py:16
  463.8 11.9 %collective-permute-done.1 = bf16[128,4,128]{2,0,1:T(8,128)(2,1)S(1)} collective-permute-done((bf16[128,4,128]{2,0,1:T(8,128)(2,1)S(1)}, bf16[128,4,128]{2,0,1:T(8,128)(2,1)S(1)}, u32[]{:S(2)}, u32[]{:S(2)}) %collective-permute-start.1) | collective-permute-done | bytes 131104 | tf_op jit(solution)/shard_map/while/body/eval_jaxpr/ppermute | solution.py:16
  482.4 12.4 %collective-permute-done.1 = bf16[128,4,128]{2,0,1:T(8,128)(2,1)S(1)} collective-permute-done((bf16[128,4,128]{2,0,1:T(8,128)(2,1)S(1)}, bf16[128,4,128]{2,0,1:T(8,128)(2,1)S(1)}, u32[]{:S(2)}, u32[]{:S(2)}) %collective-permute-start.1) | collective-permute-done | bytes 131104 | tf_op jit(solution)/shard_map/while/body/eval_jaxpr/ppermute | solution.py:16
  508.1 10.9 %collective-permute-done.1 = bf16[128,4,128]{2,0,1:T(8,128)(2,1)S(1)} collective-permute-done((bf16[128,4,128]{2,0,1:T(8,128)(2,1)S(1)}, bf16[128,4,128]{2,0,1:T(8,128)(2,1)S(1)}, u32[]{:S(2)}, u32[]{:S(2)}) %collective-permute-start.1) | collective-permute-done | bytes 131104 | tf_op jit(solution)/shard_map/while/body/eval_jaxpr/ppermute | solution.py:16
  528.5 9.6 %collective-permute-done.1 = bf16[128,4,128]{2,0,1:T(8,128)(2,1)S(1)} collective-permute-done((bf16[128,4,128]{2,0,1:T(8,128)(2,1)S(1)}, bf16[128,4,128]{2,0,1:T(8,128)(2,1)S(1)}, u32[]{:S(2)}, u32[]{:S(2)}) %collective-permute-start.1) | collective-permute-done | bytes 131104 | tf_op jit(solution)/shard_map/while/body/eval_jaxpr/ppermute | solution.py:16
  541.2 9.6 %collective-permute-start.1 = (bf16[128,4,128]{2,0,1:T(8,128)(2,1)S(1)}, bf16[128,4,128]{2,0,1:T(8,128)(2,1)S(1)}, u32[]{:S(2)}, u32[]{:S(2)}) collective-permute-start(bf16[128,4,128]{2,0,1:T(8,128)(2,1)S(1)} %fusion.114), channel_id=1, source_target_pairs={{0,1},{1,2},{2,3},{3,4},{4,5},{5,6},{6,7},{7,8},{8,9},{9,10},{10,1... | collective-permute-start | bytes 393224 | tf_op jit(solution)/shard_map/while/body/eval_jaxpr/ppermute | solution.py:16
  551.4 10.9 %collective-permute-done.1 = bf16[128,4,128]{2,0,1:T(8,128)(2,1)S(1)} collective-permute-done((bf16[128,4,128]{2,0,1:T(8,128)(2,1)S(1)}, bf16[128,4,128]{2,0,1:T(8,128)(2,1)S(1)}, u32[]{:S(2)}, u32[]{:S(2)}) %collective-permute-start.1) | collective-permute-done | bytes 131104 | tf_op jit(solution)/shard_map/while/body/eval_jaxpr/ppermute | solution.py:16
  571.9 9.6 %collective-permute-done.1 = bf16[128,4,128]{2,0,1:T(8,128)(2,1)S(1)} collective-permute-done((bf16[128,4,128]{2,0,1:T(8,128)(2,1)S(1)}, bf16[128,4,128]{2,0,1:T(8,128)(2,1)S(1)}, u32[]{:S(2)}, u32[]{:S(2)}) %collective-permute-start.1) | collective-permute-done | bytes 131104 | tf_op jit(solution)/shard_map/while/body/eval_jaxpr/ppermute | solution.py:16
  594.7 10.9 %collective-permute-done.1 = bf16[128,4,128]{2,0,1:T(8,128)(2,1)S(1)} collective-permute-done((bf16[128,4,128]{2,0,1:T(8,128)(2,1)S(1)}, bf16[128,4,128]{2,0,1:T(8,128)(2,1)S(1)}, u32[]{:S(2)}, u32[]{:S(2)}) %collective-permute-start.1) | collective-permute-done | bytes 131104 | tf_op jit(solution)/shard_map/while/body/eval_jaxpr/ppermute | solution.py:16
  609.7 13.4 %collective-permute-done.2 = bf16[128,4,128]{0,2,1:T(8,128)(2,1)S(1)} collective-permute-done((bf16[128,4,128]{0,2,1:T(8,128)(2,1)S(1)}, bf16[128,4,128]{0,2,1:T(8,128)(2,1)S(1)}, u32[]{:S(2)}, u32[]{:S(2)}) %collective-permute-start.2) | collective-permute-done | bytes 131104 | tf_op jit(solution)/shard_map/ppermute | solution.py:16
  624.4 22.7 %scatter_fusion.1 = bf16[32,8,2048]{2,1,0:T(8,128)(2,1)} fusion(bf16[32,8,2048]{2,1,0:T(8,128)(2,1)} %broadcast.1029, s32[128]{0:T(128)S(1)} %get-tuple-element.554, bf16[128,2048]{1,0:T(8,128)(2,1)S(1)} %pad_maximum_fusion), kind=kCustom, calls=%fused_computation.5 | custom fusion | bytes 1573888 | tf_op jit(solution)/shard_map/scatter | solution.py:174
  647.1 26.3 %all-to-all-start.1 = ((bf16[32,8,2048]{2,1,0:T(8,128)(2,1)}), bf16[32,8,2048]{2,1,0:T(8,128)(2,1)S(1)}, u32[]{:S(2)}, u32[]{:S(2)}) async-start(bf16[32,8,2048]{2,1,0:T(8,128)(2,1)} %scatter_fusion.1), calls=%async_computation.1 | async-start | bytes 2097152 | tf_op jit(solution)/shard_map/all_to_all | solution.py:176
  674.2 50.4 %all-to-all-done.1 = bf16[32,8,2048]{2,1,0:T(8,128)(2,1)S(1)} async-done(((bf16[32,8,2048]{2,1,0:T(8,128)(2,1)}), bf16[32,8,2048]{2,1,0:T(8,128)(2,1)S(1)}, u32[]{:S(2)}, u32[]{:S(2)}) %all-to-all-start.1) | async-done | bytes 1048608 | tf_op jit(solution)/shard_map/all_to_all | solution.py:176
  (362 shorter events, 226.5 us)
Async XLA Ops:
  33.7 67.2 %all-to-all-start = ((bf16[32,8,2048]{2,1,0:T(8,128)(2,1)}), bf16[32,8,2048]{2,1,0:T(8,128)(2,1)S(1)}, u32[]{:S(2)}, u32[]{:S(2)}) async-start(bf16[32,8,2048]{2,1,0:T(8,128)(2,1)} %scatter_fusion), calls=%async_computation | async-start | bytes 2097152 | tf_op jit(solution)/shard_map/all_to_all | solution.py:54
  49.3 135.2 %all-gather.3.cloned.1.call-start = ((), (), s32[]{:S(2)}) async-start(), calls=%async_computation.2 | async-start | bytes 2228224 | tf_op jit(solution)/shard_map/all_gather | solution.py:80
  104.1 167.1 %all-gather.5.cloned.1.call-start = ((), (), s32[]{:S(2)}) async-start(), calls=%async_computation.3 | async-start | bytes 2228224 | tf_op jit(solution)/shard_map/all_gather | solution.py:79
  282.4 22.1 %collective-permute-start = (bf16[2,128,4,128]{3,1,2,0:T(8,128)(2,1)S(1)}, bf16[2,128,4,128]{3,1,2,0:T(8,128)(2,1)S(1)}, u32[]{:S(2)}, u32[]{:S(2)}) collective-permute-start(bf16[2,128,4,128]{3,1,2,0:T(8,128)(2,1)S(1)} %copy.96), channel_id=1, source_target_pairs={{0,1},{1,2},{2,3},{3,4},{4,5},{5,6},{6,7},{7,8},{8,9},{9,10},{10,1... | collective-permute-start | bytes 786440 | tf_op jit(solution)/shard_map/while/body/eval_jaxpr/ppermute | solution.py:16
  304.5 19.1 %collective-permute-start = (bf16[2,128,4,128]{3,1,2,0:T(8,128)(2,1)S(1)}, bf16[2,128,4,128]{3,1,2,0:T(8,128)(2,1)S(1)}, u32[]{:S(2)}, u32[]{:S(2)}) collective-permute-start(bf16[2,128,4,128]{3,1,2,0:T(8,128)(2,1)S(1)} %copy.96), channel_id=1, source_target_pairs={{0,1},{1,2},{2,3},{3,4},{4,5},{5,6},{6,7},{7,8},{8,9},{9,10},{10,1... | collective-permute-start | bytes 786440 | tf_op jit(solution)/shard_map/while/body/eval_jaxpr/ppermute | solution.py:16
  323.7 22.0 %collective-permute-start = (bf16[2,128,4,128]{3,1,2,0:T(8,128)(2,1)S(1)}, bf16[2,128,4,128]{3,1,2,0:T(8,128)(2,1)S(1)}, u32[]{:S(2)}, u32[]{:S(2)}) collective-permute-start(bf16[2,128,4,128]{3,1,2,0:T(8,128)(2,1)S(1)} %copy.96), channel_id=1, source_target_pairs={{0,1},{1,2},{2,3},{3,4},{4,5},{5,6},{6,7},{7,8},{8,9},{9,10},{10,1... | collective-permute-start | bytes 786440 | tf_op jit(solution)/shard_map/while/body/eval_jaxpr/ppermute | solution.py:16
  345.7 19.2 %collective-permute-start = (bf16[2,128,4,128]{3,1,2,0:T(8,128)(2,1)S(1)}, bf16[2,128,4,128]{3,1,2,0:T(8,128)(2,1)S(1)}, u32[]{:S(2)}, u32[]{:S(2)}) collective-permute-start(bf16[2,128,4,128]{3,1,2,0:T(8,128)(2,1)S(1)} %copy.96), channel_id=1, source_target_pairs={{0,1},{1,2},{2,3},{3,4},{4,5},{5,6},{6,7},{7,8},{8,9},{9,10},{10,1... | collective-permute-start | bytes 786440 | tf_op jit(solution)/shard_map/while/body/eval_jaxpr/ppermute | solution.py:16
  364.9 24.1 %collective-permute-start = (bf16[2,128,4,128]{3,1,2,0:T(8,128)(2,1)S(1)}, bf16[2,128,4,128]{3,1,2,0:T(8,128)(2,1)S(1)}, u32[]{:S(2)}, u32[]{:S(2)}) collective-permute-start(bf16[2,128,4,128]{3,1,2,0:T(8,128)(2,1)S(1)} %copy.96), channel_id=1, source_target_pairs={{0,1},{1,2},{2,3},{3,4},{4,5},{5,6},{6,7},{7,8},{8,9},{9,10},{10,1... | collective-permute-start | bytes 786440 | tf_op jit(solution)/shard_map/while/body/eval_jaxpr/ppermute | solution.py:16
  368.0 21.1 %collective-permute-start.1 = (bf16[128,4,128]{2,0,1:T(8,128)(2,1)S(1)}, bf16[128,4,128]{2,0,1:T(8,128)(2,1)S(1)}, u32[]{:S(2)}, u32[]{:S(2)}) collective-permute-start(bf16[128,4,128]{2,0,1:T(8,128)(2,1)S(1)} %fusion.114), channel_id=1, source_target_pairs={{0,1},{1,2},{2,3},{3,4},{4,5},{5,6},{6,7},{7,8},{8,9},{9,10},{10,1... | collective-permute-start | bytes 393224 | tf_op jit(solution)/shard_map/while/body/eval_jaxpr/ppermute | solution.py:16
  389.1 19.1 %collective-permute-start = (bf16[2,128,4,128]{3,1,2,0:T(8,128)(2,1)S(1)}, bf16[2,128,4,128]{3,1,2,0:T(8,128)(2,1)S(1)}, u32[]{:S(2)}, u32[]{:S(2)}) collective-permute-start(bf16[2,128,4,128]{3,1,2,0:T(8,128)(2,1)S(1)} %copy.96), channel_id=1, source_target_pairs={{0,1},{1,2},{2,3},{3,4},{4,5},{5,6},{6,7},{7,8},{8,9},{9,10},{10,1... | collective-permute-start | bytes 786440 | tf_op jit(solution)/shard_map/while/body/eval_jaxpr/ppermute | solution.py:16
  408.2 24.1 %collective-permute-start = (bf16[2,128,4,128]{3,1,2,0:T(8,128)(2,1)S(1)}, bf16[2,128,4,128]{3,1,2,0:T(8,128)(2,1)S(1)}, u32[]{:S(2)}, u32[]{:S(2)}) collective-permute-start(bf16[2,128,4,128]{3,1,2,0:T(8,128)(2,1)S(1)} %copy.96), channel_id=1, source_target_pairs={{0,1},{1,2},{2,3},{3,4},{4,5},{5,6},{6,7},{7,8},{8,9},{9,10},{10,1... | collective-permute-start | bytes 786440 | tf_op jit(solution)/shard_map/while/body/eval_jaxpr/ppermute | solution.py:16
  411.3 21.1 %collective-permute-start.1 = (bf16[128,4,128]{2,0,1:T(8,128)(2,1)S(1)}, bf16[128,4,128]{2,0,1:T(8,128)(2,1)S(1)}, u32[]{:S(2)}, u32[]{:S(2)}) collective-permute-start(bf16[128,4,128]{2,0,1:T(8,128)(2,1)S(1)} %fusion.114), channel_id=1, source_target_pairs={{0,1},{1,2},{2,3},{3,4},{4,5},{5,6},{6,7},{7,8},{8,9},{9,10},{10,1... | collective-permute-start | bytes 393224 | tf_op jit(solution)/shard_map/while/body/eval_jaxpr/ppermute | solution.py:16
  432.4 19.1 %collective-permute-start = (bf16[2,128,4,128]{3,1,2,0:T(8,128)(2,1)S(1)}, bf16[2,128,4,128]{3,1,2,0:T(8,128)(2,1)S(1)}, u32[]{:S(2)}, u32[]{:S(2)}) collective-permute-start(bf16[2,128,4,128]{3,1,2,0:T(8,128)(2,1)S(1)} %copy.96), channel_id=1, source_target_pairs={{0,1},{1,2},{2,3},{3,4},{4,5},{5,6},{6,7},{7,8},{8,9},{9,10},{10,1... | collective-permute-start | bytes 786440 | tf_op jit(solution)/shard_map/while/body/eval_jaxpr/ppermute | solution.py:16
  451.6 24.1 %collective-permute-start = (bf16[2,128,4,128]{3,1,2,0:T(8,128)(2,1)S(1)}, bf16[2,128,4,128]{3,1,2,0:T(8,128)(2,1)S(1)}, u32[]{:S(2)}, u32[]{:S(2)}) collective-permute-start(bf16[2,128,4,128]{3,1,2,0:T(8,128)(2,1)S(1)} %copy.96), channel_id=1, source_target_pairs={{0,1},{1,2},{2,3},{3,4},{4,5},{5,6},{6,7},{7,8},{8,9},{9,10},{10,1... | collective-permute-start | bytes 786440 | tf_op jit(solution)/shard_map/while/body/eval_jaxpr/ppermute | solution.py:16
  454.6 21.1 %collective-permute-start.1 = (bf16[128,4,128]{2,0,1:T(8,128)(2,1)S(1)}, bf16[128,4,128]{2,0,1:T(8,128)(2,1)S(1)}, u32[]{:S(2)}, u32[]{:S(2)}) collective-permute-start(bf16[128,4,128]{2,0,1:T(8,128)(2,1)S(1)} %fusion.114), channel_id=1, source_target_pairs={{0,1},{1,2},{2,3},{3,4},{4,5},{5,6},{6,7},{7,8},{8,9},{9,10},{10,1... | collective-permute-start | bytes 393224 | tf_op jit(solution)/shard_map/while/body/eval_jaxpr/ppermute | solution.py:16
  475.7 19.1 %collective-permute-start = (bf16[2,128,4,128]{3,1,2,0:T(8,128)(2,1)S(1)}, bf16[2,128,4,128]{3,1,2,0:T(8,128)(2,1)S(1)}, u32[]{:S(2)}, u32[]{:S(2)}) collective-permute-start(bf16[2,128,4,128]{3,1,2,0:T(8,128)(2,1)S(1)} %copy.96), channel_id=1, source_target_pairs={{0,1},{1,2},{2,3},{3,4},{4,5},{5,6},{6,7},{7,8},{8,9},{9,10},{10,1... | collective-permute-start | bytes 786440 | tf_op jit(solution)/shard_map/while/body/eval_jaxpr/ppermute | solution.py:16
  494.9 24.1 %collective-permute-start = (bf16[2,128,4,128]{3,1,2,0:T(8,128)(2,1)S(1)}, bf16[2,128,4,128]{3,1,2,0:T(8,128)(2,1)S(1)}, u32[]{:S(2)}, u32[]{:S(2)}) collective-permute-start(bf16[2,128,4,128]{3,1,2,0:T(8,128)(2,1)S(1)} %copy.96), channel_id=1, source_target_pairs={{0,1},{1,2},{2,3},{3,4},{4,5},{5,6},{6,7},{7,8},{8,9},{9,10},{10,1... | collective-permute-start | bytes 786440 | tf_op jit(solution)/shard_map/while/body/eval_jaxpr/ppermute | solution.py:16
  497.9 21.1 %collective-permute-start.1 = (bf16[128,4,128]{2,0,1:T(8,128)(2,1)S(1)}, bf16[128,4,128]{2,0,1:T(8,128)(2,1)S(1)}, u32[]{:S(2)}, u32[]{:S(2)}) collective-permute-start(bf16[128,4,128]{2,0,1:T(8,128)(2,1)S(1)} %fusion.114), channel_id=1, source_target_pairs={{0,1},{1,2},{2,3},{3,4},{4,5},{5,6},{6,7},{7,8},{8,9},{9,10},{10,1... | collective-permute-start | bytes 393224 | tf_op jit(solution)/shard_map/while/body/eval_jaxpr/ppermute | solution.py:16
  519.1 19.1 %collective-permute-start = (bf16[2,128,4,128]{3,1,2,0:T(8,128)(2,1)S(1)}, bf16[2,128,4,128]{3,1,2,0:T(8,128)(2,1)S(1)}, u32[]{:S(2)}, u32[]{:S(2)}) collective-permute-start(bf16[2,128,4,128]{3,1,2,0:T(8,128)(2,1)S(1)} %copy.96), channel_id=1, source_target_pairs={{0,1},{1,2},{2,3},{3,4},{4,5},{5,6},{6,7},{7,8},{8,9},{9,10},{10,1... | collective-permute-start | bytes 786440 | tf_op jit(solution)/shard_map/while/body/eval_jaxpr/ppermute | solution.py:16
  538.2 24.1 %collective-permute-start = (bf16[2,128,4,128]{3,1,2,0:T(8,128)(2,1)S(1)}, bf16[2,128,4,128]{3,1,2,0:T(8,128)(2,1)S(1)}, u32[]{:S(2)}, u32[]{:S(2)}) collective-permute-start(bf16[2,128,4,128]{3,1,2,0:T(8,128)(2,1)S(1)} %copy.96), channel_id=1, source_target_pairs={{0,1},{1,2},{2,3},{3,4},{4,5},{5,6},{6,7},{7,8},{8,9},{9,10},{10,1... | collective-permute-start | bytes 786440 | tf_op jit(solution)/shard_map/while/body/eval_jaxpr/ppermute | solution.py:16
  541.2 21.1 %collective-permute-start.1 = (bf16[128,4,128]{2,0,1:T(8,128)(2,1)S(1)}, bf16[128,4,128]{2,0,1:T(8,128)(2,1)S(1)}, u32[]{:S(2)}, u32[]{:S(2)}) collective-permute-start(bf16[128,4,128]{2,0,1:T(8,128)(2,1)S(1)} %fusion.114), channel_id=1, source_target_pairs={{0,1},{1,2},{2,3},{3,4},{4,5},{5,6},{6,7},{7,8},{8,9},{9,10},{10,1... | collective-permute-start | bytes 393224 | tf_op jit(solution)/shard_map/while/body/eval_jaxpr/ppermute | solution.py:16
  581.5 24.1 %collective-permute-start = (bf16[2,128,4,128]{3,1,2,0:T(8,128)(2,1)S(1)}, bf16[2,128,4,128]{3,1,2,0:T(8,128)(2,1)S(1)}, u32[]{:S(2)}, u32[]{:S(2)}) collective-permute-start(bf16[2,128,4,128]{3,1,2,0:T(8,128)(2,1)S(1)} %copy.96), channel_id=1, source_target_pairs={{0,1},{1,2},{2,3},{3,4},{4,5},{5,6},{6,7},{7,8},{8,9},{9,10},{10,1... | collective-permute-start | bytes 786440 | tf_op jit(solution)/shard_map/while/body/eval_jaxpr/ppermute | solution.py:16
  584.6 21.1 %collective-permute-start.1 = (bf16[128,4,128]{2,0,1:T(8,128)(2,1)S(1)}, bf16[128,4,128]{2,0,1:T(8,128)(2,1)S(1)}, u32[]{:S(2)}, u32[]{:S(2)}) collective-permute-start(bf16[128,4,128]{2,0,1:T(8,128)(2,1)S(1)} %fusion.114), channel_id=1, source_target_pairs={{0,1},{1,2},{2,3},{3,4},{4,5},{5,6},{6,7},{7,8},{8,9},{9,10},{10,1... | collective-permute-start | bytes 393224 | tf_op jit(solution)/shard_map/while/body/eval_jaxpr/ppermute | solution.py:16
  647.1 77.5 %all-to-all-start.1 = ((bf16[32,8,2048]{2,1,0:T(8,128)(2,1)}), bf16[32,8,2048]{2,1,0:T(8,128)(2,1)S(1)}, u32[]{:S(2)}, u32[]{:S(2)}) async-start(bf16[32,8,2048]{2,1,0:T(8,128)(2,1)} %scatter_fusion.1), calls=%async_computation.1 | async-start | bytes 2097152 | tf_op jit(solution)/shard_map/all_to_all | solution.py:176
  (20 other events, 545.7 us)
Sparse Core Ops, SparseCore 0:
  104.2 80.1 all-gather.2
  188.3 82.8 all-gather.4
where the time goes:
time: 737 us; the launch traced here: 735 us
  waiting for transfers between devices  389 us (53%)
  starting transfers between devices  193 us (26%)
  local copies, waits for them, and re-layouts  98.1 us (13%)
  matrix products  23.3 us (3%)
  other arithmetic  14.7 us (2%)
  between operations  14.5 us (2%)
    ppermute x31, waiting for transfers between devices, from_behind(): lax.ppermute(array, axis, [(i, (i + by) % peers) for i in range(peers)])  161 us
    ppermute x31, starting transfers between devices, from_behind(): lax.ppermute(array, axis, [(i, (i + by) % peers) for i in range(peers)])  151 us
    all_gather x1, waiting for transfers between devices, body(): piece_keys = lax.all_gather(key_rows, 'ctx', axis=0, tiled=True)  83.9 us
    all_gather x1, waiting for transfers between devices, body(): piece_values = lax.all_gather(values, 'ctx', axis=0, tiled=True)  73.1 us
    all_to_all x1, waiting for transfers between devices, body(): lax.all_to_all(returning, 'dp', split_axis=0, concat_axis=0, tiled=True)  50.4 us
    scatter x2, local copies, waits for them, and re-layouts, body(): jnp.zeros((row_count,), jnp.int32).at[landing_rows]  31 us
    all_to_all x1, starting transfers between devices, body(): lax.all_to_all(returning, 'dp', split_axis=0, concat_axis=0, tiled=True)  26.3 us
    scatter x1, local copies, waits for them, and re-layouts, body(): jnp.zeros((dp_count, capacity, features), jnp.bfloat16)  23.6 us
  transfers between devices with their start and end apart: 35, of which 20 were waited for; matrix products, arithmetic and copies ran while one was open for 9% of the time, Pallas kernels for 0%

commit v1 on v0

v1 whole, which is shorter than its diff:
```python
import functools

import jax
import jax.numpy as jnp
from jax import lax
from jax.experimental import pallas as pl
from jax.experimental.pallas import tpu as pltpu
from jax.sharding import Mesh
from jax.sharding import PartitionSpec as P

HEADS = 4
HEAD_DIM = 128
BLOCK = 128
USERS = 3
EPSILON = 1e-06
SCALE = HEAD_DIM ** (-0.5)
ROWS = 128
CAP = 8
N_DP = 32
N_X = 4
REACH = 2
PART = HEADS * ROWS
GROUP = N_X * PART
STEP = 256
VMEM_LIMIT = 48 * 1024 * 1024
CHUNK = 2 * CAP

F32 = jnp.float32
BF16 = jnp.bfloat16


def dot_nn(a, b):
    return lax.dot_general(a, b, (((1,), (0,)), ((), ())), preferred_element_type=F32)


def dot_nt(a, b):
    return lax.dot_general(a, b, (((1,), (1,)), ((), ())), preferred_element_type=F32)


def iota(shape, dim):
    return lax.broadcasted_iota(jnp.int32, shape, dim)


def call(kernel, outs, ins, smem, scratch=(), flops=0, nbytes=0):
    specs = [
        pl.BlockSpec(memory_space=pltpu.SMEM if s else pltpu.VMEM) for s in smem
    ]
    return pl.pallas_call(
        kernel,
        out_shape=outs,
        in_specs=specs,
        out_specs=[pl.BlockSpec(memory_space=pltpu.VMEM)] * len(outs),
        scratch_shapes=list(scratch),
        compiler_params=pltpu.CompilerParams(vmem_limit_bytes=VMEM_LIMIT),
        cost_estimate=pl.CostEstimate(flops=flops, bytes_accessed=nbytes, transcendentals=0),
    )(*ins)


def shape(*dims, dtype=BF16):
    return jax.ShapeDtypeStruct(dims, dtype)


def owners_of(dest_ref, dp):
    targets = dest_ref[pl.ds(dp, 1), :]
    owners = lax.shift_right_logical(targets, 7).astype(F32)
    across = jnp.broadcast_to(owners, (ROWS, ROWS))
    return across, across.T


def pack_kernel(ids_ref, dest_ref, proj_ref, out_ref):
    across, down = owners_of(dest_ref, ids_ref[0])
    square = (ROWS, ROWS)
    earlier = (across == down) & (iota(square, 0) < iota(square, 1))
    slot = jnp.sum(jnp.where(earlier, 1.0, 0.0), axis=0, keepdims=True)
    key = (across[0:1] * CAP + slot).astype(jnp.int32)
    pick = jnp.where(iota((N_DP * CAP, ROWS), 0) == key, 1.0, 0.0).astype(BF16)
    for j in range(2):
        for pair in range(0, HEADS, 2):
            halves = []
            for block in (j, 2 + j):
                at = (block * HEADS + pair) * HEAD_DIM
                moved = dot_nn(pick, proj_ref[:, at : at + 2 * HEAD_DIM])
                halves.append(moved.reshape(N_DP, CAP, 2 * HEAD_DIM))
            chunks = jnp.concatenate(halves, axis=1).astype(BF16)
            for h in range(2):
                out_ref[:, pair + h, :, j * HEAD_DIM : (j + 1) * HEAD_DIM] = chunks[
                    :, :, h * HEAD_DIM : (h + 1) * HEAD_DIM
                ]


def head_columns(h):
    return pl.ds(pl.multiple_of(h * HEAD_DIM, HEAD_DIM), HEAD_DIM)


def block_rows(c):
    return pl.ds(pl.multiple_of(c * ROWS, ROWS), ROWS)


def side_kernel(ids_ref, dest_ref, grad_ref, *out_refs):
    group = ids_ref[0]
    mapping = dest_ref[...]
    landing = lax.shift_right_logical(mapping, 7) == group
    landing_f = jnp.where(landing, 1.0, 0.0)
    square = (ROWS, ROWS)
    before = jnp.where(iota(square, 0) < iota(square, 1), 1.0, 0.0).astype(BF16)
    slot = dot_nn(landing_f.astype(BF16), before)
    code = iota((N_DP, ROWS), 0).astype(F32) * CAP + slot
    place = jnp.where(landing, mapping & (ROWS - 1), ROWS)
    row_of = iota(square, 0)
    total = jnp.zeros(square, F32)
    for i in range(N_DP):
        total = total + jnp.where(row_of == place[i : i + 1], code[i : i + 1], 0.0)
    codes = jnp.broadcast_to(jnp.sum(total, axis=1, keepdims=True), square).T
    for k, out_ref in enumerate(out_refs):
        out_ref[:ROWS] = grad_ref[:, head_columns(ids_ref[2] ^ k)]
        out_ref[ROWS:] = codes[:CHUNK].astype(BF16)


def chunk_row(code, half):
    return (code >> 3) * CHUNK + half * CAP + (code & (CAP - 1))


def code_across(side_ref):
    return side_ref[ROWS : ROWS + CHUNK].astype(F32)[0:1]


def both_halves(code, axis):
    return jnp.concatenate([chunk_row(code, half) for half in range(2)], axis=axis)


def pick_down(code):
    lane = iota((2 * ROWS, N_DP * CHUNK), 1)
    return jnp.where(lane == both_halves(code, 0), 1.0, 0.0).astype(BF16)


def unpack_kernel(
    ids_ref, s0, s1, s2, s3, arrived_ref, gate_ref, query_ref, vk_ref,
):
    for k, side_ref in enumerate((s0, s1, s2, s3)):
        c = ids_ref[2] ^ k
        rows = block_rows(c)
        chunks = arrived_ref[:, c].reshape(N_DP * CHUNK, 2 * HEAD_DIM)
        code = jnp.broadcast_to(code_across(side_ref), (ROWS, ROWS)).T.astype(jnp.int32)
        moved = dot_nn(pick_down(code[:, 0:1]), chunks).astype(BF16)
        gate_ref[rows] = moved[:ROWS, :HEAD_DIM]
        vk_ref[rows, :HEAD_DIM] = moved[:ROWS, HEAD_DIM:]
        query_ref[rows] = moved[ROWS:, :HEAD_DIM]
        vk_ref[rows, HEAD_DIM:] = moved[ROWS:, HEAD_DIM:]


def user_bounds(lengths_ref):
    bounds, start = [], jnp.int32(0)
    for u in range(USERS):
        length = lengths_ref[0, u]
        padded = (length + BLOCK - 1) // BLOCK * BLOCK
        bounds.append((start, start + length, start + padded))
        start = start + padded
    return bounds


def first_key(positions, bounds):
    low = jnp.full(positions.shape, 2 * GROUP, jnp.int32)
    for start, end, _ in bounds:
        low = jnp.where((positions >= start) & (positions < end), start, low)
    return low


def half_scores(a, b):
    return dot_nt(a, b) * (0.5 * SCALE)


def silu_of(half, tanh):
    return half + half * tanh


def slope_of(half, tanh):
    return (0.5 + 0.5 * tanh) * (1.0 + half * (1.0 - tanh))


def key_steps(base, bounds):
    lowest = jnp.int32(0)
    for start, _, _ in bounds:
        lowest = jnp.where(start <= base, start, lowest)
    return lowest // STEP, (base + PART) // STEP


def gather_parts(held, parts):
    for n, part in enumerate(parts):
        held[n * PART : (n + 1) * PART] = part[...]


def forward_kernel(
    ids_ref, lengths_ref, s0, s1, s2, s3, gate_ref, query_ref, vk2_ref, vk1_ref, vk0_ref,
    mixed_ref, gate_grad_ref, l0, l1, l2, l3, held,
):
    gather_parts(held, (vk2_ref, vk1_ref, vk0_ref))
    bounds = user_bounds(lengths_ref)
    base = ids_ref[1] * PART
    first_step, last_step = key_steps(base, bounds)
    query_pos = base + iota((PART, 1), 0)
    low = first_key(query_pos, bounds)
    queries = query_ref[...]

    def step(k, total):
        at = k * STEP
        rows = pl.ds(pl.multiple_of(at - base + REACH * PART, STEP), STEP)
        values = held[rows, :HEAD_DIM]
        keys = held[rows, HEAD_DIM:]
        half = half_scores(queries, keys)
        key_pos = at + iota((1, STEP), 1)
        allowed = (key_pos >= low) & (key_pos <= query_pos)
        weights = jnp.where(allowed, silu_of(half, jnp.tanh(half)), 0.0).astype(BF16)
        return total + dot_nn(weights, values)

    mixed_sum = lax.fori_loop(first_step, last_step, step, jnp.zeros((PART, HEAD_DIM), F32))
    center = mixed_sum - jnp.mean(mixed_sum, axis=-1, keepdims=True)
    inverse = lax.rsqrt(jnp.mean(center * center, axis=-1, keepdims=True) + EPSILON)
    normed = center * inverse
    gating = gate_ref[...].astype(F32)
    head = ids_ref[2]
    for k, part in enumerate((s0, s1, s2, s3)):
        held[block_rows(head ^ k), HEAD_DIM:] = part[:ROWS]
    upstream = held[:PART, HEAD_DIM:].astype(F32)
    layer = (normed * gating).astype(BF16)
    grad_normed = upstream * gating
    mixed_ref[...] = (
        (
            grad_normed
            - jnp.mean(grad_normed, axis=-1, keepdims=True)
            - normed * jnp.mean(grad_normed * normed, axis=-1, keepdims=True)
        )
        * inverse
    ).astype(BF16)
    gate_grad_ref[...] = (upstream * normed).astype(BF16)
    held[:PART, :HEAD_DIM] = layer
    for k, layer_ref in enumerate((l0, l1, l2, l3)):
        layer_ref[...] = held[block_rows(head ^ k), :HEAD_DIM]


def query_steps(base, bounds):
    highest = bounds[-1][2]
    for start, _, _ in reversed(bounds):
        highest = jnp.where(start >= base + PART, start, highest)
    return base // STEP, (highest + STEP - 1) // STEP


def query_grad_kernel(
    ids_ref, lengths_ref, s0, s1, s2, s3, mixed_ref, gate_grad_ref, q0_ref, q1_ref, q2_ref,
    vk2_ref, vk1_ref, vk0_ref, out_ref, weights_ref, slope_ref, held, held_q, done,
):
    gather_parts(held, (vk2_ref, vk1_ref, vk0_ref))
    gather_parts(held_q, (q0_ref, q1_ref, q2_ref))
    bounds = user_bounds(lengths_ref)
    base = ids_ref[1] * PART
    own_pos = base + iota((PART, 1), 0)
    low = first_key(own_pos, bounds)
    queries = q0_ref[...]
    grad_mixed = mixed_ref[...]

    def step(k, total):
        at = k * STEP
        rows = pl.ds(pl.multiple_of(at - base + REACH * PART, STEP), STEP)
        values = held[rows, :HEAD_DIM]
        keys = held[rows, HEAD_DIM:]
        half = half_scores(queries, keys)
        key_pos = at + iota((1, STEP), 1)
        allowed = (key_pos >= low) & (key_pos <= own_pos)
        slope = jnp.where(allowed, slope_of(half, jnp.tanh(half)), 0.0)
        grad_scores = (dot_nt(grad_mixed, values) * slope).astype(BF16)
        return total + dot_nn(grad_scores, keys)

    total = lax.fori_loop(*key_steps(base, bounds), step, jnp.zeros((PART, HEAD_DIM), F32))
    done[0] = gate_grad_ref[...]
    done[1] = (total * SCALE).astype(BF16)
    pack_back(ids_ref, (s0, s1, s2, s3), done, out_ref, 0)
    own_keys = vk0_ref[:, HEAD_DIM:]

    def key_step(k, carry):
        at = k * STEP
        n = k - base // STEP
        query_pos = at + iota((1, STEP), 1)
        first = first_key(query_pos, bounds)
        half = half_scores(own_keys, held_q[pl.ds(pl.multiple_of(n * STEP, STEP), STEP)])
        allowed = (own_pos >= first) & (own_pos <= query_pos)
        tanh = jnp.tanh(half)
        weights_ref[n] = jnp.where(allowed, silu_of(half, tanh), 0.0).astype(BF16)
        slope_ref[n] = jnp.where(allowed, slope_of(half, tanh), 0.0)
        return carry

    lax.fori_loop(*query_steps(base, bounds), key_step, 0)


def pack_back(ids_ref, sides, done, out_ref, j):
    sublane = iota((N_DP * CHUNK, 2 * ROWS), 0)
    for k, side_ref in enumerate(sides):
        c = ids_ref[2] ^ k
        at = both_halves(code_across(side_ref).astype(jnp.int32), 1)
        pick = jnp.where(sublane == at, 1.0, 0.0).astype(BF16)
        rows = jnp.concatenate([done[0, block_rows(c)], done[1, block_rows(c)]], axis=0)
        out_ref[:, c, :, j * HEAD_DIM : (j + 1) * HEAD_DIM] = (
            dot_nn(pick, rows).astype(BF16).reshape(N_DP, CHUNK, HEAD_DIM)
        )


def backward_kernel(
    ids_ref, lengths_ref, s0, s1, s2, s3, vk_ref, q0_ref, q1_ref, q2_ref,
    m0_ref, m1_ref, m2_ref, weights_ref, slope_ref, gq_ref, out_ref, held_q, held_m, done,
):
    gather_parts(held_q, (q0_ref, q1_ref, q2_ref))
    gather_parts(held_m, (m0_ref, m1_ref, m2_ref))
    out_ref[:, :, :, :HEAD_DIM] = gq_ref[...]
    bounds = user_bounds(lengths_ref)
    base = ids_ref[1] * PART
    values = vk_ref[:, :HEAD_DIM]

    def step(k, totals):
        grad_values, grad_keys = totals
        n = k - base // STEP
        rows = pl.ds(pl.multiple_of(n * STEP, STEP), STEP)
        grad_mixed = held_m[rows]
        grad_scores = (dot_nt(values, grad_mixed) * slope_ref[n]).astype(BF16)
        return (
            grad_values + dot_nn(weights_ref[n], grad_mixed),
            grad_keys + dot_nn(grad_scores, held_q[rows]),
        )

    zeros = jnp.zeros((PART, HEAD_DIM), F32)
    grad_values, grad_keys = lax.fori_loop(*query_steps(base, bounds), step, (zeros, zeros))
    done[0] = grad_values.astype(BF16)
    done[1] = (grad_keys * SCALE).astype(BF16)
    pack_back(ids_ref, (s0, s1, s2, s3), done, out_ref, 1)


def finish_kernel(ids_ref, dest_ref, l0, l1, l2, l3, back_ref, grad_ref, out_ref):
    across, down = owners_of(dest_ref, ids_ref[0])
    square = (ROWS, ROWS)
    earlier = (across == down) & (iota(square, 1) < iota(square, 0))
    slot = jnp.sum(jnp.where(earlier, 1.0, 0.0), axis=1, keepdims=True)
    code = (down[:, 0:1] * CAP + slot).astype(jnp.int32)
    pick = pick_down(code)
    for k, layer_ref in enumerate((l0, l1, l2, l3)):
        out_ref[:, head_columns(ids_ref[2] ^ k)] = layer_ref[...]
    for h in range(HEADS):
        chunks = back_ref[:, h].reshape(N_DP * CHUNK, 2 * HEAD_DIM)
        moved = dot_nn(pick, chunks).astype(BF16)
        for half in range(2):
            for j in range(2):
                at = ((2 * half + j) * HEADS + h) * HEAD_DIM
                grad_ref[:, at : at + HEAD_DIM] = moved[
                    half * ROWS : (half + 1) * ROWS, j * HEAD_DIM : (j + 1) * HEAD_DIM
                ]


def route(chunks):
    flat = chunks.reshape(N_DP * HEADS * CHUNK, 2 * HEAD_DIM)
    moved = lax.all_to_all(flat, ("dp", "h"), 0, 0, tiled=True)
    return moved.reshape(chunks.shape)


def from_quarter(array, by):
    pairs = [(i, i - by) for i in range(N_X) if 0 <= i - by < N_X]
    return lax.ppermute(array, "x", pairs)


def swap_heads(pieces):
    moved = [
        lax.ppermute(piece, "h", [(i, i ^ k) for i in range(HEADS)])
        for k, piece in enumerate(pieces)
        if k
    ]
    return [pieces[0], *moved]


def body(projected, destination, lengths, grad_out):
    ids = jnp.stack([lax.axis_index(axis) for axis in ("dp", "x", "h")]).astype(jnp.int32)
    mapping = destination.reshape(N_DP, ROWS)
    chunked = shape(N_DP, HEADS, CHUNK, 2 * HEAD_DIM)
    half_chunked = shape(N_DP, HEADS, CHUNK, HEAD_DIM)
    head_part = shape(PART, HEAD_DIM)
    pieces = [shape(ROWS, HEAD_DIM)] * HEADS
    (packed,) = call(
        pack_kernel, [chunked], (ids, mapping, projected), (1, 0, 0),
        flops=2 * 256 * 128 * 2048, nbytes=3 << 19,
    )
    side_out = call(
        side_kernel, [shape(ROWS + CHUNK, HEAD_DIM)] * HEADS, (ids, mapping, grad_out), (1, 0, 0),
        nbytes=3 << 17,
    )
    side = swap_heads(side_out)
    arrived = route(packed)
    gate, queries, vk = call(
        unpack_kernel, [head_part, head_part, shape(PART, 2 * HEAD_DIM)],
        (ids, *side, arrived), (1,) + (0,) * 5,
        flops=1 << 28, nbytes=2 << 20,
    )
    vk_parts = (from_quarter(vk, -2), from_quarter(vk, -1), vk)
    query_parts = (queries, from_quarter(queries, 1), from_quarter(queries, 2))
    span = (REACH + 1) * PART
    held_vk = pltpu.VMEM((span, 2 * HEAD_DIM), BF16)
    held_one = pltpu.VMEM((span, HEAD_DIM), BF16)
    done = pltpu.VMEM((2, PART, HEAD_DIM), BF16)
    mixed, gate_grad, *layer = call(
        forward_kernel, [head_part, head_part, *pieces],
        (ids, lengths, *side, gate, queries, *vk_parts), (1, 1) + (0,) * 9,
        scratch=[held_vk], flops=1 << 29, nbytes=2 << 20,
    )
    mixed_parts = (mixed, from_quarter(mixed, 1), from_quarter(mixed, 2))
    layer_home = swap_heads(layer)
    gq_back, weights, slopes = call(
        query_grad_kernel,
        [half_chunked, shape(span // STEP, PART, STEP), shape(span // STEP, PART, STEP, dtype=F32)],
        (ids, lengths, *side, mixed, gate_grad, *query_parts, *vk_parts), (1, 1) + (0,) * 12,
        scratch=[held_vk, held_one, done], flops=1 << 29, nbytes=2 << 20,
    )
    (back,) = call(
        backward_kernel, [chunked],
        (ids, lengths, *side, vk, *query_parts, *mixed_parts, weights, slopes, gq_back),
        (1, 1) + (0,) * 14,
        scratch=[held_one, held_one, done], flops=1 << 30, nbytes=3 << 20,
    )
    home = route(back)
    grad_projected, layer_output = call(
        finish_kernel, [shape(ROWS, 4 * HEADS * HEAD_DIM), shape(ROWS, HEADS * HEAD_DIM)],
        (ids, mapping, *layer_home, home), (1, 0, 0, 0, 0, 0, 0),
        flops=1 << 28, nbytes=2 << 20,
    )
    return (layer_output, grad_projected)


def solution(mesh):
    fine = Mesh(mesh.devices.reshape(N_DP, N_X, HEADS), ("dp", "x", "h"))
    rows = P(("dp", "x", "h"), None)
    in_specs = (rows, P(("x", "h"), None), P("dp", None), rows)
    return jax.shard_map(
        body, mesh=fine, in_specs=in_specs, out_specs=(rows, rows), check_vma=False
    )
```

time: 737 us -> 192 us (0.26)
  the two profiles are of different devices: /device:TPU:38 before, /device:TPU:37 now
where the time goes in v1:
time: 192 us; the launch traced here: 191 us
  waiting for transfers between devices  88.1 us (46%)
  starting transfers between devices  79.7 us (42%)
  Pallas kernels  20.5 us (11%)
    ppermute x6, waiting for transfers between devices, swap_heads(): lax.ppermute(piece, 'h', [(i, i ^ k) for i in range(HEADS)])  84.7 us
    ppermute x6, starting transfers between devices, swap_heads(): lax.ppermute(piece, 'h', [(i, i ^ k) for i in range(HEADS)])  33.2 us
    all_to_all x2, starting transfers between devices, route(): moved = lax.all_to_all(flat, ('dp', 'h'), 0, 0, tiled=True)  31.7 us
    pallas_call x7, Pallas kernels, call(): pl.pallas_call(kernel, out_shape=outs, in_specs=specs, out_specs=[pl.Bloc...  20.5 us
    ppermute x6, starting transfers between devices, from_quarter(): return lax.ppermute(array, 'x', pairs)  14.8 us
  transfers between devices with their start and end apart: 14, of which 5 were waited for; matrix products, arithmetic and copies ran while one was open for 0% of the time, Pallas kernels for 5%

profile of v1, /device:TPU:37, one launch (start us, length us, event | category | flops | bytes accessed | tf_op | source)
XLA Modules:
  0.0 191.0 jit_solution(16292866309161465908)
XLA Ops:
  2.5 2.1 %shard_map.60 = bf16[32,4,16,256]{3,2,1,0:T(8,128)(2,1)} custom-call(s32[3]{0:T(128)S(1)} %pad_add_fusion.ids_ref, s32[32,128]{1,0:T(8,128)S(1)} %bitcast.10, bf16[128,2048]{1,0:T(8,128)(2,1)S(1)} %copy-done), custom_call_target="tpu_custom_call" | custom-call | flops 134217728 | bytes 1572864 | tf_op jit(solution)/shard_map/pallas_call | solution.py:48
  4.6 19.5 %all-to-all-start = ((bf16[128,16,256]{2,1,0:T(8,128)(2,1)}), bf16[128,16,256]{2,1,0:T(8,128)(2,1)S(1)}, u32[]{:S(2)}, u32[]{:S(2)}) async-start(bf16[128,16,256]{2,1,0:T(8,128)(2,1)} %bitcast.4), calls=%async_computation | async-start | bytes 2097152 | tf_op jit(solution)/shard_map/all_to_all | solution.py:356
  25.2 2.3 %collective-permute-start = (bf16[144,128]{1,0:T(8,128)(2,1)S(1)}, bf16[144,128]{1,0:T(8,128)(2,1)S(1)}, u32[]{:S(2)}, u32[]{:S(2)}) collective-permute-start(bf16[144,128]{1,0:T(8,128)(2,1)S(1)} %get-tuple-element.21), channel_id=1, source_target_pairs={{0,1},{1,0},{2,3},{3,2},{4,5},{5,4},{6,7},{7,6},{8,9},{9,8},{10,11... | collective-permute-start | bytes 110600 | tf_op jit(solution)/shard_map/ppermute | solution.py:367
  27.4 10.9 %collective-permute-start.1 = (bf16[144,128]{1,0:T(8,128)(2,1)S(1)}, bf16[144,128]{1,0:T(8,128)(2,1)S(1)}, u32[]{:S(2)}, u32[]{:S(2)}) collective-permute-start(bf16[144,128]{1,0:T(8,128)(2,1)S(1)} %get-tuple-element.22), channel_id=1, source_target_pairs={{0,2},{1,3},{2,0},{3,1},{4,6},{5,7},{6,4},{7,5},{8,10},{9,11},{10,... | collective-permute-start | bytes 110600 | tf_op jit(solution)/shard_map/ppermute | solution.py:367
  38.4 3.4 %collective-permute-start.2 = (bf16[144,128]{1,0:T(8,128)(2,1)S(1)}, bf16[144,128]{1,0:T(8,128)(2,1)S(1)}, u32[]{:S(2)}, u32[]{:S(2)}) collective-permute-start(bf16[144,128]{1,0:T(8,128)(2,1)S(1)} %get-tuple-element.23), channel_id=1, source_target_pairs={{0,3},{1,2},{2,1},{3,0},{4,7},{5,6},{6,5},{7,4},{8,11},{9,10},{10,... | collective-permute-start | bytes 110600 | tf_op jit(solution)/shard_map/ppermute | solution.py:367
  41.8 40.1 %collective-permute-done.1.s2 = bf16[144,128]{1,0:T(8,128)(2,1)S(1)} collective-permute-done((bf16[144,128]{1,0:T(8,128)(2,1)S(1)}, bf16[144,128]{1,0:T(8,128)(2,1)S(1)}, u32[]{:S(2)}, u32[]{:S(2)}) %collective-permute-start.1) | collective-permute-done | bytes 36896 | tf_op jit(solution)/shard_map/ppermute | solution.py:367
  81.9 2.0 %collective-permute-done.2.s3 = bf16[144,128]{1,0:T(8,128)(2,1)S(1)} collective-permute-done((bf16[144,128]{1,0:T(8,128)(2,1)S(1)}, bf16[144,128]{1,0:T(8,128)(2,1)S(1)}, u32[]{:S(2)}, u32[]{:S(2)}) %collective-permute-start.2) | collective-permute-done | bytes 36896 | tf_op jit(solution)/shard_map/ppermute | solution.py:367
  85.1 2.8 %collective-permute-start.4 = (bf16[512,256]{1,0:T(8,128)(2,1)S(1)}, bf16[512,256]{1,0:T(8,128)(2,1)S(1)}, u32[]{:S(2)}, u32[]{:S(2)}) collective-permute-start(bf16[512,256]{1,0:T(8,128)(2,1)S(1)} %get-tuple-element.26.vk0_ref.vk_ref), channel_id=1, source_target_pairs={{0,4},{4,8},{8,12},{1,5},{5,9},{9,13},{2,6},{6,10},{10,14},{3,7},{... | collective-permute-start | bytes 786440 | tf_op jit(solution)/shard_map/ppermute | solution.py:362
  87.9 1.3 collective-permute-start.3
  89.2 5.5 %collective-permute-start.9 = (bf16[512,128]{1,0:T(8,128)(2,1)S(1)}, bf16[512,128]{1,0:T(8,128)(2,1)S(1)}, u32[]{:S(2)}, u32[]{:S(2)}) collective-permute-start(bf16[512,128]{1,0:T(8,128)(2,1)S(1)} %get-tuple-element.25.query_ref.q0_ref), channel_id=1, source_target_pairs={{8,0},{12,4},{9,1},{13,5},{10,2},{14,6},{11,3},{15,7},{24,16},{28,... | collective-permute-start | bytes 393224 | tf_op jit(solution)/shard_map/ppermute | solution.py:362
  94.7 1.9 %collective-permute-start.8 = (bf16[512,128]{1,0:T(8,128)(2,1)S(1)}, bf16[512,128]{1,0:T(8,128)(2,1)S(1)}, u32[]{:S(2)}, u32[]{:S(2)}) collective-permute-start(bf16[512,128]{1,0:T(8,128)(2,1)S(1)} %get-tuple-element.25.query_ref.q0_ref), channel_id=1, source_target_pairs={{4,0},{8,4},{12,8},{5,1},{9,5},{13,9},{6,2},{10,6},{14,10},{7,3},{... | collective-permute-start | bytes 393224 | tf_op jit(solution)/shard_map/ppermute | solution.py:362
  96.7 3.4 %collective-permute-done.3.vk2_ref = bf16[512,256]{1,0:T(8,128)(2,1)S(1)} collective-permute-done((bf16[512,256]{1,0:T(8,128)(2,1)S(1)}, bf16[512,256]{1,0:T(8,128)(2,1)S(1)}, u32[]{:S(2)}, u32[]{:S(2)}) %collective-permute-start.3) | collective-permute-done | bytes 262176 | tf_op jit(solution)/shard_map/ppermute | solution.py:362
  100.1 2.5 %shard_map.62 = (bf16[512,128]{1,0:T(8,128)(2,1)S(1)}, bf16[512,128]{1,0:T(8,128)(2,1)S(1)}, bf16[128,128]{1,0:T(8,128)(2,1)S(1)}, bf16[128,128]{1,0:T(8,128)(2,...) custom-call(s32[3]{0:T(128)S(1)} %pad_add_fusion.ids_ref, s32[1,3]{1,0:T(1,128)S(1)} %copy-done.4, ...), custom_call_target="tpu_custom_call" | custom-call | flops 536870912 | bytes 2097152 | tf_op jit(solution)/shard_map/pallas_call | solution.py:48
  102.5 1.3 collective-permute-start.11
  103.8 1.9 %collective-permute-start.10 = (bf16[512,128]{1,0:T(8,128)(2,1)S(1)}, bf16[512,128]{1,0:T(8,128)(2,1)S(1)}, u32[]{:S(2)}, u32[]{:S(2)}) collective-permute-start(bf16[512,128]{1,0:T(8,128)(2,1)S(1)} %get-tuple-element.31.mixed_ref.m0_ref), channel_id=1, source_target_pairs={{4,0},{8,4},{12,8},{5,1},{9,5},{13,9},{6,2},{10,6},{14,10},{7,3},{... | collective-permute-start | bytes 393224 | tf_op jit(solution)/shard_map/ppermute | solution.py:362
  105.8 6.4 %shard_map.63 = (bf16[32,4,16,128]{3,2,1,0:T(8,128)(2,1)S(1)}, bf16[6,512,256]{2,1,0:T(8,128)(2,1)S(1)}, f32[6,512,256]{2,1,0:T(8,128)}) custom-call(s32[3]{0:T(128)S(1)} %pad_add_fusion.ids_ref, s32[1,3]{1,0:T(1,128)S(1)} %copy-done.4, bf16[144,128]{1,0:T(8,128)(2,1)S(1)} %get-tuple-element.20.s0, bf16[144,128]{1,0:T(8,128)(2,1)S(1)} %collective-permute-done.s1, ...), custom_call_target="tpu_custom_call" | custom-call | flops 536870912 | bytes 2097152 | tf_op jit(solution)/shard_map/pallas_call | solution.py:48
  112.2 5.4 %shard_map.64 = bf16[32,4,16,256]{3,2,1,0:T(8,128)(2,1)} custom-call(s32[3]{0:T(128)S(1)} %pad_add_fusion.ids_ref, s32[1,3]{1,0:T(1,128)S(1)} %copy-done.4, bf16[144,128]{1,0:T(8,128)(2,1)S(1)} %get-tuple-element.20.s0, bf16[144,128]{1,0:T(8,128)(2,1)S(1)} %collective-permute-done.s1, bf16[144,128]{1,0:T(8,128)(2,1)S(1)} %collective-permute-done.1.s2, ...), custom_call_target="tpu_custom_call" | custom-call | flops 1073741824 | bytes 3145728 | tf_op jit(solution)/shard_map/pallas_call | solution.py:48
  117.6 12.2 %all-to-all-start.1 = ((bf16[128,16,256]{2,1,0:T(8,128)(2,1)}), bf16[128,16,256]{2,1,0:T(8,128)(2,1)S(1)}, u32[]{:S(2)}, u32[]{:S(2)}) async-start(bf16[128,16,256]{2,1,0:T(8,128)(2,1)} %bitcast.6), calls=%async_computation.1 | async-start | bytes 2097152 | tf_op jit(solution)/shard_map/all_to_all | solution.py:356
  129.8 2.3 %collective-permute-start.5 = (bf16[128,128]{1,0:T(8,128)(2,1)S(1)}, bf16[128,128]{1,0:T(8,128)(2,1)S(1)}, u32[]{:S(2)}, u32[]{:S(2)}) collective-permute-start(bf16[128,128]{1,0:T(8,128)(2,1)S(1)} %get-tuple-element.28), channel_id=1, source_target_pairs={{0,1},{1,0},{2,3},{3,2},{4,5},{5,4},{6,7},{7,6},{8,9},{9,8},{10,11... | collective-permute-start | bytes 98312 | tf_op jit(solution)/shard_map/ppermute | solution.py:367
  132.1 10.9 %collective-permute-start.6 = (bf16[128,128]{1,0:T(8,128)(2,1)S(1)}, bf16[128,128]{1,0:T(8,128)(2,1)S(1)}, u32[]{:S(2)}, u32[]{:S(2)}) collective-permute-start(bf16[128,128]{1,0:T(8,128)(2,1)S(1)} %get-tuple-element.29), channel_id=1, source_target_pairs={{0,2},{1,3},{2,0},{3,1},{4,6},{5,7},{6,4},{7,5},{8,10},{9,11},{10,... | collective-permute-start | bytes 98312 | tf_op jit(solution)/shard_map/ppermute | solution.py:367
  143.0 3.4 %collective-permute-start.7 = (bf16[128,128]{1,0:T(8,128)(2,1)S(1)}, bf16[128,128]{1,0:T(8,128)(2,1)S(1)}, u32[]{:S(2)}, u32[]{:S(2)}) collective-permute-start(bf16[128,128]{1,0:T(8,128)(2,1)S(1)} %get-tuple-element.30), channel_id=1, source_target_pairs={{0,3},{1,2},{2,1},{3,0},{4,7},{5,6},{6,5},{7,4},{8,11},{9,10},{10,... | collective-permute-start | bytes 98312 | tf_op jit(solution)/shard_map/ppermute | solution.py:367
  146.4 41.0 %collective-permute-done.6.l2 = bf16[128,128]{1,0:T(8,128)(2,1)S(1)} collective-permute-done((bf16[128,128]{1,0:T(8,128)(2,1)S(1)}, bf16[128,128]{1,0:T(8,128)(2,1)S(1)}, u32[]{:S(2)}, u32[]{:S(2)}) %collective-permute-start.6) | collective-permute-done | bytes 32800 | tf_op jit(solution)/shard_map/ppermute | solution.py:367
  187.5 1.6 collective-permute-done.7.l3
  189.0 2.0 %shard_map.65 = (bf16[128,2048]{1,0:T(8,128)(2,1)}, bf16[128,512]{1,0:T(8,128)(2,1)}) custom-call(s32[3]{0:T(128)S(1)} %pad_add_fusion.ids_ref, s32[32,128]{1,0:T(8,128)S(1)} %bitcast.12, bf16[128,128]{1,0:T(8,128)(2,1)S(1)} %get-tuple-element.27.l0, bf16[128,128]{1,0:T(8,128)(2,1)S(1)} %collective-permute-done.5.l1, ...), custom_call_target="tpu_custom_call" | custom-call | flops 268435456 | bytes 2097152 | tf_op jit(solution)/shard_map/pallas_call | solution.py:48
  (22 shorter events, 4.1 us)
Async XLA Ops:
  0.6 23.4 %copy-start.2 = (s32[1,4096]{1,0:T(1,128)S(1)}, s32[1,4096]{1,0:T(1,128)}, u32[]{:S(2)}) copy-start(s32[1,4096]{1,0:T(1,128)} %param.5) | copy-start | bytes 49156
  0.6 99.4 %copy-start.4 = (s32[1,3]{1,0:T(1,128)S(1)}, s32[1,3]{1,0:T(1,128)}, u32[]{:S(2)}) copy-start(s32[1,3]{1,0:T(1,128)} %lengths_ref.5) | copy-start | bytes 40
  0.7 1.0 copy-start
  1.8 0.7 copy-start.1
  2.5 21.6 %copy-start.3 = (bf16[128,512]{1,0:T(8,128)(2,1)S(1)}, bf16[128,512]{1,0:T(8,128)(2,1)}, u32[]{:S(2)}) copy-start(bf16[128,512]{1,0:T(8,128)(2,1)} %grad_ref.1) | copy-start | bytes 393220
  4.6 79.3 %all-to-all-start = ((bf16[128,16,256]{2,1,0:T(8,128)(2,1)}), bf16[128,16,256]{2,1,0:T(8,128)(2,1)S(1)}, u32[]{:S(2)}, u32[]{:S(2)}) async-start(bf16[128,16,256]{2,1,0:T(8,128)(2,1)} %bitcast.4), calls=%async_computation | async-start | bytes 2097152 | tf_op jit(solution)/shard_map/all_to_all | solution.py:356
  25.2 16.6 %collective-permute-start = (bf16[144,128]{1,0:T(8,128)(2,1)S(1)}, bf16[144,128]{1,0:T(8,128)(2,1)S(1)}, u32[]{:S(2)}, u32[]{:S(2)}) collective-permute-start(bf16[144,128]{1,0:T(8,128)(2,1)S(1)} %get-tuple-element.21), channel_id=1, source_target_pairs={{0,1},{1,0},{2,3},{3,2},{4,5},{5,4},{6,7},{7,6},{8,9},{9,8},{10,11... | collective-permute-start | bytes 110600 | tf_op jit(solution)/shard_map/ppermute | solution.py:367
  27.4 54.4 %collective-permute-start.1 = (bf16[144,128]{1,0:T(8,128)(2,1)S(1)}, bf16[144,128]{1,0:T(8,128)(2,1)S(1)}, u32[]{:S(2)}, u32[]{:S(2)}) collective-permute-start(bf16[144,128]{1,0:T(8,128)(2,1)S(1)} %get-tuple-element.22), channel_id=1, source_target_pairs={{0,2},{1,3},{2,0},{3,1},{4,6},{5,7},{6,4},{7,5},{8,10},{9,11},{10,... | collective-permute-start | bytes 110600 | tf_op jit(solution)/shard_map/ppermute | solution.py:367
  38.4 45.5 %collective-permute-start.2 = (bf16[144,128]{1,0:T(8,128)(2,1)S(1)}, bf16[144,128]{1,0:T(8,128)(2,1)S(1)}, u32[]{:S(2)}, u32[]{:S(2)}) collective-permute-start(bf16[144,128]{1,0:T(8,128)(2,1)S(1)} %get-tuple-element.23), channel_id=1, source_target_pairs={{0,3},{1,2},{2,1},{3,0},{4,7},{5,6},{6,5},{7,4},{8,11},{9,10},{10,... | collective-permute-start | bytes 110600 | tf_op jit(solution)/shard_map/ppermute | solution.py:367
  85.1 11.6 %collective-permute-start.4 = (bf16[512,256]{1,0:T(8,128)(2,1)S(1)}, bf16[512,256]{1,0:T(8,128)(2,1)S(1)}, u32[]{:S(2)}, u32[]{:S(2)}) collective-permute-start(bf16[512,256]{1,0:T(8,128)(2,1)S(1)} %get-tuple-element.26.vk0_ref.vk_ref), channel_id=1, source_target_pairs={{0,4},{4,8},{8,12},{1,5},{5,9},{9,13},{2,6},{6,10},{10,14},{3,7},{... | collective-permute-start | bytes 786440 | tf_op jit(solution)/shard_map/ppermute | solution.py:362
  87.9 12.1 %collective-permute-start.3 = (bf16[512,256]{1,0:T(8,128)(2,1)S(1)}, bf16[512,256]{1,0:T(8,128)(2,1)S(1)}, u32[]{:S(2)}, u32[]{:S(2)}) collective-permute-start(bf16[512,256]{1,0:T(8,128)(2,1)S(1)} %get-tuple-element.26.vk0_ref.vk_ref), channel_id=1, source_target_pairs={{0,8},{4,12},{1,9},{5,13},{2,10},{6,14},{3,11},{7,15},{16,24},{20,... | collective-permute-start | bytes 786440 | tf_op jit(solution)/shard_map/ppermute | solution.py:362
  89.2 16.6 %collective-permute-start.9 = (bf16[512,128]{1,0:T(8,128)(2,1)S(1)}, bf16[512,128]{1,0:T(8,128)(2,1)S(1)}, u32[]{:S(2)}, u32[]{:S(2)}) collective-permute-start(bf16[512,128]{1,0:T(8,128)(2,1)S(1)} %get-tuple-element.25.query_ref.q0_ref), channel_id=1, source_target_pairs={{8,0},{12,4},{9,1},{13,5},{10,2},{14,6},{11,3},{15,7},{24,16},{28,... | collective-permute-start | bytes 393224 | tf_op jit(solution)/shard_map/ppermute | solution.py:362
  94.7 11.1 %collective-permute-start.8 = (bf16[512,128]{1,0:T(8,128)(2,1)S(1)}, bf16[512,128]{1,0:T(8,128)(2,1)S(1)}, u32[]{:S(2)}, u32[]{:S(2)}) collective-permute-start(bf16[512,128]{1,0:T(8,128)(2,1)S(1)} %get-tuple-element.25.query_ref.q0_ref), channel_id=1, source_target_pairs={{4,0},{8,4},{12,8},{5,1},{9,5},{13,9},{6,2},{10,6},{14,10},{7,3},{... | collective-permute-start | bytes 393224 | tf_op jit(solution)/shard_map/ppermute | solution.py:362
  102.5 9.6 %collective-permute-start.11 = (bf16[512,128]{1,0:T(8,128)(2,1)S(1)}, bf16[512,128]{1,0:T(8,128)(2,1)S(1)}, u32[]{:S(2)}, u32[]{:S(2)}) collective-permute-start(bf16[512,128]{1,0:T(8,128)(2,1)S(1)} %get-tuple-element.31.mixed_ref.m0_ref), channel_id=1, source_target_pairs={{8,0},{12,4},{9,1},{13,5},{10,2},{14,6},{11,3},{15,7},{24,16},{28,... | collective-permute-start | bytes 393224 | tf_op jit(solution)/shard_map/ppermute | solution.py:362
  103.8 8.3 %collective-permute-start.10 = (bf16[512,128]{1,0:T(8,128)(2,1)S(1)}, bf16[512,128]{1,0:T(8,128)(2,1)S(1)}, u32[]{:S(2)}, u32[]{:S(2)}) collective-permute-start(bf16[512,128]{1,0:T(8,128)(2,1)S(1)} %get-tuple-element.31.mixed_ref.m0_ref), channel_id=1, source_target_pairs={{4,0},{8,4},{12,8},{5,1},{9,5},{13,9},{6,2},{10,6},{14,10},{7,3},{... | collective-permute-start | bytes 393224 | tf_op jit(solution)/shard_map/ppermute | solution.py:362
  117.6 71.5 %all-to-all-start.1 = ((bf16[128,16,256]{2,1,0:T(8,128)(2,1)}), bf16[128,16,256]{2,1,0:T(8,128)(2,1)S(1)}, u32[]{:S(2)}, u32[]{:S(2)}) async-start(bf16[128,16,256]{2,1,0:T(8,128)(2,1)} %bitcast.6), calls=%async_computation.1 | async-start | bytes 2097152 | tf_op jit(solution)/shard_map/all_to_all | solution.py:356
  129.8 16.6 %collective-permute-start.5 = (bf16[128,128]{1,0:T(8,128)(2,1)S(1)}, bf16[128,128]{1,0:T(8,128)(2,1)S(1)}, u32[]{:S(2)}, u32[]{:S(2)}) collective-permute-start(bf16[128,128]{1,0:T(8,128)(2,1)S(1)} %get-tuple-element.28), channel_id=1, source_target_pairs={{0,1},{1,0},{2,3},{3,2},{4,5},{5,4},{6,7},{7,6},{8,9},{9,8},{10,11... | collective-permute-start | bytes 98312 | tf_op jit(solution)/shard_map/ppermute | solution.py:367
  132.1 55.4 %collective-permute-start.6 = (bf16[128,128]{1,0:T(8,128)(2,1)S(1)}, bf16[128,128]{1,0:T(8,128)(2,1)S(1)}, u32[]{:S(2)}, u32[]{:S(2)}) collective-permute-start(bf16[128,128]{1,0:T(8,128)(2,1)S(1)} %get-tuple-element.29), channel_id=1, source_target_pairs={{0,2},{1,3},{2,0},{3,1},{4,6},{5,7},{6,4},{7,5},{8,10},{9,11},{10,... | collective-permute-start | bytes 98312 | tf_op jit(solution)/shard_map/ppermute | solution.py:367
  143.0 46.1 %collective-permute-start.7 = (bf16[128,128]{1,0:T(8,128)(2,1)S(1)}, bf16[128,128]{1,0:T(8,128)(2,1)S(1)}, u32[]{:S(2)}, u32[]{:S(2)}) collective-permute-start(bf16[128,128]{1,0:T(8,128)(2,1)S(1)} %get-tuple-element.30), channel_id=1, source_target_pairs={{0,3},{1,2},{2,1},{3,0},{4,7},{5,6},{6,5},{7,4},{8,11},{9,10},{10,... | collective-permute-start | bytes 98312 | tf_op jit(solution)/shard_map/ppermute | solution.py:367

commit v2 on v1

v2 whole, which is shorter than its diff:
```python
import functools

import jax
import jax.numpy as jnp
from jax import lax
from jax.experimental import pallas as pl
from jax.experimental.pallas import tpu as pltpu
from jax.sharding import Mesh
from jax.sharding import PartitionSpec as P

HEADS = 4
HEAD_DIM = 128
BLOCK = 128
USERS = 3
EPSILON = 1e-06
SCALE = HEAD_DIM ** (-0.5)
ROWS = 128
CAP = 8
N_DP = 32
N_X = 4
REACH = 2
PART = HEADS * ROWS
GROUP = N_X * PART
STEP = 256
VMEM_LIMIT = 48 * 1024 * 1024
CHUNK = 2 * CAP

F32 = jnp.float32
BF16 = jnp.bfloat16


def dot_nn(a, b):
    return lax.dot_general(a, b, (((1,), (0,)), ((), ())), preferred_element_type=F32)


def dot_nt(a, b):
    return lax.dot_general(a, b, (((1,), (1,)), ((), ())), preferred_element_type=F32)


def iota(shape, dim):
    return lax.broadcasted_iota(jnp.int32, shape, dim)


def call(kernel, outs, ins, smem, scratch=(), flops=0, nbytes=0, hbm_in=(), hbm_out=False, limit=VMEM_LIMIT):
    spaces = [pltpu.SMEM if s else pltpu.VMEM for s in smem]
    for n in hbm_in:
        spaces[n] = pl.ANY
    return pl.pallas_call(
        kernel,
        out_shape=outs,
        in_specs=[pl.BlockSpec(memory_space=space) for space in spaces],
        out_specs=[pl.BlockSpec(memory_space=pl.ANY if hbm_out else pltpu.VMEM)] * len(outs),
        scratch_shapes=list(scratch),
        compiler_params=pltpu.CompilerParams(vmem_limit_bytes=limit),
        name=kernel.__name__,
        cost_estimate=pl.CostEstimate(flops=flops, bytes_accessed=nbytes, transcendentals=0),
    )(*ins)


def shape(*dims, dtype=BF16):
    return jax.ShapeDtypeStruct(dims, dtype)


def owners_of(dest_ref, dp):
    targets = dest_ref[pl.ds(dp, 1), :]
    owners = lax.shift_right_logical(targets, 7).astype(F32)
    across = jnp.broadcast_to(owners, (ROWS, ROWS))
    return across, across.T


def pack_kernel(ids_ref, dest_ref, proj_ref, out_ref, proj, packed, in_sem, out_sems):
    load = pltpu.make_async_copy(proj_ref, proj, in_sem)
    load.start()
    across, down = owners_of(dest_ref, ids_ref[0])
    square = (ROWS, ROWS)
    earlier = (across == down) & (iota(square, 0) < iota(square, 1))
    slot = jnp.sum(jnp.where(earlier, 1.0, 0.0), axis=0, keepdims=True)
    key = (across[0:1] * CAP + slot).astype(jnp.int32)
    pick = jnp.where(iota((N_DP * CAP, ROWS), 0) == key, 1.0, 0.0).astype(BF16)
    load.wait()
    stores = []
    for pair in range(0, HEADS, 2):
        for j in range(2):
            halves = []
            for block in (j, 2 + j):
                at = (block * HEADS + pair) * HEAD_DIM
                moved = dot_nn(pick, proj[:, at : at + 2 * HEAD_DIM])
                halves.append(moved.reshape(N_DP, CAP, 2 * HEAD_DIM))
            chunks = jnp.concatenate(halves, axis=1).astype(BF16)
            for h in range(2):
                packed[:, pair + h, :, j * HEAD_DIM : (j + 1) * HEAD_DIM] = chunks[
                    :, :, h * HEAD_DIM : (h + 1) * HEAD_DIM
                ]
        heads = slice(pair, pair + 2)
        stores.append(
            pltpu.make_async_copy(packed.at[:, heads], out_ref.at[:, heads], out_sems.at[pair // 2])
        )
        stores[-1].start()
    for store in stores:
        store.wait()


def head_columns(h):
    return pl.ds(pl.multiple_of(h * HEAD_DIM, HEAD_DIM), HEAD_DIM)


def block_rows(c):
    return pl.ds(pl.multiple_of(c * ROWS, ROWS), ROWS)


def side_kernel(ids_ref, dest_ref, grad_ref, *out_refs):
    *out_refs, home_ref = out_refs
    across, down = owners_of(dest_ref, ids_ref[0])
    earlier = (across == down) & (iota((ROWS, ROWS), 1) < iota((ROWS, ROWS), 0))
    rank = jnp.sum(jnp.where(earlier, 1.0, 0.0), axis=1, keepdims=True)
    home_ref[...] = pick_down((down[:, 0:1] * CAP + rank).astype(jnp.int32))
    group = ids_ref[0]
    mapping = dest_ref[...]
    landing = lax.shift_right_logical(mapping, 7) == group
    landing_f = jnp.where(landing, 1.0, 0.0)
    square = (ROWS, ROWS)
    before = jnp.where(iota(square, 0) < iota(square, 1), 1.0, 0.0).astype(BF16)
    slot = dot_nn(landing_f.astype(BF16), before)
    code = iota((N_DP, ROWS), 0).astype(F32) * CAP + slot
    place = jnp.where(landing, mapping & (ROWS - 1), ROWS)
    row_of = iota(square, 0)
    total = jnp.zeros(square, F32)
    for i in range(N_DP):
        total = total + jnp.where(row_of == place[i : i + 1], code[i : i + 1], 0.0)
    codes = jnp.broadcast_to(jnp.sum(total, axis=1, keepdims=True), square).T
    for k, out_ref in enumerate(out_refs):
        out_ref[:ROWS] = grad_ref[:, head_columns(ids_ref[2] ^ k)]
        out_ref[ROWS:] = codes[:CHUNK].astype(BF16)


def chunk_row(code, half):
    return (code >> 3) * CHUNK + half * CAP + (code & (CAP - 1))


def code_across(side_ref):
    return side_ref[ROWS : ROWS + CHUNK].astype(F32)[0:1]


def both_halves(code, axis):
    return jnp.concatenate([chunk_row(code, half) for half in range(2)], axis=axis)


def pick_down(code):
    lane = iota((2 * ROWS, N_DP * CHUNK), 1)
    return jnp.where(lane == both_halves(code, 0), 1.0, 0.0).astype(BF16)


def unpack_kernel(
    ids_ref, s0, s1, s2, s3, arrived_ref, gate_ref, query_ref, vk_ref,
):
    for k, side_ref in enumerate((s0, s1, s2, s3)):
        c = ids_ref[2] ^ k
        rows = block_rows(c)
        chunks = arrived_ref[:, c].reshape(N_DP * CHUNK, 2 * HEAD_DIM)
        code = jnp.broadcast_to(code_across(side_ref), (ROWS, ROWS)).T.astype(jnp.int32)
        moved = dot_nn(pick_down(code[:, 0:1]), chunks).astype(BF16)
        gate_ref[rows] = moved[:ROWS, :HEAD_DIM]
        vk_ref[rows, :HEAD_DIM] = moved[:ROWS, HEAD_DIM:]
        query_ref[rows] = moved[ROWS:, :HEAD_DIM]
        vk_ref[rows, HEAD_DIM:] = moved[ROWS:, HEAD_DIM:]


def user_bounds(lengths_ref):
    bounds, start = [], jnp.int32(0)
    for u in range(USERS):
        length = lengths_ref[0, u]
        padded = (length + BLOCK - 1) // BLOCK * BLOCK
        bounds.append((start, start + length, start + padded))
        start = start + padded
    return bounds


def first_key(positions, bounds):
    low = jnp.full(positions.shape, 2 * GROUP, jnp.int32)
    for start, end, _ in bounds:
        low = jnp.where((positions >= start) & (positions < end), start, low)
    return low


def half_scores(a, b):
    return dot_nt(a, b) * (0.5 * SCALE)


def silu_of(half, tanh):
    return half + half * tanh


def slope_of(half, tanh):
    return (0.5 + 0.5 * tanh) * (1.0 + half * (1.0 - tanh))


def pairs_allowed(key_pos, query_pos, bounds):
    low = first_key(query_pos, bounds)
    return (key_pos >= low) & (key_pos <= query_pos)


def steps_of(parts, quarters):
    for part, quarter in zip(parts, quarters):
        for at in range(0, PART, STEP):
            yield part, slice(at, at + STEP), quarter * PART + at


def forward_kernel(
    ids_ref, lengths_ref, s0, s1, s2, s3, gate_ref, query_ref, vk1_ref, vk2_ref, vk0_ref,
    mixed_ref, gate_grad_ref, l0, l1, l2, l3, held,
):
    bounds = user_bounds(lengths_ref)
    quarter = ids_ref[1]
    query_pos = quarter * PART + iota((PART, 1), 0)
    queries = query_ref[...]
    mixed_sum = jnp.zeros((PART, HEAD_DIM), F32)
    for vk_ref, rows, at in steps_of(
        (vk2_ref, vk1_ref, vk0_ref), (quarter - 2, quarter - 1, quarter)
    ):
        half = half_scores(queries, vk_ref[rows, HEAD_DIM:])
        allowed = pairs_allowed(at + iota((1, STEP), 1), query_pos, bounds)
        weights = jnp.where(allowed, silu_of(half, jnp.tanh(half)), 0.0).astype(BF16)
        mixed_sum = mixed_sum + dot_nn(weights, vk_ref[rows, :HEAD_DIM])
    center = mixed_sum - jnp.mean(mixed_sum, axis=-1, keepdims=True)
    inverse = lax.rsqrt(jnp.mean(center * center, axis=-1, keepdims=True) + EPSILON)
    normed = center * inverse
    gating = gate_ref[...].astype(F32)
    head = ids_ref[2]
    for k, part in enumerate((s0, s1, s2, s3)):
        held[block_rows(head ^ k), HEAD_DIM:] = part[:ROWS]
    upstream = held[:, HEAD_DIM:].astype(F32)
    layer = (normed * gating).astype(BF16)
    grad_normed = upstream * gating
    mixed_ref[...] = (
        (
            grad_normed
            - jnp.mean(grad_normed, axis=-1, keepdims=True)
            - normed * jnp.mean(grad_normed * normed, axis=-1, keepdims=True)
        )
        * inverse
    ).astype(BF16)
    gate_grad_ref[...] = (upstream * normed).astype(BF16)
    held[:, :HEAD_DIM] = layer
    for k, layer_ref in enumerate((l0, l1, l2, l3)):
        layer_ref[...] = held[block_rows(head ^ k), :HEAD_DIM]


def key_grads(keys, values, key_pos, queries, grad_mixed, query_pos, bounds):
    half = half_scores(keys, queries)
    allowed = pairs_allowed(key_pos, query_pos, bounds)
    tanh = jnp.tanh(half)
    weights = jnp.where(allowed, silu_of(half, tanh), 0.0).astype(BF16)
    slope = jnp.where(allowed, slope_of(half, tanh), 0.0)
    grad_scores = (dot_nt(values, grad_mixed) * slope).astype(BF16)
    return dot_nn(weights, grad_mixed), dot_nn(grad_scores, queries)


def query_grad_kernel(
    ids_ref, lengths_ref, s0, s1, s2, s3, mixed_ref, gate_grad_ref, query_ref,
    vk1_ref, vk2_ref, vk0_ref, out_ref, own_ref, picks_ref, done,
):
    bounds = user_bounds(lengths_ref)
    quarter = ids_ref[1]
    own_pos = quarter * PART + iota((PART, 1), 0)
    queries = query_ref[...]
    grad_mixed = mixed_ref[...]
    total = jnp.zeros((PART, HEAD_DIM), F32)
    for vk_ref, rows, at in steps_of(
        (vk2_ref, vk1_ref, vk0_ref), (quarter - 2, quarter - 1, quarter)
    ):
        keys = vk_ref[rows, HEAD_DIM:]
        half = half_scores(queries, keys)
        allowed = pairs_allowed(at + iota((1, STEP), 1), own_pos, bounds)
        slope = jnp.where(allowed, slope_of(half, jnp.tanh(half)), 0.0)
        grad_scores = (dot_nt(grad_mixed, vk_ref[rows, :HEAD_DIM]) * slope).astype(BF16)
        total = total + dot_nn(grad_scores, keys)
    done[0] = gate_grad_ref[...]
    done[1] = (total * SCALE).astype(BF16)
    back_picks(ids_ref, (s0, s1, s2, s3), picks_ref)
    pack_back(picks_ref, done, out_ref, 0)
    values, keys = vk0_ref[:, :HEAD_DIM], vk0_ref[:, HEAD_DIM:]
    sums = (0.0, 0.0)
    for part, rows, at in steps_of((query_ref,), (quarter,)):
        terms = key_grads(
            keys, values, own_pos, part[rows], mixed_ref[rows], at + iota((1, STEP), 1), bounds
        )
        sums = tuple(a + b for a, b in zip(sums, terms))
    for n in range(2):
        own_ref[n] = sums[n]


def back_picks(ids_ref, sides, picks_ref):
    sublane = iota((N_DP * CHUNK, 2 * ROWS), 0)
    for k, side_ref in enumerate(sides):
        at = both_halves(code_across(side_ref).astype(jnp.int32), 1)
        picks_ref[ids_ref[2] ^ k] = jnp.where(sublane == at, 1.0, 0.0).astype(BF16)


def pack_back(picks_ref, done, out_ref, j, finished=lambda c: None):
    for c in range(HEADS):
        rows = slice(c * ROWS, (c + 1) * ROWS)
        both = jnp.concatenate([done[0, rows], done[1, rows]], axis=0)
        out_ref[:, c, :, j * HEAD_DIM : (j + 1) * HEAD_DIM] = (
            dot_nn(picks_ref[c], both).astype(BF16).reshape(N_DP, CHUNK, HEAD_DIM)
        )
        finished(c)


def backward_kernel(
    ids_ref, lengths_ref, picks_ref, vk_ref, q2_ref, q1_ref, m2_ref, m1_ref,
    own_ref, gq_ref, out_ref, done, packed, sems,
):
    packed[:, :, :, :HEAD_DIM] = gq_ref[...]
    bounds = user_bounds(lengths_ref)
    quarter = ids_ref[1]
    own_pos = quarter * PART + iota((PART, 1), 0)
    values, keys = vk_ref[:, :HEAD_DIM], vk_ref[:, HEAD_DIM:]
    sums = (own_ref[0], own_ref[1])
    for (part, mixed), rows, at in steps_of(
        ((q1_ref, m1_ref), (q2_ref, m2_ref)), (quarter + 1, quarter + 2)
    ):
        terms = key_grads(
            keys, values, own_pos, part[rows], mixed[rows], at + iota((1, STEP), 1), bounds
        )
        sums = tuple(a + b for a, b in zip(sums, terms))
    done[0] = sums[0].astype(BF16)
    done[1] = (sums[1] * SCALE).astype(BF16)
    stores = []

    def send(c):
        stores.append(pltpu.make_async_copy(packed.at[:, c], out_ref.at[:, c], sems.at[c]))
        stores[-1].start()

    pack_back(picks_ref, done, packed, 1, send)
    for store in stores:
        store.wait()


def finish_kernel(
    ids_ref, home_ref, l0, l1, l2, l3, back_ref, grad_ref, out_ref, grads, layer, sems
):
    head = ids_ref[2]
    for k, layer_ref in enumerate((l0, l1, l2, l3)):
        layer[:, head_columns(head ^ k)] = layer_ref[...]
    stores = [pltpu.make_async_copy(layer, out_ref, sems.at[HEADS])]
    stores[0].start()
    pick = home_ref[...]
    for h in range(HEADS):
        chunks = back_ref[:, h].reshape(N_DP * CHUNK, 2 * HEAD_DIM)
        moved = dot_nn(pick, chunks).astype(BF16)
        for half in range(2):
            for j in range(2):
                block = 2 * half + j
                at = (block * HEADS + h) * HEAD_DIM
                columns = slice(at, at + HEAD_DIM)
                grads[:, columns] = moved[
                    half * ROWS : (half + 1) * ROWS, j * HEAD_DIM : (j + 1) * HEAD_DIM
                ]
                stores.append(
                    pltpu.make_async_copy(
                        grads.at[:, columns], grad_ref.at[:, columns], sems.at[HEADS + 1 + 4 * h + block]
                    )
                )
                stores[-1].start()
    for store in stores:
        store.wait()


def route(chunks):
    flat = chunks.reshape(N_DP * HEADS * CHUNK, 2 * HEAD_DIM)
    moved = lax.all_to_all(flat, ("dp", "h"), 0, 0, tiled=True)
    return moved.reshape(chunks.shape)


def from_quarter(array, by):
    pairs = [(i, i - by) for i in range(N_X) if 0 <= i - by < N_X]
    return lax.ppermute(array, "x", pairs)


def swap_heads(pieces):
    moved = [
        lax.ppermute(piece, "h", [(i, i ^ k) for i in range(HEADS)])
        for k, piece in enumerate(pieces)
        if k
    ]
    return [pieces[0], *moved]


def body(projected, destination, lengths, grad_out):
    ids = jnp.stack([lax.axis_index(axis) for axis in ("dp", "x", "h")]).astype(jnp.int32)
    mapping = destination.reshape(N_DP, ROWS)
    chunked = shape(N_DP, HEADS, CHUNK, 2 * HEAD_DIM)
    half_chunked = shape(N_DP, HEADS, CHUNK, HEAD_DIM)
    head_part = shape(PART, HEAD_DIM)
    pieces = [shape(ROWS, HEAD_DIM)] * HEADS
    (packed,) = call(
        pack_kernel, [chunked], (ids, mapping, projected), (1, 0, 0),
        scratch=[
            pltpu.VMEM(projected.shape, BF16), pltpu.VMEM(chunked.shape, BF16),
            pltpu.SemaphoreType.DMA, pltpu.SemaphoreType.DMA((2,)),
        ],
        flops=2 * 256 * 128 * 2048, nbytes=3 << 19, hbm_in=(2,), hbm_out=True, limit=62 * 1024 * 1024,
    )
    *side_out, home = call(
        side_kernel, [shape(ROWS + CHUNK, HEAD_DIM)] * HEADS + [shape(2 * ROWS, N_DP * CHUNK)], (ids, mapping, grad_out), (1, 0, 0),
        nbytes=3 << 17,
    )
    side = swap_heads(side_out)
    arrived = route(packed)
    gate, queries, vk = call(
        unpack_kernel, [head_part, head_part, shape(PART, 2 * HEAD_DIM)],
        (ids, *side, arrived), (1,) + (0,) * 5,
        flops=1 << 28, nbytes=2 << 20,
    )
    vk_parts = (from_quarter(vk, -1), from_quarter(vk, -2), vk)
    query_parts = (from_quarter(queries, 2), from_quarter(queries, 1))
    held = pltpu.VMEM((PART, 2 * HEAD_DIM), BF16)
    done = pltpu.VMEM((2, PART, HEAD_DIM), BF16)
    mixed, gate_grad, *layer = call(
        forward_kernel, [head_part, head_part, *pieces],
        (ids, lengths, *side, gate, queries, *vk_parts), (1, 1) + (0,) * 9,
        scratch=[held], flops=1 << 29, nbytes=2 << 20,
    )
    mixed_parts = (from_quarter(mixed, 2), from_quarter(mixed, 1))
    layer_home = swap_heads(layer)
    gq_back, own, picks = call(
        query_grad_kernel,
        [half_chunked, shape(2, PART, HEAD_DIM, dtype=F32), shape(HEADS, N_DP * CHUNK, 2 * ROWS)],
        (ids, lengths, *side, mixed, gate_grad, queries, *vk_parts), (1, 1) + (0,) * 10,
        scratch=[done], flops=1 << 29, nbytes=2 << 20,
    )
    (back,) = call(
        backward_kernel, [chunked],
        (ids, lengths, picks, vk, *query_parts, *mixed_parts, own, gq_back),
        (1, 1) + (0,) * 8,
        scratch=[done, pltpu.VMEM(chunked.shape, BF16), pltpu.SemaphoreType.DMA((HEADS,))],
        flops=1 << 30, nbytes=3 << 20, hbm_out=True,
    )
    returned = route(back)
    grad_projected, layer_output = call(
        finish_kernel, [shape(ROWS, 4 * HEADS * HEAD_DIM), shape(ROWS, HEADS * HEAD_DIM)],
        (ids, home, *layer_home, returned), (1, 0, 0, 0, 0, 0, 0),
        scratch=[
            pltpu.VMEM(projected.shape, BF16), pltpu.VMEM(grad_out.shape, BF16),
            pltpu.SemaphoreType.DMA((5 * HEADS + 1,)),
        ],
        flops=1 << 28, nbytes=2 << 20, hbm_out=True,
    )
    return (layer_output, grad_projected)


def solution(mesh):
    fine = Mesh(mesh.devices.reshape(N_DP, N_X, HEADS), ("dp", "x", "h"))
    rows = P(("dp", "x", "h"), None)
    in_specs = (rows, P(("x", "h"), None), P("dp", None), rows)
    return jax.shard_map(
        body, mesh=fine, in_specs=in_specs, out_specs=(rows, rows), check_vma=False
    )
```

time: 192 us -> 186 us (0.969)
  the two profiles are of different devices: /device:TPU:37 before, /device:TPU:39 now
where the time goes in v2:
time: 186 us; the launch traced here: 185 us
  waiting for transfers between devices  84.8 us (46%)
  starting transfers between devices  81.3 us (44%)
  Pallas kernels  17.5 us (9%)
    ppermute x6, waiting for transfers between devices, swap_heads(): lax.ppermute(piece, 'h', [(i, i ^ k) for i in range(HEADS)])  84.7 us
    ppermute x6, starting transfers between devices, swap_heads(): lax.ppermute(piece, 'h', [(i, i ^ k) for i in range(HEADS)])  33.2 us
    all_to_all x2, starting transfers between devices, route(): moved = lax.all_to_all(flat, ('dp', 'h'), 0, 0, tiled=True)  29.5 us
    ppermute x6, starting transfers between devices, from_quarter(): return lax.ppermute(array, 'x', pairs)  18.6 us
    pallas_call x7, Pallas kernels, call(): pl.pallas_call(kernel, out_shape=outs, in_specs=[pl.BlockSpec(memory_spac...  17.5 us
  transfers between devices with their start and end apart: 14, of which 4 were waited for; matrix products, arithmetic and copies ran while one was open for 0% of the time, Pallas kernels for 4%

profile of v2, /device:TPU:39, one launch (start us, length us, event | category | flops | bytes accessed | tf_op | source)
XLA Modules:
  0.0 185.2 jit_solution(11915994135346910391)
XLA Ops:
  1.3 3.1 %pack_kernel.1 = bf16[32,4,16,256]{3,2,1,0:T(8,128)(2,1)} custom-call(s32[3]{0:T(128)} %pad_add_fusion.ids_ref, s32[32,128]{1,0:T(8,128)} %bitcast.10, bf16[128,2048]{1,0:T(8,128)(2,1)} %proj_ref.1), custom_call_target="tpu_custom_call" | custom-call | flops 134217728 | bytes 1572864 | tf_op jit(solution)/shard_map/pack_kernel/pallas_call | solution.py:48
  4.4 19.6 %all-to-all-start = ((bf16[128,16,256]{2,1,0:T(8,128)(2,1)}), bf16[128,16,256]{2,1,0:T(8,128)(2,1)S(1)}, u32[]{:S(2)}, u32[]{:S(2)}) async-start(bf16[128,16,256]{2,1,0:T(8,128)(2,1)} %bitcast.12), calls=%async_computation | async-start | bytes 2097152 | tf_op jit(solution)/shard_map/all_to_all | solution.py:371
  25.2 2.3 %collective-permute-start = (bf16[144,128]{1,0:T(8,128)(2,1)S(1)}, bf16[144,128]{1,0:T(8,128)(2,1)S(1)}, u32[]{:S(2)}, u32[]{:S(2)}) collective-permute-start(bf16[144,128]{1,0:T(8,128)(2,1)S(1)} %get-tuple-element.23), channel_id=1, source_target_pairs={{0,1},{1,0},{2,3},{3,2},{4,5},{5,4},{6,7},{7,6},{8,9},{9,8},{10,11... | collective-permute-start | bytes 110600 | tf_op jit(solution)/shard_map/ppermute | solution.py:382
  27.5 10.9 %collective-permute-start.1 = (bf16[144,128]{1,0:T(8,128)(2,1)S(1)}, bf16[144,128]{1,0:T(8,128)(2,1)S(1)}, u32[]{:S(2)}, u32[]{:S(2)}) collective-permute-start(bf16[144,128]{1,0:T(8,128)(2,1)S(1)} %get-tuple-element.24), channel_id=1, source_target_pairs={{0,2},{1,3},{2,0},{3,1},{4,6},{5,7},{6,4},{7,5},{8,10},{9,11},{10,... | collective-permute-start | bytes 110600 | tf_op jit(solution)/shard_map/ppermute | solution.py:382
  38.4 3.4 %collective-permute-start.2 = (bf16[144,128]{1,0:T(8,128)(2,1)S(1)}, bf16[144,128]{1,0:T(8,128)(2,1)S(1)}, u32[]{:S(2)}, u32[]{:S(2)}) collective-permute-start(bf16[144,128]{1,0:T(8,128)(2,1)S(1)} %get-tuple-element.25), channel_id=1, source_target_pairs={{0,3},{1,2},{2,1},{3,0},{4,7},{5,6},{6,5},{7,4},{8,11},{9,10},{10,... | collective-permute-start | bytes 110600 | tf_op jit(solution)/shard_map/ppermute | solution.py:382
  41.8 40.0 %collective-permute-done.1.s2 = bf16[144,128]{1,0:T(8,128)(2,1)S(1)} collective-permute-done((bf16[144,128]{1,0:T(8,128)(2,1)S(1)}, bf16[144,128]{1,0:T(8,128)(2,1)S(1)}, u32[]{:S(2)}, u32[]{:S(2)}) %collective-permute-start.1) | collective-permute-done | bytes 36896 | tf_op jit(solution)/shard_map/ppermute | solution.py:382
  81.9 2.0 %collective-permute-done.2.s3 = bf16[144,128]{1,0:T(8,128)(2,1)S(1)} collective-permute-done((bf16[144,128]{1,0:T(8,128)(2,1)S(1)}, bf16[144,128]{1,0:T(8,128)(2,1)S(1)}, u32[]{:S(2)}, u32[]{:S(2)}) %collective-permute-start.2) | collective-permute-done | bytes 36896 | tf_op jit(solution)/shard_map/ppermute | solution.py:382
  83.9 1.2 unpack_kernel.1
  85.1 1.3 collective-permute-start.3
  86.4 1.3 collective-permute-start.4
  87.7 5.5 %collective-permute-start.8 = (bf16[512,128]{1,0:T(8,128)(2,1)S(1)}, bf16[512,128]{1,0:T(8,128)(2,1)S(1)}, u32[]{:S(2)}, u32[]{:S(2)}) collective-permute-start(bf16[512,128]{1,0:T(8,128)(2,1)S(1)} %get-tuple-element.27.query_ref), channel_id=1, source_target_pairs={{8,0},{12,4},{9,1},{13,5},{10,2},{14,6},{11,3},{15,7},{24,16},{28,... | collective-permute-start | bytes 393224 | tf_op jit(solution)/shard_map/ppermute | solution.py:377
  93.2 4.0 %collective-permute-start.9 = (bf16[512,128]{1,0:T(8,128)(2,1)S(1)}, bf16[512,128]{1,0:T(8,128)(2,1)S(1)}, u32[]{:S(2)}, u32[]{:S(2)}) collective-permute-start(bf16[512,128]{1,0:T(8,128)(2,1)S(1)} %get-tuple-element.27.query_ref), channel_id=1, source_target_pairs={{4,0},{8,4},{12,8},{5,1},{9,5},{13,9},{6,2},{10,6},{14,10},{7,3},{... | collective-permute-start | bytes 393224 | tf_op jit(solution)/shard_map/ppermute | solution.py:377
  97.3 2.3 %forward_kernel.1 = (bf16[512,128]{1,0:T(8,128)(2,1)S(1)}, bf16[512,128]{1,0:T(8,128)(2,1)S(1)}, bf16[128,128]{1,0:T(8,128)(2,1)S(1)}, bf16[128,128]{1,0:T(8,128...) custom-call(s32[3]{0:T(128)S(1)} %copy-done.2, s32[1,3]{1,0:T(1,128)S(1)} %copy-done.3, ...), custom_call_target="tpu_custom_call" | custom-call | flops 536870912 | bytes 2097152 | tf_op jit(solution)/shard_map/forward_kernel/pallas_call | solution.py:48
  99.6 1.9 %collective-permute-start.10 = (bf16[512,128]{1,0:T(8,128)(2,1)S(1)}, bf16[512,128]{1,0:T(8,128)(2,1)S(1)}, u32[]{:S(2)}, u32[]{:S(2)}) collective-permute-start(bf16[512,128]{1,0:T(8,128)(2,1)S(1)} %get-tuple-element.33.mixed_ref), channel_id=1, source_target_pairs={{8,0},{12,4},{9,1},{13,5},{10,2},{14,6},{11,3},{15,7},{24,16},{28,... | collective-permute-start | bytes 393224 | tf_op jit(solution)/shard_map/ppermute | solution.py:377
  101.5 4.7 %collective-permute-start.11 = (bf16[512,128]{1,0:T(8,128)(2,1)S(1)}, bf16[512,128]{1,0:T(8,128)(2,1)S(1)}, u32[]{:S(2)}, u32[]{:S(2)}) collective-permute-start(bf16[512,128]{1,0:T(8,128)(2,1)S(1)} %get-tuple-element.33.mixed_ref), channel_id=1, source_target_pairs={{4,0},{8,4},{12,8},{5,1},{9,5},{13,9},{6,2},{10,6},{14,10},{7,3},{... | collective-permute-start | bytes 393224 | tf_op jit(solution)/shard_map/ppermute | solution.py:377
  106.1 4.2 %query_grad_kernel.1 = (bf16[32,4,16,128]{3,2,1,0:T(8,128)(2,1)S(1)}, f32[2,512,128]{2,1,0:T(8,128)S(1)}, bf16[4,512,256]{2,1,0:T(8,128)(2,1)S(1)}) custom-call(s32[3]{0:T(128)S(1)} %copy-done.2, s32[1,3]{1,0:T(1,128)S(1)} %copy-done.3, bf16[144,128]{1,0:T(8,128)(2,1)S(1)} %get-tuple-element.22.s0, bf16[144,128]{1,0:T(8,128)(2,1)S(1)} %collective-permute-done.s1, ...), custom_call_target="tpu_custom_call" | custom-call | flops 536870912 | bytes 2097152 | tf_op jit(solution)/shard_map/query_grad_kernel/pallas_call | solution.py:48
  110.4 3.8 %backward_kernel.1 = bf16[32,4,16,256]{3,2,1,0:T(8,128)(2,1)} custom-call(s32[3]{0:T(128)S(1)} %copy-done.2, s32[1,3]{1,0:T(1,128)S(1)} %copy-done.3, bf16[4,512,256]{2,1,0:T(8,128)(2,1)S(1)} %get-tuple-element.35.picks_ref, bf16[512,256]{1,0:T(8,128)(2,1)S(1)} %get-tuple-element.28.vk0_ref.vk_ref, bf16[512,128]{1,0:T(8,128)(2,1)S(1)} %collective-permute-done.8.q2_ref, ...), custom_call_target="tpu_custom_call" | custom-call | flops 1073741824 | bytes 3145728 | tf_op jit(solution)/shard_map/backward_kernel/pallas_call | solution.py:48
  114.1 9.8 %all-to-all-start.1 = ((bf16[128,16,256]{2,1,0:T(8,128)(2,1)}), bf16[128,16,256]{2,1,0:T(8,128)(2,1)S(1)}, u32[]{:S(2)}, u32[]{:S(2)}) async-start(bf16[128,16,256]{2,1,0:T(8,128)(2,1)} %bitcast.6), calls=%async_computation.1 | async-start | bytes 2097152 | tf_op jit(solution)/shard_map/all_to_all | solution.py:371
  124.0 2.3 %collective-permute-start.5 = (bf16[128,128]{1,0:T(8,128)(2,1)S(1)}, bf16[128,128]{1,0:T(8,128)(2,1)S(1)}, u32[]{:S(2)}, u32[]{:S(2)}) collective-permute-start(bf16[128,128]{1,0:T(8,128)(2,1)S(1)} %get-tuple-element.30), channel_id=1, source_target_pairs={{0,1},{1,0},{2,3},{3,2},{4,5},{5,4},{6,7},{7,6},{8,9},{9,8},{10,11... | collective-permute-start | bytes 98312 | tf_op jit(solution)/shard_map/ppermute | solution.py:382
  126.2 10.9 %collective-permute-start.6 = (bf16[128,128]{1,0:T(8,128)(2,1)S(1)}, bf16[128,128]{1,0:T(8,128)(2,1)S(1)}, u32[]{:S(2)}, u32[]{:S(2)}) collective-permute-start(bf16[128,128]{1,0:T(8,128)(2,1)S(1)} %get-tuple-element.31), channel_id=1, source_target_pairs={{0,2},{1,3},{2,0},{3,1},{4,6},{5,7},{6,4},{7,5},{8,10},{9,11},{10,... | collective-permute-start | bytes 98312 | tf_op jit(solution)/shard_map/ppermute | solution.py:382
  137.2 3.4 %collective-permute-start.7 = (bf16[128,128]{1,0:T(8,128)(2,1)S(1)}, bf16[128,128]{1,0:T(8,128)(2,1)S(1)}, u32[]{:S(2)}, u32[]{:S(2)}) collective-permute-start(bf16[128,128]{1,0:T(8,128)(2,1)S(1)} %get-tuple-element.32), channel_id=1, source_target_pairs={{0,3},{1,2},{2,1},{3,0},{4,7},{5,6},{6,5},{7,4},{8,11},{9,10},{10,... | collective-permute-start | bytes 98312 | tf_op jit(solution)/shard_map/ppermute | solution.py:382
  140.6 41.0 %collective-permute-done.6.l2 = bf16[128,128]{1,0:T(8,128)(2,1)S(1)} collective-permute-done((bf16[128,128]{1,0:T(8,128)(2,1)S(1)}, bf16[128,128]{1,0:T(8,128)(2,1)S(1)}, u32[]{:S(2)}, u32[]{:S(2)}) %collective-permute-start.6) | collective-permute-done | bytes 32800 | tf_op jit(solution)/shard_map/ppermute | solution.py:382
  181.6 1.6 collective-permute-done.7.l3
  183.2 1.8 finish_kernel.1
  (20 shorter events, 1.9 us)
Async XLA Ops:
  4.4 19.7 %copy-start = (bf16[128,512]{1,0:T(8,128)(2,1)S(1)}, bf16[128,512]{1,0:T(8,128)(2,1)}, u32[]{:S(2)}) copy-start(bf16[128,512]{1,0:T(8,128)(2,1)} %grad_ref.1) | copy-start | bytes 393220
  4.4 19.7 %copy-start.1 = (s32[1,4096]{1,0:T(1,128)S(1)}, s32[1,4096]{1,0:T(1,128)}, u32[]{:S(2)}) copy-start(s32[1,4096]{1,0:T(1,128)} %param.5) | copy-start | bytes 49156
  4.4 19.7 %copy-start.2 = (s32[3]{0:T(128)S(1)}, s32[3]{0:T(128)}, u32[]{:S(2)}) copy-start(s32[3]{0:T(128)} %pad_add_fusion.ids_ref) | copy-start | bytes 40
  4.4 79.5 %all-to-all-start = ((bf16[128,16,256]{2,1,0:T(8,128)(2,1)}), bf16[128,16,256]{2,1,0:T(8,128)(2,1)S(1)}, u32[]{:S(2)}, u32[]{:S(2)}) async-start(bf16[128,16,256]{2,1,0:T(8,128)(2,1)} %bitcast.12), calls=%async_computation | async-start | bytes 2097152 | tf_op jit(solution)/shard_map/all_to_all | solution.py:371
  25.2 16.6 %collective-permute-start = (bf16[144,128]{1,0:T(8,128)(2,1)S(1)}, bf16[144,128]{1,0:T(8,128)(2,1)S(1)}, u32[]{:S(2)}, u32[]{:S(2)}) collective-permute-start(bf16[144,128]{1,0:T(8,128)(2,1)S(1)} %get-tuple-element.23), channel_id=1, source_target_pairs={{0,1},{1,0},{2,3},{3,2},{4,5},{5,4},{6,7},{7,6},{8,9},{9,8},{10,11... | collective-permute-start | bytes 110600 | tf_op jit(solution)/shard_map/ppermute | solution.py:382
  27.5 54.4 %collective-permute-start.1 = (bf16[144,128]{1,0:T(8,128)(2,1)S(1)}, bf16[144,128]{1,0:T(8,128)(2,1)S(1)}, u32[]{:S(2)}, u32[]{:S(2)}) collective-permute-start(bf16[144,128]{1,0:T(8,128)(2,1)S(1)} %get-tuple-element.24), channel_id=1, source_target_pairs={{0,2},{1,3},{2,0},{3,1},{4,6},{5,7},{6,4},{7,5},{8,10},{9,11},{10,... | collective-permute-start | bytes 110600 | tf_op jit(solution)/shard_map/ppermute | solution.py:382
  38.4 45.5 %collective-permute-start.2 = (bf16[144,128]{1,0:T(8,128)(2,1)S(1)}, bf16[144,128]{1,0:T(8,128)(2,1)S(1)}, u32[]{:S(2)}, u32[]{:S(2)}) collective-permute-start(bf16[144,128]{1,0:T(8,128)(2,1)S(1)} %get-tuple-element.25), channel_id=1, source_target_pairs={{0,3},{1,2},{2,1},{3,0},{4,7},{5,6},{6,5},{7,4},{8,11},{9,10},{10,... | collective-permute-start | bytes 110600 | tf_op jit(solution)/shard_map/ppermute | solution.py:382
  85.1 12.1 %collective-permute-start.3 = (bf16[512,256]{1,0:T(8,128)(2,1)S(1)}, bf16[512,256]{1,0:T(8,128)(2,1)S(1)}, u32[]{:S(2)}, u32[]{:S(2)}) collective-permute-start(bf16[512,256]{1,0:T(8,128)(2,1)S(1)} %get-tuple-element.28.vk0_ref.vk_ref), channel_id=1, source_target_pairs={{0,4},{4,8},{8,12},{1,5},{5,9},{9,13},{2,6},{6,10},{10,14},{3,7},{... | collective-permute-start | bytes 786440 | tf_op jit(solution)/shard_map/ppermute | solution.py:377
  86.4 10.9 %collective-permute-start.4 = (bf16[512,256]{1,0:T(8,128)(2,1)S(1)}, bf16[512,256]{1,0:T(8,128)(2,1)S(1)}, u32[]{:S(2)}, u32[]{:S(2)}) collective-permute-start(bf16[512,256]{1,0:T(8,128)(2,1)S(1)} %get-tuple-element.28.vk0_ref.vk_ref), channel_id=1, source_target_pairs={{0,8},{4,12},{1,9},{5,13},{2,10},{6,14},{3,11},{7,15},{16,24},{20,... | collective-permute-start | bytes 786440 | tf_op jit(solution)/shard_map/ppermute | solution.py:377
  87.7 9.6 %copy-start.3 = (s32[1,3]{1,0:T(1,128)S(1)}, s32[1,3]{1,0:T(1,128)}, u32[]{:S(2)}) copy-start(s32[1,3]{1,0:T(1,128)} %lengths_ref.5) | copy-start | bytes 40
  87.7 22.7 %collective-permute-start.8 = (bf16[512,128]{1,0:T(8,128)(2,1)S(1)}, bf16[512,128]{1,0:T(8,128)(2,1)S(1)}, u32[]{:S(2)}, u32[]{:S(2)}) collective-permute-start(bf16[512,128]{1,0:T(8,128)(2,1)S(1)} %get-tuple-element.27.query_ref), channel_id=1, source_target_pairs={{8,0},{12,4},{9,1},{13,5},{10,2},{14,6},{11,3},{15,7},{24,16},{28,... | collective-permute-start | bytes 393224 | tf_op jit(solution)/shard_map/ppermute | solution.py:377
  93.2 17.1 %collective-permute-start.9 = (bf16[512,128]{1,0:T(8,128)(2,1)S(1)}, bf16[512,128]{1,0:T(8,128)(2,1)S(1)}, u32[]{:S(2)}, u32[]{:S(2)}) collective-permute-start(bf16[512,128]{1,0:T(8,128)(2,1)S(1)} %get-tuple-element.27.query_ref), channel_id=1, source_target_pairs={{4,0},{8,4},{12,8},{5,1},{9,5},{13,9},{6,2},{10,6},{14,10},{7,3},{... | collective-permute-start | bytes 393224 | tf_op jit(solution)/shard_map/ppermute | solution.py:377
  99.6 10.8 %collective-permute-start.10 = (bf16[512,128]{1,0:T(8,128)(2,1)S(1)}, bf16[512,128]{1,0:T(8,128)(2,1)S(1)}, u32[]{:S(2)}, u32[]{:S(2)}) collective-permute-start(bf16[512,128]{1,0:T(8,128)(2,1)S(1)} %get-tuple-element.33.mixed_ref), channel_id=1, source_target_pairs={{8,0},{12,4},{9,1},{13,5},{10,2},{14,6},{11,3},{15,7},{24,16},{28,... | collective-permute-start | bytes 393224 | tf_op jit(solution)/shard_map/ppermute | solution.py:377
  101.5 8.9 %collective-permute-start.11 = (bf16[512,128]{1,0:T(8,128)(2,1)S(1)}, bf16[512,128]{1,0:T(8,128)(2,1)S(1)}, u32[]{:S(2)}, u32[]{:S(2)}) collective-permute-start(bf16[512,128]{1,0:T(8,128)(2,1)S(1)} %get-tuple-element.33.mixed_ref), channel_id=1, source_target_pairs={{4,0},{8,4},{12,8},{5,1},{9,5},{13,9},{6,2},{10,6},{14,10},{7,3},{... | collective-permute-start | bytes 393224 | tf_op jit(solution)/shard_map/ppermute | solution.py:377
  114.1 69.1 %all-to-all-start.1 = ((bf16[128,16,256]{2,1,0:T(8,128)(2,1)}), bf16[128,16,256]{2,1,0:T(8,128)(2,1)S(1)}, u32[]{:S(2)}, u32[]{:S(2)}) async-start(bf16[128,16,256]{2,1,0:T(8,128)(2,1)} %bitcast.6), calls=%async_computation.1 | async-start | bytes 2097152 | tf_op jit(solution)/shard_map/all_to_all | solution.py:371
  124.0 16.6 %collective-permute-start.5 = (bf16[128,128]{1,0:T(8,128)(2,1)S(1)}, bf16[128,128]{1,0:T(8,128)(2,1)S(1)}, u32[]{:S(2)}, u32[]{:S(2)}) collective-permute-start(bf16[128,128]{1,0:T(8,128)(2,1)S(1)} %get-tuple-element.30), channel_id=1, source_target_pairs={{0,1},{1,0},{2,3},{3,2},{4,5},{5,4},{6,7},{7,6},{8,9},{9,8},{10,11... | collective-permute-start | bytes 98312 | tf_op jit(solution)/shard_map/ppermute | solution.py:382
  126.2 55.4 %collective-permute-start.6 = (bf16[128,128]{1,0:T(8,128)(2,1)S(1)}, bf16[128,128]{1,0:T(8,128)(2,1)S(1)}, u32[]{:S(2)}, u32[]{:S(2)}) collective-permute-start(bf16[128,128]{1,0:T(8,128)(2,1)S(1)} %get-tuple-element.31), channel_id=1, source_target_pairs={{0,2},{1,3},{2,0},{3,1},{4,6},{5,7},{6,4},{7,5},{8,10},{9,11},{10,... | collective-permute-start | bytes 98312 | tf_op jit(solution)/shard_map/ppermute | solution.py:382
  137.2 46.1 %collective-permute-start.7 = (bf16[128,128]{1,0:T(8,128)(2,1)S(1)}, bf16[128,128]{1,0:T(8,128)(2,1)S(1)}, u32[]{:S(2)}, u32[]{:S(2)}) collective-permute-start(bf16[128,128]{1,0:T(8,128)(2,1)S(1)} %get-tuple-element.32), channel_id=1, source_target_pairs={{0,3},{1,2},{2,1},{3,0},{4,7},{5,6},{6,5},{7,4},{8,11},{9,10},{10,... | collective-permute-start | bytes 98312 | tf_op jit(solution)/shard_map/ppermute | solution.py:382

commit v3 on v2

--- a/solution.py
+++ b/solution.py
@@ -41,8 +41,10 @@
     return lax.broadcasted_iota(jnp.int32, shape, dim)
 
 
-def call(kernel, outs, ins, smem, scratch=(), flops=0, nbytes=0, hbm_in=(), hbm_out=False, limit=VMEM_LIMIT):
-    spaces = [pltpu.SMEM if s else pltpu.VMEM for s in smem]
+def call(kernel, outs, ins, smem=(), scratch=(), flops=0, nbytes=0, hbm_in=(), hbm_out=False, limit=VMEM_LIMIT):
+    spaces = [pltpu.VMEM] * len(ins)
+    for n in smem:
+        spaces[n] = pltpu.SMEM
     for n in hbm_in:
         spaces[n] = pl.ANY
     return pl.pallas_call(
@@ -68,10 +70,10 @@
     return across, across.T
 
 
-def pack_kernel(ids_ref, dest_ref, proj_ref, out_ref, proj, packed, in_sem, out_sems):
+def pack_kernel(dest_ref, proj_ref, out_ref, proj, packed, in_sem, out_sems):
     load = pltpu.make_async_copy(proj_ref, proj, in_sem)
     load.start()
-    across, down = owners_of(dest_ref, ids_ref[0])
+    across, down = owners_of(dest_ref, lax.axis_index("dp"))
     square = (ROWS, ROWS)
     earlier = (across == down) & (iota(square, 0) < iota(square, 1))
     slot = jnp.sum(jnp.where(earlier, 1.0, 0.0), axis=0, keepdims=True)
@@ -108,13 +110,34 @@
     return pl.ds(pl.multiple_of(c * ROWS, ROWS), ROWS)
 
 
-def side_kernel(ids_ref, dest_ref, grad_ref, *out_refs):
-    *out_refs, home_ref = out_refs
-    across, down = owners_of(dest_ref, ids_ref[0])
+def user_bounds(lengths_ref):
+    bounds, start = [], jnp.int32(0)
+    for u in range(USERS):
+        length = lengths_ref[0, u]
+        padded = (length + BLOCK - 1) // BLOCK * BLOCK
+        bounds.append((start, start + length, start + padded))
+        start = start + padded
+    return bounds
+
+
+def first_key(positions, bounds):
+    low = jnp.full(positions.shape, 2 * GROUP, jnp.int32)
+    for start, end, _ in bounds:
+        low = jnp.where((positions >= start) & (positions < end), start, low)
+    return low
+
+
+def side_kernel(lengths_ref, dest_ref, grad_ref, *out_refs):
+    *out_refs, home_ref, low_ref, low_rows_ref = out_refs
+    bounds = user_bounds(lengths_ref)
+    base = lax.axis_index("x") * PART
+    low_ref[...] = first_key(base + iota(low_ref.shape, 0), bounds)
+    low_rows_ref[...] = first_key(base + iota(low_rows_ref.shape, 1), bounds)
+    across, down = owners_of(dest_ref, lax.axis_index("dp"))
     earlier = (across == down) & (iota((ROWS, ROWS), 1) < iota((ROWS, ROWS), 0))
     rank = jnp.sum(jnp.where(earlier, 1.0, 0.0), axis=1, keepdims=True)
     home_ref[...] = pick_down((down[:, 0:1] * CAP + rank).astype(jnp.int32))
-    group = ids_ref[0]
+    group = lax.axis_index("dp")
     mapping = dest_ref[...]
     landing = lax.shift_right_logical(mapping, 7) == group
     landing_f = jnp.where(landing, 1.0, 0.0)
@@ -129,7 +152,7 @@
         total = total + jnp.where(row_of == place[i : i + 1], code[i : i + 1], 0.0)
     codes = jnp.broadcast_to(jnp.sum(total, axis=1, keepdims=True), square).T
     for k, out_ref in enumerate(out_refs):
-        out_ref[:ROWS] = grad_ref[:, head_columns(ids_ref[2] ^ k)]
+        out_ref[:ROWS] = grad_ref[:, head_columns(lax.axis_index("h") ^ k)]
         out_ref[ROWS:] = codes[:CHUNK].astype(BF16)
 
 
@@ -150,14 +173,21 @@
     return jnp.where(lane == both_halves(code, 0), 1.0, 0.0).astype(BF16)
 
 
+def code_of_block(c, head, sides):
+    code = jnp.zeros((1, ROWS), F32)
+    for k, side_ref in enumerate(sides):
+        code = jnp.where((head ^ k) == c, code_across(side_ref), code)
+    return code
+
+
 def unpack_kernel(
-    ids_ref, s0, s1, s2, s3, arrived_ref, gate_ref, query_ref, vk_ref,
+    s0, s1, s2, s3, arrived_ref, gate_ref, query_ref, vk_ref,
 ):
-    for k, side_ref in enumerate((s0, s1, s2, s3)):
-        c = ids_ref[2] ^ k
-        rows = block_rows(c)
+    for c in range(HEADS):
+        rows = slice(c * ROWS, (c + 1) * ROWS)
+        code = code_of_block(c, lax.axis_index("h"), (s0, s1, s2, s3))
+        code = jnp.broadcast_to(code, (ROWS, ROWS)).T.astype(jnp.int32)
         chunks = arrived_ref[:, c].reshape(N_DP * CHUNK, 2 * HEAD_DIM)
-        code = jnp.broadcast_to(code_across(side_ref), (ROWS, ROWS)).T.astype(jnp.int32)
         moved = dot_nn(pick_down(code[:, 0:1]), chunks).astype(BF16)
         gate_ref[rows] = moved[:ROWS, :HEAD_DIM]
         vk_ref[rows, :HEAD_DIM] = moved[:ROWS, HEAD_DIM:]
@@ -165,23 +195,6 @@
         vk_ref[rows, HEAD_DIM:] = moved[ROWS:, HEAD_DIM:]
 
 
-def user_bounds(lengths_ref):
-    bounds, start = [], jnp.int32(0)
-    for u in range(USERS):
-        length = lengths_ref[0, u]
-        padded = (length + BLOCK - 1) // BLOCK * BLOCK
-        bounds.append((start, start + length, start + padded))
-        start = start + padded
-    return bounds
-
-
-def first_key(positions, bounds):
-    low = jnp.full(positions.shape, 2 * GROUP, jnp.int32)
-    for start, end, _ in bounds:
-        low = jnp.where((positions >= start) & (positions < end), start, low)
-    return low
-
-
 def half_scores(a, b):
     return dot_nt(a, b) * (0.5 * SCALE)
 
@@ -194,8 +207,11 @@
     return (0.5 + 0.5 * tanh) * (1.0 + half * (1.0 - tanh))
 
 
-def pairs_allowed(key_pos, query_pos, bounds):
-    low = first_key(query_pos, bounds)
+def low_down(low_ref):
+    return jnp.concatenate([low_ref[...]] * (STEP // ROWS), axis=1)
+
+
+def pairs_allowed(key_pos, query_pos, low):
     return (key_pos >= low) & (key_pos <= query_pos)
 
 
@@ -206,11 +222,11 @@
 
 
 def forward_kernel(
-    ids_ref, lengths_ref, s0, s1, s2, s3, gate_ref, query_ref, vk1_ref, vk2_ref, vk0_ref,
+    low_ref, s0, s1, s2, s3, gate_ref, query_ref, vk1_ref, vk2_ref, vk0_ref,
     mixed_ref, gate_grad_ref, l0, l1, l2, l3, held,
 ):
-    bounds = user_bounds(lengths_ref)
-    quarter = ids_ref[1]
+    low = low_down(low_ref)
+    quarter = lax.axis_index("x")
     query_pos = quarter * PART + iota((PART, 1), 0)
     queries = query_ref[...]
     mixed_sum = jnp.zeros((PART, HEAD_DIM), F32)
@@ -218,14 +234,14 @@
         (vk2_ref, vk1_ref, vk0_ref), (quarter - 2, quarter - 1, quarter)
     ):
         half = half_scores(queries, vk_ref[rows, HEAD_DIM:])
-        allowed = pairs_allowed(at + iota((1, STEP), 1), query_pos, bounds)
+        allowed = pairs_allowed(at + iota((1, STEP), 1), query_pos, low)
         weights = jnp.where(allowed, silu_of(half, jnp.tanh(half)), 0.0).astype(BF16)
         mixed_sum = mixed_sum + dot_nn(weights, vk_ref[rows, :HEAD_DIM])
     center = mixed_sum - jnp.mean(mixed_sum, axis=-1, keepdims=True)
     inverse = lax.rsqrt(jnp.mean(center * center, axis=-1, keepdims=True) + EPSILON)
     normed = center * inverse
     gating = gate_ref[...].astype(F32)
-    head = ids_ref[2]
+    head = lax.axis_index("h")
     for k, part in enumerate((s0, s1, s2, s3)):
         held[block_rows(head ^ k), HEAD_DIM:] = part[:ROWS]
     upstream = held[:, HEAD_DIM:].astype(F32)
@@ -245,9 +261,9 @@
         layer_ref[...] = held[block_rows(head ^ k), :HEAD_DIM]
 
 
-def key_grads(keys, values, key_pos, queries, grad_mixed, query_pos, bounds):
+def key_grads(keys, values, key_pos, queries, grad_mixed, query_pos, low):
     half = half_scores(keys, queries)
-    allowed = pairs_allowed(key_pos, query_pos, bounds)
+    allowed = pairs_allowed(key_pos, query_pos, low)
     tanh = jnp.tanh(half)
     weights = jnp.where(allowed, silu_of(half, tanh), 0.0).astype(BF16)
     slope = jnp.where(allowed, slope_of(half, tanh), 0.0)
@@ -256,11 +272,11 @@
 
 
 def query_grad_kernel(
-    ids_ref, lengths_ref, s0, s1, s2, s3, mixed_ref, gate_grad_ref, query_ref,
+    low_ref, low_rows_ref, s0, s1, s2, s3, mixed_ref, gate_grad_ref, query_ref,
     vk1_ref, vk2_ref, vk0_ref, out_ref, own_ref, picks_ref, done,
 ):
-    bounds = user_bounds(lengths_ref)
-    quarter = ids_ref[1]
+    low = low_down(low_ref)
+    quarter = lax.axis_index("x")
     own_pos = quarter * PART + iota((PART, 1), 0)
     queries = query_ref[...]
     grad_mixed = mixed_ref[...]
@@ -270,30 +286,31 @@
     ):
         keys = vk_ref[rows, HEAD_DIM:]
         half = half_scores(queries, keys)
-        allowed = pairs_allowed(at + iota((1, STEP), 1), own_pos, bounds)
+        allowed = pairs_allowed(at + iota((1, STEP), 1), own_pos, low)
         slope = jnp.where(allowed, slope_of(half, jnp.tanh(half)), 0.0)
         grad_scores = (dot_nt(grad_mixed, vk_ref[rows, :HEAD_DIM]) * slope).astype(BF16)
         total = total + dot_nn(grad_scores, keys)
     done[0] = gate_grad_ref[...]
     done[1] = (total * SCALE).astype(BF16)
-    back_picks(ids_ref, (s0, s1, s2, s3), picks_ref)
+    back_picks((s0, s1, s2, s3), picks_ref)
     pack_back(picks_ref, done, out_ref, 0)
     values, keys = vk0_ref[:, :HEAD_DIM], vk0_ref[:, HEAD_DIM:]
     sums = (0.0, 0.0)
     for part, rows, at in steps_of((query_ref,), (quarter,)):
         terms = key_grads(
-            keys, values, own_pos, part[rows], mixed_ref[rows], at + iota((1, STEP), 1), bounds
+            keys, values, own_pos, part[rows], mixed_ref[rows], at + iota((1, STEP), 1),
+            low_rows_ref[0:1, rows],
         )
         sums = tuple(a + b for a, b in zip(sums, terms))
     for n in range(2):
         own_ref[n] = sums[n]
 
 
-def back_picks(ids_ref, sides, picks_ref):
+def back_picks(sides, picks_ref):
     sublane = iota((N_DP * CHUNK, 2 * ROWS), 0)
     for k, side_ref in enumerate(sides):
         at = both_halves(code_across(side_ref).astype(jnp.int32), 1)
-        picks_ref[ids_ref[2] ^ k] = jnp.where(sublane == at, 1.0, 0.0).astype(BF16)
+        picks_ref[lax.axis_index("h") ^ k] = jnp.where(sublane == at, 1.0, 0.0).astype(BF16)
 
 
 def pack_back(picks_ref, done, out_ref, j, finished=lambda c: None):
@@ -307,20 +324,20 @@
 
 
 def backward_kernel(
-    ids_ref, lengths_ref, picks_ref, vk_ref, q2_ref, q1_ref, m2_ref, m1_ref,
+    low_rows_ref, picks_ref, vk_ref, q2_ref, q1_ref, m2_ref, m1_ref,
     own_ref, gq_ref, out_ref, done, packed, sems,
 ):
     packed[:, :, :, :HEAD_DIM] = gq_ref[...]
-    bounds = user_bounds(lengths_ref)
-    quarter = ids_ref[1]
+    quarter = lax.axis_index("x")
     own_pos = quarter * PART + iota((PART, 1), 0)
     values, keys = vk_ref[:, :HEAD_DIM], vk_ref[:, HEAD_DIM:]
     sums = (own_ref[0], own_ref[1])
-    for (part, mixed), rows, at in steps_of(
-        ((q1_ref, m1_ref), (q2_ref, m2_ref)), (quarter + 1, quarter + 2)
-    ):
+    later = steps_of(((q1_ref, m1_ref), (q2_ref, m2_ref)), (quarter + 1, quarter + 2))
+    for n, ((part, mixed), rows, at) in enumerate(later):
+        along = PART + n * STEP
         terms = key_grads(
-            keys, values, own_pos, part[rows], mixed[rows], at + iota((1, STEP), 1), bounds
+            keys, values, own_pos, part[rows], mixed[rows], at + iota((1, STEP), 1),
+            low_rows_ref[0:1, along : along + STEP],
         )
         sums = tuple(a + b for a, b in zip(sums, terms))
     done[0] = sums[0].astype(BF16)
@@ -337,13 +354,13 @@
 
 
 def finish_kernel(
-    ids_ref, home_ref, l0, l1, l2, l3, back_ref, grad_ref, out_ref, grads, layer, sems
+    home_ref, l0, l1, l2, l3, back_ref, grad_ref, out_ref, grads, sems
 ):
-    head = ids_ref[2]
+    stores = []
     for k, layer_ref in enumerate((l0, l1, l2, l3)):
-        layer[:, head_columns(head ^ k)] = layer_ref[...]
-    stores = [pltpu.make_async_copy(layer, out_ref, sems.at[HEADS])]
-    stores[0].start()
+        columns = head_columns(lax.axis_index("h") ^ k)
+        stores.append(pltpu.make_async_copy(layer_ref, out_ref.at[:, columns], sems.at[k]))
+        stores[-1].start()
     pick = home_ref[...]
     for h in range(HEADS):
         chunks = back_ref[:, h].reshape(N_DP * CHUNK, 2 * HEAD_DIM)
@@ -358,7 +375,7 @@
                 ]
                 stores.append(
                     pltpu.make_async_copy(
-                        grads.at[:, columns], grad_ref.at[:, columns], sems.at[HEADS + 1 + 4 * h + block]
+                        grads.at[:, columns], grad_ref.at[:, columns], sems.at[HEADS + 4 * h + block]
                     )
                 )
                 stores[-1].start()
@@ -387,29 +404,33 @@
 
 
 def body(projected, destination, lengths, grad_out):
-    ids = jnp.stack([lax.axis_index(axis) for axis in ("dp", "x", "h")]).astype(jnp.int32)
     mapping = destination.reshape(N_DP, ROWS)
     chunked = shape(N_DP, HEADS, CHUNK, 2 * HEAD_DIM)
     half_chunked = shape(N_DP, HEADS, CHUNK, HEAD_DIM)
     head_part = shape(PART, HEAD_DIM)
     pieces = [shape(ROWS, HEAD_DIM)] * HEADS
+    dma = pltpu.SemaphoreType.DMA
     (packed,) = call(
-        pack_kernel, [chunked], (ids, mapping, projected), (1, 0, 0),
+        pack_kernel, [chunked], (mapping, projected),
         scratch=[
-            pltpu.VMEM(projected.shape, BF16), pltpu.VMEM(chunked.shape, BF16),
-            pltpu.SemaphoreType.DMA, pltpu.SemaphoreType.DMA((2,)),
+            pltpu.VMEM(projected.shape, BF16), pltpu.VMEM(chunked.shape, BF16), dma, dma((2,)),
         ],
-        flops=2 * 256 * 128 * 2048, nbytes=3 << 19, hbm_in=(2,), hbm_out=True, limit=62 * 1024 * 1024,
-    )
-    *side_out, home = call(
-        side_kernel, [shape(ROWS + CHUNK, HEAD_DIM)] * HEADS + [shape(2 * ROWS, N_DP * CHUNK)], (ids, mapping, grad_out), (1, 0, 0),
-        nbytes=3 << 17,
+        flops=2 * 256 * 128 * 2048, nbytes=3 << 19,
+        hbm_in=(1,), hbm_out=True, limit=62 * 1024 * 1024,
+    )
+    *side_out, home, low, low_rows = call(
+        side_kernel,
+        [shape(ROWS + CHUNK, HEAD_DIM)] * HEADS
+        + [
+            shape(2 * ROWS, N_DP * CHUNK), shape(PART, ROWS, dtype=jnp.int32),
+            shape(8, (REACH + 1) * PART, dtype=jnp.int32),
+        ],
+        (lengths, mapping, grad_out), smem=(0,), nbytes=3 << 17,
     )
     side = swap_heads(side_out)
     arrived = route(packed)
     gate, queries, vk = call(
-        unpack_kernel, [head_part, head_part, shape(PART, 2 * HEAD_DIM)],
-        (ids, *side, arrived), (1,) + (0,) * 5,
+        unpack_kernel, [head_part, head_part, shape(PART, 2 * HEAD_DIM)], (*side, arrived),
         flops=1 << 28, nbytes=2 << 20,
     )
     vk_parts = (from_quarter(vk, -1), from_quarter(vk, -2), vk)
@@ -418,7 +439,7 @@
     done = pltpu.VMEM((2, PART, HEAD_DIM), BF16)
     mixed, gate_grad, *layer = call(
         forward_kernel, [head_part, head_part, *pieces],
-        (ids, lengths, *side, gate, queries, *vk_parts), (1, 1) + (0,) * 9,
+        (low, *side, gate, queries, *vk_parts),
         scratch=[held], flops=1 << 29, nbytes=2 << 20,
     )
     mixed_parts = (from_quarter(mixed, 2), from_quarter(mixed, 1))
@@ -426,24 +447,20 @@
     gq_back, own, picks = call(
         query_grad_kernel,
         [half_chunked, shape(2, PART, HEAD_DIM, dtype=F32), shape(HEADS, N_DP * CHUNK, 2 * ROWS)],
-        (ids, lengths, *side, mixed, gate_grad, queries, *vk_parts), (1, 1) + (0,) * 10,
+        (low, low_rows, *side, mixed, gate_grad, queries, *vk_parts),
         scratch=[done], flops=1 << 29, nbytes=2 << 20,
     )
     (back,) = call(
         backward_kernel, [chunked],
-        (ids, lengths, picks, vk, *query_parts, *mixed_parts, own, gq_back),
-        (1, 1) + (0,) * 8,
-        scratch=[done, pltpu.VMEM(chunked.shape, BF16), pltpu.SemaphoreType.DMA((HEADS,))],
+        (low_rows, picks, vk, *query_parts, *mixed_parts, own, gq_back),
+        scratch=[done, pltpu.VMEM(chunked.shape, BF16), dma((HEADS,))],
         flops=1 << 30, nbytes=3 << 20, hbm_out=True,
     )
     returned = route(back)
     grad_projected, layer_output = call(
         finish_kernel, [shape(ROWS, 4 * HEADS * HEAD_DIM), shape(ROWS, HEADS * HEAD_DIM)],
-        (ids, home, *layer_home, returned), (1, 0, 0, 0, 0, 0, 0),
-        scratch=[
-            pltpu.VMEM(projected.shape, BF16), pltpu.VMEM(grad_out.shape, BF16),
-            pltpu.SemaphoreType.DMA((5 * HEADS + 1,)),
-        ],
+        (home, *layer_home, returned),
+        scratch=[pltpu.VMEM(projected.shape, BF16), dma((5 * HEADS,))],
         flops=1 << 28, nbytes=2 << 20, hbm_out=True,
     )
     return (layer_output, grad_projected)

time: 186 us -> 183 us (0.984)
  the two profiles are of different devices: /device:TPU:39 before, /device:TPU:37 now
where the time goes in v3:
time: 183 us; the launch traced here: 182 us
  waiting for transfers between devices  88.3 us (48%)
  starting transfers between devices  78.1 us (43%)
  Pallas kernels  14.5 us (8%)
    ppermute x6, waiting for transfers between devices, swap_heads(): lax.ppermute(piece, 'h', [(i, i ^ k) for i in range(HEADS)])  84.6 us
    ppermute x6, starting transfers between devices, swap_heads(): lax.ppermute(piece, 'h', [(i, i ^ k) for i in range(HEADS)])  33.2 us
    all_to_all x2, starting transfers between devices, route(): moved = lax.all_to_all(flat, ('dp', 'h'), 0, 0, tiled=True)  30.1 us
    ppermute x6, starting transfers between devices, from_quarter(): return lax.ppermute(array, 'x', pairs)  14.8 us
    pallas_call x7, Pallas kernels, call(): pl.pallas_call(kernel, out_shape=outs, in_specs=[pl.BlockSpec(memory_spac...  14.5 us
    ppermute x6, waiting for transfers between devices, from_quarter(): return lax.ppermute(array, 'x', pairs)  3.68 us
  transfers between devices with their start and end apart: 14, of which 6 were waited for; matrix products, arithmetic and copies ran while one was open for 0% of the time, Pallas kernels for 3%

profile of v3, /device:TPU:37, one launch (start us, length us, event | category | flops | bytes accessed | tf_op | source)
XLA Modules:
  0.0 181.8 jit_solution(2713142438013716947)
XLA Ops:
  0.6 3.1 %pack_kernel.1 = bf16[32,4,16,256]{3,2,1,0:T(8,128)(2,1)} custom-call(s32[32,128]{1,0:T(8,128)} %bitcast.7, bf16[128,2048]{1,0:T(8,128)(2,1)} %proj_ref.1), custom_call_target="tpu_custom_call" | custom-call | flops 134217728 | bytes 1572864 | tf_op jit(solution)/shard_map/pack_kernel/pallas_call | solution.py:50
  3.8 19.6 %all-to-all-start = ((bf16[128,16,256]{2,1,0:T(8,128)(2,1)}), bf16[128,16,256]{2,1,0:T(8,128)(2,1)S(1)}, u32[]{:S(2)}, u32[]{:S(2)}) async-start(bf16[128,16,256]{2,1,0:T(8,128)(2,1)} %bitcast.9), calls=%async_computation | async-start | bytes 2097152 | tf_op jit(solution)/shard_map/all_to_all | solution.py:388
  24.6 2.3 %collective-permute-start = (bf16[144,128]{1,0:T(8,128)(2,1)S(1)}, bf16[144,128]{1,0:T(8,128)(2,1)S(1)}, u32[]{:S(2)}, u32[]{:S(2)}) collective-permute-start(bf16[144,128]{1,0:T(8,128)(2,1)S(1)} %get-tuple-element.26), channel_id=1, source_target_pairs={{0,1},{1,0},{2,3},{3,2},{4,5},{5,4},{6,7},{7,6},{8,9},{9,8},{10,11... | collective-permute-start | bytes 110600 | tf_op jit(solution)/shard_map/ppermute | solution.py:399
  26.9 10.9 %collective-permute-start.1 = (bf16[144,128]{1,0:T(8,128)(2,1)S(1)}, bf16[144,128]{1,0:T(8,128)(2,1)S(1)}, u32[]{:S(2)}, u32[]{:S(2)}) collective-permute-start(bf16[144,128]{1,0:T(8,128)(2,1)S(1)} %get-tuple-element.27), channel_id=1, source_target_pairs={{0,2},{1,3},{2,0},{3,1},{4,6},{5,7},{6,4},{7,5},{8,10},{9,11},{10,... | collective-permute-start | bytes 110600 | tf_op jit(solution)/shard_map/ppermute | solution.py:399
  37.8 3.4 %collective-permute-start.2 = (bf16[144,128]{1,0:T(8,128)(2,1)S(1)}, bf16[144,128]{1,0:T(8,128)(2,1)S(1)}, u32[]{:S(2)}, u32[]{:S(2)}) collective-permute-start(bf16[144,128]{1,0:T(8,128)(2,1)S(1)} %get-tuple-element.28), channel_id=1, source_target_pairs={{0,3},{1,2},{2,1},{3,0},{4,7},{5,6},{6,5},{7,4},{8,11},{9,10},{10,... | collective-permute-start | bytes 110600 | tf_op jit(solution)/shard_map/ppermute | solution.py:399
  41.2 40.0 %collective-permute-done.1.s2 = bf16[144,128]{1,0:T(8,128)(2,1)S(1)} collective-permute-done((bf16[144,128]{1,0:T(8,128)(2,1)S(1)}, bf16[144,128]{1,0:T(8,128)(2,1)S(1)}, u32[]{:S(2)}, u32[]{:S(2)}) %collective-permute-start.1) | collective-permute-done | bytes 36896 | tf_op jit(solution)/shard_map/ppermute | solution.py:399
  81.2 2.0 %collective-permute-done.2.s3 = bf16[144,128]{1,0:T(8,128)(2,1)S(1)} collective-permute-done((bf16[144,128]{1,0:T(8,128)(2,1)S(1)}, bf16[144,128]{1,0:T(8,128)(2,1)S(1)}, u32[]{:S(2)}, u32[]{:S(2)}) %collective-permute-start.2) | collective-permute-done | bytes 36896 | tf_op jit(solution)/shard_map/ppermute | solution.py:399
  83.9 2.8 %collective-permute-start.3 = (bf16[512,256]{1,0:T(8,128)(2,1)S(1)}, bf16[512,256]{1,0:T(8,128)(2,1)S(1)}, u32[]{:S(2)}, u32[]{:S(2)}) collective-permute-start(bf16[512,256]{1,0:T(8,128)(2,1)S(1)} %get-tuple-element.31.vk0_ref.vk_ref), channel_id=1, source_target_pairs={{0,4},{4,8},{8,12},{1,5},{5,9},{9,13},{2,6},{6,10},{10,14},{3,7},{... | collective-permute-start | bytes 786440 | tf_op jit(solution)/shard_map/ppermute | solution.py:394
  86.7 1.3 collective-permute-start.4
  88.0 5.5 %collective-permute-start.8 = (bf16[512,128]{1,0:T(8,128)(2,1)S(1)}, bf16[512,128]{1,0:T(8,128)(2,1)S(1)}, u32[]{:S(2)}, u32[]{:S(2)}) collective-permute-start(bf16[512,128]{1,0:T(8,128)(2,1)S(1)} %get-tuple-element.30.query_ref), channel_id=1, source_target_pairs={{8,0},{12,4},{9,1},{13,5},{10,2},{14,6},{11,3},{15,7},{24,16},{28,... | collective-permute-start | bytes 393224 | tf_op jit(solution)/shard_map/ppermute | solution.py:394
  93.5 1.9 %collective-permute-start.9 = (bf16[512,128]{1,0:T(8,128)(2,1)S(1)}, bf16[512,128]{1,0:T(8,128)(2,1)S(1)}, u32[]{:S(2)}, u32[]{:S(2)}) collective-permute-start(bf16[512,128]{1,0:T(8,128)(2,1)S(1)} %get-tuple-element.30.query_ref), channel_id=1, source_target_pairs={{4,0},{8,4},{12,8},{5,1},{9,5},{13,9},{6,2},{10,6},{14,10},{7,3},{... | collective-permute-start | bytes 393224 | tf_op jit(solution)/shard_map/ppermute | solution.py:394
  95.5 3.4 %collective-permute-done.4.vk2_ref = bf16[512,256]{1,0:T(8,128)(2,1)S(1)} collective-permute-done((bf16[512,256]{1,0:T(8,128)(2,1)S(1)}, bf16[512,256]{1,0:T(8,128)(2,1)S(1)}, u32[]{:S(2)}, u32[]{:S(2)}) %collective-permute-start.4) | collective-permute-done | bytes 262176 | tf_op jit(solution)/shard_map/ppermute | solution.py:394
  98.9 1.7 forward_kernel.1
  100.5 1.3 collective-permute-start.10
  101.8 1.9 %collective-permute-start.11 = (bf16[512,128]{1,0:T(8,128)(2,1)S(1)}, bf16[512,128]{1,0:T(8,128)(2,1)S(1)}, u32[]{:S(2)}, u32[]{:S(2)}) collective-permute-start(bf16[512,128]{1,0:T(8,128)(2,1)S(1)} %get-tuple-element.37.mixed_ref), channel_id=1, source_target_pairs={{4,0},{8,4},{12,8},{5,1},{9,5},{13,9},{6,2},{10,6},{14,10},{7,3},{... | collective-permute-start | bytes 393224 | tf_op jit(solution)/shard_map/ppermute | solution.py:394
  103.8 3.5 %query_grad_kernel.1 = (bf16[32,4,16,128]{3,2,1,0:T(8,128)(2,1)S(1)}, f32[2,512,128]{2,1,0:T(8,128)S(1)}, bf16[4,512,256]{2,1,0:T(8,128)(2,1)S(1)}) custom-call(s32[512,128]{1,0:T(8,128)S(1)} %get-tuple-element.24.low_ref, s32[8,1536]{1,0:T(8,128)S(1)} %get-tuple-element.36.low_rows_ref, bf16[144,128]{1,0:T(8,128)(2,1)S(1)} %get-tuple-element.25.s0, ...), custom_call_target="tpu_custom_call" | custom-call | flops 536870912 | bytes 2097152 | tf_op jit(solution)/shard_map/query_grad_kernel/pallas_call | solution.py:50
  107.5 3.2 %backward_kernel.1 = bf16[32,4,16,256]{3,2,1,0:T(8,128)(2,1)} custom-call(s32[8,1536]{1,0:T(8,128)S(1)} %get-tuple-element.36.low_rows_ref, bf16[4,512,256]{2,1,0:T(8,128)(2,1)S(1)} %get-tuple-element.39.picks_ref, bf16[512,256]{1,0:T(8,128)(2,1)S(1)} %get-tuple-element.31.vk0_ref.vk_ref, bf16[512,128]{1,0:T(8,128)(2,1)S(1)} %collective-permute-done.8.q2_ref, ...), custom_call_target="tpu_custom_call" | custom-call | flops 1073741824 | bytes 3145728 | tf_op jit(solution)/shard_map/backward_kernel/pallas_call | solution.py:50
  110.7 10.5 %all-to-all-start.1 = ((bf16[128,16,256]{2,1,0:T(8,128)(2,1)}), bf16[128,16,256]{2,1,0:T(8,128)(2,1)S(1)}, u32[]{:S(2)}, u32[]{:S(2)}) async-start(bf16[128,16,256]{2,1,0:T(8,128)(2,1)} %bitcast.3), calls=%async_computation.1 | async-start | bytes 2097152 | tf_op jit(solution)/shard_map/all_to_all | solution.py:388
  121.3 2.3 %collective-permute-start.5 = (bf16[128,128]{1,0:T(8,128)(2,1)S(1)}, bf16[128,128]{1,0:T(8,128)(2,1)S(1)}, u32[]{:S(2)}, u32[]{:S(2)}) collective-permute-start(bf16[128,128]{1,0:T(8,128)(2,1)S(1)} %get-tuple-element.33), channel_id=1, source_target_pairs={{0,1},{1,0},{2,3},{3,2},{4,5},{5,4},{6,7},{7,6},{8,9},{9,8},{10,11... | collective-permute-start | bytes 98312 | tf_op jit(solution)/shard_map/ppermute | solution.py:399
  123.5 10.9 %collective-permute-start.6 = (bf16[128,128]{1,0:T(8,128)(2,1)S(1)}, bf16[128,128]{1,0:T(8,128)(2,1)S(1)}, u32[]{:S(2)}, u32[]{:S(2)}) collective-permute-start(bf16[128,128]{1,0:T(8,128)(2,1)S(1)} %get-tuple-element.34), channel_id=1, source_target_pairs={{0,2},{1,3},{2,0},{3,1},{4,6},{5,7},{6,4},{7,5},{8,10},{9,11},{10,... | collective-permute-start | bytes 98312 | tf_op jit(solution)/shard_map/ppermute | solution.py:399
  134.5 3.4 %collective-permute-start.7 = (bf16[128,128]{1,0:T(8,128)(2,1)S(1)}, bf16[128,128]{1,0:T(8,128)(2,1)S(1)}, u32[]{:S(2)}, u32[]{:S(2)}) collective-permute-start(bf16[128,128]{1,0:T(8,128)(2,1)S(1)} %get-tuple-element.35), channel_id=1, source_target_pairs={{0,3},{1,2},{2,1},{3,0},{4,7},{5,6},{6,5},{7,4},{8,11},{9,10},{10,... | collective-permute-start | bytes 98312 | tf_op jit(solution)/shard_map/ppermute | solution.py:399
  137.9 41.0 %collective-permute-done.6.l2 = bf16[128,128]{1,0:T(8,128)(2,1)S(1)} collective-permute-done((bf16[128,128]{1,0:T(8,128)(2,1)S(1)}, bf16[128,128]{1,0:T(8,128)(2,1)S(1)}, u32[]{:S(2)}, u32[]{:S(2)}) %collective-permute-start.6) | collective-permute-done | bytes 32800 | tf_op jit(solution)/shard_map/ppermute | solution.py:399
  178.9 1.6 collective-permute-done.7.l3
  180.5 1.3 finish_kernel.1
  (17 shorter events, 2.1 us)
Async XLA Ops:
  3.7 19.7 %copy-start = (bf16[128,512]{1,0:T(8,128)(2,1)S(1)}, bf16[128,512]{1,0:T(8,128)(2,1)}, u32[]{:S(2)}) copy-start(bf16[128,512]{1,0:T(8,128)(2,1)} %grad_ref.1) | copy-start | bytes 393220
  3.7 19.7 %copy-start.1 = (s32[1,4096]{1,0:T(1,128)S(1)}, s32[1,4096]{1,0:T(1,128)}, u32[]{:S(2)}) copy-start(s32[1,4096]{1,0:T(1,128)} %param.5) | copy-start | bytes 49156
  3.7 19.7 %copy-start.2 = (s32[1,3]{1,0:T(1,128)S(1)}, s32[1,3]{1,0:T(1,128)}, u32[]{:S(2)}) copy-start(s32[1,3]{1,0:T(1,128)} %lengths_ref.1) | copy-start | bytes 40
  3.8 79.5 %all-to-all-start = ((bf16[128,16,256]{2,1,0:T(8,128)(2,1)}), bf16[128,16,256]{2,1,0:T(8,128)(2,1)S(1)}, u32[]{:S(2)}, u32[]{:S(2)}) async-start(bf16[128,16,256]{2,1,0:T(8,128)(2,1)} %bitcast.9), calls=%async_computation | async-start | bytes 2097152 | tf_op jit(solution)/shard_map/all_to_all | solution.py:388
  24.6 16.6 %collective-permute-start = (bf16[144,128]{1,0:T(8,128)(2,1)S(1)}, bf16[144,128]{1,0:T(8,128)(2,1)S(1)}, u32[]{:S(2)}, u32[]{:S(2)}) collective-permute-start(bf16[144,128]{1,0:T(8,128)(2,1)S(1)} %get-tuple-element.26), channel_id=1, source_target_pairs={{0,1},{1,0},{2,3},{3,2},{4,5},{5,4},{6,7},{7,6},{8,9},{9,8},{10,11... | collective-permute-start | bytes 110600 | tf_op jit(solution)/shard_map/ppermute | solution.py:399
  26.9 54.3 %collective-permute-start.1 = (bf16[144,128]{1,0:T(8,128)(2,1)S(1)}, bf16[144,128]{1,0:T(8,128)(2,1)S(1)}, u32[]{:S(2)}, u32[]{:S(2)}) collective-permute-start(bf16[144,128]{1,0:T(8,128)(2,1)S(1)} %get-tuple-element.27), channel_id=1, source_target_pairs={{0,2},{1,3},{2,0},{3,1},{4,6},{5,7},{6,4},{7,5},{8,10},{9,11},{10,... | collective-permute-start | bytes 110600 | tf_op jit(solution)/shard_map/ppermute | solution.py:399
  37.8 45.5 %collective-permute-start.2 = (bf16[144,128]{1,0:T(8,128)(2,1)S(1)}, bf16[144,128]{1,0:T(8,128)(2,1)S(1)}, u32[]{:S(2)}, u32[]{:S(2)}) collective-permute-start(bf16[144,128]{1,0:T(8,128)(2,1)S(1)} %get-tuple-element.28), channel_id=1, source_target_pairs={{0,3},{1,2},{2,1},{3,0},{4,7},{5,6},{6,5},{7,4},{8,11},{9,10},{10,... | collective-permute-start | bytes 110600 | tf_op jit(solution)/shard_map/ppermute | solution.py:399
  83.9 11.6 %collective-permute-start.3 = (bf16[512,256]{1,0:T(8,128)(2,1)S(1)}, bf16[512,256]{1,0:T(8,128)(2,1)S(1)}, u32[]{:S(2)}, u32[]{:S(2)}) collective-permute-start(bf16[512,256]{1,0:T(8,128)(2,1)S(1)} %get-tuple-element.31.vk0_ref.vk_ref), channel_id=1, source_target_pairs={{0,4},{4,8},{8,12},{1,5},{5,9},{9,13},{2,6},{6,10},{10,14},{3,7},{... | collective-permute-start | bytes 786440 | tf_op jit(solution)/shard_map/ppermute | solution.py:394
  86.7 12.1 %collective-permute-start.4 = (bf16[512,256]{1,0:T(8,128)(2,1)S(1)}, bf16[512,256]{1,0:T(8,128)(2,1)S(1)}, u32[]{:S(2)}, u32[]{:S(2)}) collective-permute-start(bf16[512,256]{1,0:T(8,128)(2,1)S(1)} %get-tuple-element.31.vk0_ref.vk_ref), channel_id=1, source_target_pairs={{0,8},{4,12},{1,9},{5,13},{2,10},{6,14},{3,11},{7,15},{16,24},{20,... | collective-permute-start | bytes 786440 | tf_op jit(solution)/shard_map/ppermute | solution.py:394
  88.0 19.2 %collective-permute-start.8 = (bf16[512,128]{1,0:T(8,128)(2,1)S(1)}, bf16[512,128]{1,0:T(8,128)(2,1)S(1)}, u32[]{:S(2)}, u32[]{:S(2)}) collective-permute-start(bf16[512,128]{1,0:T(8,128)(2,1)S(1)} %get-tuple-element.30.query_ref), channel_id=1, source_target_pairs={{8,0},{12,4},{9,1},{13,5},{10,2},{14,6},{11,3},{15,7},{24,16},{28,... | collective-permute-start | bytes 393224 | tf_op jit(solution)/shard_map/ppermute | solution.py:394
  93.5 13.7 %collective-permute-start.9 = (bf16[512,128]{1,0:T(8,128)(2,1)S(1)}, bf16[512,128]{1,0:T(8,128)(2,1)S(1)}, u32[]{:S(2)}, u32[]{:S(2)}) collective-permute-start(bf16[512,128]{1,0:T(8,128)(2,1)S(1)} %get-tuple-element.30.query_ref), channel_id=1, source_target_pairs={{4,0},{8,4},{12,8},{5,1},{9,5},{13,9},{6,2},{10,6},{14,10},{7,3},{... | collective-permute-start | bytes 393224 | tf_op jit(solution)/shard_map/ppermute | solution.py:394
  100.5 6.7 %collective-permute-start.10 = (bf16[512,128]{1,0:T(8,128)(2,1)S(1)}, bf16[512,128]{1,0:T(8,128)(2,1)S(1)}, u32[]{:S(2)}, u32[]{:S(2)}) collective-permute-start(bf16[512,128]{1,0:T(8,128)(2,1)S(1)} %get-tuple-element.37.mixed_ref), channel_id=1, source_target_pairs={{8,0},{12,4},{9,1},{13,5},{10,2},{14,6},{11,3},{15,7},{24,16},{28,... | collective-permute-start | bytes 393224 | tf_op jit(solution)/shard_map/ppermute | solution.py:394
  101.8 5.7 %collective-permute-start.11 = (bf16[512,128]{1,0:T(8,128)(2,1)S(1)}, bf16[512,128]{1,0:T(8,128)(2,1)S(1)}, u32[]{:S(2)}, u32[]{:S(2)}) collective-permute-start(bf16[512,128]{1,0:T(8,128)(2,1)S(1)} %get-tuple-element.37.mixed_ref), channel_id=1, source_target_pairs={{4,0},{8,4},{12,8},{5,1},{9,5},{13,9},{6,2},{10,6},{14,10},{7,3},{... | collective-permute-start | bytes 393224 | tf_op jit(solution)/shard_map/ppermute | solution.py:394
  110.7 69.8 %all-to-all-start.1 = ((bf16[128,16,256]{2,1,0:T(8,128)(2,1)}), bf16[128,16,256]{2,1,0:T(8,128)(2,1)S(1)}, u32[]{:S(2)}, u32[]{:S(2)}) async-start(bf16[128,16,256]{2,1,0:T(8,128)(2,1)} %bitcast.3), calls=%async_computation.1 | async-start | bytes 2097152 | tf_op jit(solution)/shard_map/all_to_all | solution.py:388
  121.3 16.6 %collective-permute-start.5 = (bf16[128,128]{1,0:T(8,128)(2,1)S(1)}, bf16[128,128]{1,0:T(8,128)(2,1)S(1)}, u32[]{:S(2)}, u32[]{:S(2)}) collective-permute-start(bf16[128,128]{1,0:T(8,128)(2,1)S(1)} %get-tuple-element.33), channel_id=1, source_target_pairs={{0,1},{1,0},{2,3},{3,2},{4,5},{5,4},{6,7},{7,6},{8,9},{9,8},{10,11... | collective-permute-start | bytes 98312 | tf_op jit(solution)/shard_map/ppermute | solution.py:399
  123.5 55.4 %collective-permute-start.6 = (bf16[128,128]{1,0:T(8,128)(2,1)S(1)}, bf16[128,128]{1,0:T(8,128)(2,1)S(1)}, u32[]{:S(2)}, u32[]{:S(2)}) collective-permute-start(bf16[128,128]{1,0:T(8,128)(2,1)S(1)} %get-tuple-element.34), channel_id=1, source_target_pairs={{0,2},{1,3},{2,0},{3,1},{4,6},{5,7},{6,4},{7,5},{8,10},{9,11},{10,... | collective-permute-start | bytes 98312 | tf_op jit(solution)/shard_map/ppermute | solution.py:399
  134.5 46.1 %collective-permute-start.7 = (bf16[128,128]{1,0:T(8,128)(2,1)S(1)}, bf16[128,128]{1,0:T(8,128)(2,1)S(1)}, u32[]{:S(2)}, u32[]{:S(2)}) collective-permute-start(bf16[128,128]{1,0:T(8,128)(2,1)S(1)} %get-tuple-element.35), channel_id=1, source_target_pairs={{0,3},{1,2},{2,1},{3,0},{4,7},{5,6},{6,5},{7,4},{8,11},{9,10},{10,... | collective-permute-start | bytes 98312 | tf_op jit(solution)/shard_map/ppermute | solution.py:399

commit v4 on v3

--- a/solution.py
+++ b/solution.py
@@ -181,7 +181,7 @@
 
 
 def unpack_kernel(
-    s0, s1, s2, s3, arrived_ref, gate_ref, query_ref, vk_ref,
+    s0, s2, s3, s1, arrived_ref, gate_ref, query_ref, vk_ref,
 ):
     for c in range(HEADS):
         rows = slice(c * ROWS, (c + 1) * ROWS)
@@ -222,7 +222,7 @@
 
 
 def forward_kernel(
-    low_ref, s0, s1, s2, s3, gate_ref, query_ref, vk1_ref, vk2_ref, vk0_ref,
+    low_ref, s0, s2, s3, s1, gate_ref, query_ref, vk1_ref, vk2_ref, vk0_ref,
     mixed_ref, gate_grad_ref, l0, l1, l2, l3, held,
 ):
     low = low_down(low_ref)
@@ -272,7 +272,7 @@
 
 
 def query_grad_kernel(
-    low_ref, low_rows_ref, s0, s1, s2, s3, mixed_ref, gate_grad_ref, query_ref,
+    low_ref, low_rows_ref, s0, s2, s3, s1, mixed_ref, gate_grad_ref, query_ref,
     vk1_ref, vk2_ref, vk0_ref, out_ref, own_ref, picks_ref, done,
 ):
     low = low_down(low_ref)
@@ -354,7 +354,7 @@
 
 
 def finish_kernel(
-    home_ref, l0, l1, l2, l3, back_ref, grad_ref, out_ref, grads, sems
+    home_ref, l0, l2, l3, l1, back_ref, grad_ref, out_ref, grads, sems
 ):
     stores = []
     for k, layer_ref in enumerate((l0, l1, l2, l3)):
@@ -395,12 +395,9 @@
 
 
 def swap_heads(pieces):
-    moved = [
-        lax.ppermute(piece, "h", [(i, i ^ k) for i in range(HEADS)])
-        for k, piece in enumerate(pieces)
-        if k
+    return [pieces[0]] + [
+        lax.ppermute(pieces[k], "h", [(i, i ^ k) for i in range(HEADS)]) for k in (2, 3, 1)
     ]
-    return [pieces[0], *moved]
 
 
 def body(projected, destination, lengths, grad_out):

time: 183 us -> 183 us (level)
  no operation moved by 1% of the time
where the time goes in v4:
time: 183 us; the launch traced here: 182 us
  waiting for transfers between devices  88.7 us (48%)
  starting transfers between devices  77.8 us (43%)
  Pallas kernels  14.5 us (8%)
    ppermute x6, waiting for transfers between devices, swap_heads(): lax.ppermute(pieces[k], 'h', [(i, i ^ k) for i in range(HEADS)])  85 us
    ppermute x6, starting transfers between devices, swap_heads(): lax.ppermute(pieces[k], 'h', [(i, i ^ k) for i in range(HEADS)])  32.9 us
    all_to_all x2, starting transfers between devices, route(): moved = lax.all_to_all(flat, ('dp', 'h'), 0, 0, tiled=True)  30.1 us
    ppermute x6, starting transfers between devices, from_quarter(): return lax.ppermute(array, 'x', pairs)  14.8 us
    pallas_call x7, Pallas kernels, call(): pl.pallas_call(kernel, out_shape=outs, in_specs=[pl.BlockSpec(memory_spac...  14.5 us
    ppermute x6, waiting for transfers between devices, from_quarter(): return lax.ppermute(array, 'x', pairs)  3.68 us
  transfers between devices with their start and end apart: 14, of which 6 were waited for; matrix products, arithmetic and copies ran while one was open for 0% of the time, Pallas kernels for 3%

profile of v4, /device:TPU:37, one launch (start us, length us, event | category | flops | bytes accessed | tf_op | source)
XLA Modules:
  0.0 181.8 jit_solution(3617628953042315767)
XLA Ops:
  0.6 3.1 %pack_kernel.1 = bf16[32,4,16,256]{3,2,1,0:T(8,128)(2,1)} custom-call(s32[32,128]{1,0:T(8,128)} %bitcast.7, bf16[128,2048]{1,0:T(8,128)(2,1)} %proj_ref.1), custom_call_target="tpu_custom_call" | custom-call | flops 134217728 | bytes 1572864 | tf_op jit(solution)/shard_map/pack_kernel/pallas_call | solution.py:50
  3.8 19.6 %all-to-all-start = ((bf16[128,16,256]{2,1,0:T(8,128)(2,1)}), bf16[128,16,256]{2,1,0:T(8,128)(2,1)S(1)}, u32[]{:S(2)}, u32[]{:S(2)}) async-start(bf16[128,16,256]{2,1,0:T(8,128)(2,1)} %bitcast.9), calls=%async_computation | async-start | bytes 2097152 | tf_op jit(solution)/shard_map/all_to_all | solution.py:388
  24.6 10.9 %collective-permute-start = (bf16[144,128]{1,0:T(8,128)(2,1)S(1)}, bf16[144,128]{1,0:T(8,128)(2,1)S(1)}, u32[]{:S(2)}, u32[]{:S(2)}) collective-permute-start(bf16[144,128]{1,0:T(8,128)(2,1)S(1)} %get-tuple-element.26), channel_id=1, source_target_pairs={{0,2},{1,3},{2,0},{3,1},{4,6},{5,7},{6,4},{7,5},{8,10},{9,11},{10,... | collective-permute-start | bytes 110600 | tf_op jit(solution)/shard_map/ppermute | solution.py:399
  35.5 3.6 %collective-permute-start.1 = (bf16[144,128]{1,0:T(8,128)(2,1)S(1)}, bf16[144,128]{1,0:T(8,128)(2,1)S(1)}, u32[]{:S(2)}, u32[]{:S(2)}) collective-permute-start(bf16[144,128]{1,0:T(8,128)(2,1)S(1)} %get-tuple-element.27), channel_id=1, source_target_pairs={{0,3},{1,2},{2,1},{3,0},{4,7},{5,6},{6,5},{7,4},{8,11},{9,10},{10,... | collective-permute-start | bytes 110600 | tf_op jit(solution)/shard_map/ppermute | solution.py:399
  39.1 1.9 %collective-permute-start.2 = (bf16[144,128]{1,0:T(8,128)(2,1)S(1)}, bf16[144,128]{1,0:T(8,128)(2,1)S(1)}, u32[]{:S(2)}, u32[]{:S(2)}) collective-permute-start(bf16[144,128]{1,0:T(8,128)(2,1)S(1)} %get-tuple-element.28), channel_id=1, source_target_pairs={{0,1},{1,0},{2,3},{3,2},{4,5},{5,4},{6,7},{7,6},{8,9},{9,8},{10,11... | collective-permute-start | bytes 110600 | tf_op jit(solution)/shard_map/ppermute | solution.py:399
  41.1 40.2 %collective-permute-done.s2 = bf16[144,128]{1,0:T(8,128)(2,1)S(1)} collective-permute-done((bf16[144,128]{1,0:T(8,128)(2,1)S(1)}, bf16[144,128]{1,0:T(8,128)(2,1)S(1)}, u32[]{:S(2)}, u32[]{:S(2)}) %collective-permute-start) | collective-permute-done | bytes 36896 | tf_op jit(solution)/shard_map/ppermute | solution.py:399
  81.2 2.0 %collective-permute-done.1.s3 = bf16[144,128]{1,0:T(8,128)(2,1)S(1)} collective-permute-done((bf16[144,128]{1,0:T(8,128)(2,1)S(1)}, bf16[144,128]{1,0:T(8,128)(2,1)S(1)}, u32[]{:S(2)}, u32[]{:S(2)}) %collective-permute-start.1) | collective-permute-done | bytes 36896 | tf_op jit(solution)/shard_map/ppermute | solution.py:399
  83.9 2.8 %collective-permute-start.3 = (bf16[512,256]{1,0:T(8,128)(2,1)S(1)}, bf16[512,256]{1,0:T(8,128)(2,1)S(1)}, u32[]{:S(2)}, u32[]{:S(2)}) collective-permute-start(bf16[512,256]{1,0:T(8,128)(2,1)S(1)} %get-tuple-element.31.vk0_ref.vk_ref), channel_id=1, source_target_pairs={{0,4},{4,8},{8,12},{1,5},{5,9},{9,13},{2,6},{6,10},{10,14},{3,7},{... | collective-permute-start | bytes 786440 | tf_op jit(solution)/shard_map/ppermute | solution.py:394
  86.7 1.3 collective-permute-start.4
  88.0 5.5 %collective-permute-start.8 = (bf16[512,128]{1,0:T(8,128)(2,1)S(1)}, bf16[512,128]{1,0:T(8,128)(2,1)S(1)}, u32[]{:S(2)}, u32[]{:S(2)}) collective-permute-start(bf16[512,128]{1,0:T(8,128)(2,1)S(1)} %get-tuple-element.30.query_ref), channel_id=1, source_target_pairs={{8,0},{12,4},{9,1},{13,5},{10,2},{14,6},{11,3},{15,7},{24,16},{28,... | collective-permute-start | bytes 393224 | tf_op jit(solution)/shard_map/ppermute | solution.py:394
  93.5 1.9 %collective-permute-start.9 = (bf16[512,128]{1,0:T(8,128)(2,1)S(1)}, bf16[512,128]{1,0:T(8,128)(2,1)S(1)}, u32[]{:S(2)}, u32[]{:S(2)}) collective-permute-start(bf16[512,128]{1,0:T(8,128)(2,1)S(1)} %get-tuple-element.30.query_ref), channel_id=1, source_target_pairs={{4,0},{8,4},{12,8},{5,1},{9,5},{13,9},{6,2},{10,6},{14,10},{7,3},{... | collective-permute-start | bytes 393224 | tf_op jit(solution)/shard_map/ppermute | solution.py:394
  95.5 3.4 %collective-permute-done.4.vk2_ref = bf16[512,256]{1,0:T(8,128)(2,1)S(1)} collective-permute-done((bf16[512,256]{1,0:T(8,128)(2,1)S(1)}, bf16[512,256]{1,0:T(8,128)(2,1)S(1)}, u32[]{:S(2)}, u32[]{:S(2)}) %collective-permute-start.4) | collective-permute-done | bytes 262176 | tf_op jit(solution)/shard_map/ppermute | solution.py:394
  98.9 1.7 forward_kernel.1
  100.5 1.3 collective-permute-start.10
  101.8 1.9 %collective-permute-start.11 = (bf16[512,128]{1,0:T(8,128)(2,1)S(1)}, bf16[512,128]{1,0:T(8,128)(2,1)S(1)}, u32[]{:S(2)}, u32[]{:S(2)}) collective-permute-start(bf16[512,128]{1,0:T(8,128)(2,1)S(1)} %get-tuple-element.37.mixed_ref), channel_id=1, source_target_pairs={{4,0},{8,4},{12,8},{5,1},{9,5},{13,9},{6,2},{10,6},{14,10},{7,3},{... | collective-permute-start | bytes 393224 | tf_op jit(solution)/shard_map/ppermute | solution.py:394
  103.8 3.5 %query_grad_kernel.1 = (bf16[32,4,16,128]{3,2,1,0:T(8,128)(2,1)S(1)}, f32[2,512,128]{2,1,0:T(8,128)S(1)}, bf16[4,512,256]{2,1,0:T(8,128)(2,1)S(1)}) custom-call(s32[512,128]{1,0:T(8,128)S(1)} %get-tuple-element.24.low_ref, s32[8,1536]{1,0:T(8,128)S(1)} %get-tuple-element.36.low_rows_ref, bf16[144,128]{1,0:T(8,128)(2,1)S(1)} %get-tuple-element.25.s0, ...), custom_call_target="tpu_custom_call" | custom-call | flops 536870912 | bytes 2097152 | tf_op jit(solution)/shard_map/query_grad_kernel/pallas_call | solution.py:50
  107.5 3.2 %backward_kernel.1 = bf16[32,4,16,256]{3,2,1,0:T(8,128)(2,1)} custom-call(s32[8,1536]{1,0:T(8,128)S(1)} %get-tuple-element.36.low_rows_ref, bf16[4,512,256]{2,1,0:T(8,128)(2,1)S(1)} %get-tuple-element.39.picks_ref, bf16[512,256]{1,0:T(8,128)(2,1)S(1)} %get-tuple-element.31.vk0_ref.vk_ref, bf16[512,128]{1,0:T(8,128)(2,1)S(1)} %collective-permute-done.8.q2_ref, ...), custom_call_target="tpu_custom_call" | custom-call | flops 1073741824 | bytes 3145728 | tf_op jit(solution)/shard_map/backward_kernel/pallas_call | solution.py:50
  110.8 10.5 %all-to-all-start.1 = ((bf16[128,16,256]{2,1,0:T(8,128)(2,1)}), bf16[128,16,256]{2,1,0:T(8,128)(2,1)S(1)}, u32[]{:S(2)}, u32[]{:S(2)}) async-start(bf16[128,16,256]{2,1,0:T(8,128)(2,1)} %bitcast.3), calls=%async_computation.1 | async-start | bytes 2097152 | tf_op jit(solution)/shard_map/all_to_all | solution.py:388
  121.3 10.9 %collective-permute-start.5 = (bf16[128,128]{1,0:T(8,128)(2,1)S(1)}, bf16[128,128]{1,0:T(8,128)(2,1)S(1)}, u32[]{:S(2)}, u32[]{:S(2)}) collective-permute-start(bf16[128,128]{1,0:T(8,128)(2,1)S(1)} %get-tuple-element.33), channel_id=1, source_target_pairs={{0,2},{1,3},{2,0},{3,1},{4,6},{5,7},{6,4},{7,5},{8,10},{9,11},{10,... | collective-permute-start | bytes 98312 | tf_op jit(solution)/shard_map/ppermute | solution.py:399
  132.2 3.6 %collective-permute-start.6 = (bf16[128,128]{1,0:T(8,128)(2,1)S(1)}, bf16[128,128]{1,0:T(8,128)(2,1)S(1)}, u32[]{:S(2)}, u32[]{:S(2)}) collective-permute-start(bf16[128,128]{1,0:T(8,128)(2,1)S(1)} %get-tuple-element.34), channel_id=1, source_target_pairs={{0,3},{1,2},{2,1},{3,0},{4,7},{5,6},{6,5},{7,4},{8,11},{9,10},{10,... | collective-permute-start | bytes 98312 | tf_op jit(solution)/shard_map/ppermute | solution.py:399
  135.8 1.9 %collective-permute-start.7 = (bf16[128,128]{1,0:T(8,128)(2,1)S(1)}, bf16[128,128]{1,0:T(8,128)(2,1)S(1)}, u32[]{:S(2)}, u32[]{:S(2)}) collective-permute-start(bf16[128,128]{1,0:T(8,128)(2,1)S(1)} %get-tuple-element.35), channel_id=1, source_target_pairs={{0,1},{1,0},{2,3},{3,2},{4,5},{5,4},{6,7},{7,6},{8,9},{9,8},{10,11... | collective-permute-start | bytes 98312 | tf_op jit(solution)/shard_map/ppermute | solution.py:399
  137.7 41.2 %collective-permute-done.5.l2 = bf16[128,128]{1,0:T(8,128)(2,1)S(1)} collective-permute-done((bf16[128,128]{1,0:T(8,128)(2,1)S(1)}, bf16[128,128]{1,0:T(8,128)(2,1)S(1)}, u32[]{:S(2)}, u32[]{:S(2)}) %collective-permute-start.5) | collective-permute-done | bytes 32800 | tf_op jit(solution)/shard_map/ppermute | solution.py:399
  178.9 1.6 collective-permute-done.6.l3
  180.5 1.3 finish_kernel.1
  (17 shorter events, 2.1 us)
Async XLA Ops:
  3.7 19.7 %copy-start = (bf16[128,512]{1,0:T(8,128)(2,1)S(1)}, bf16[128,512]{1,0:T(8,128)(2,1)}, u32[]{:S(2)}) copy-start(bf16[128,512]{1,0:T(8,128)(2,1)} %grad_ref.1) | copy-start | bytes 393220
  3.7 19.7 %copy-start.1 = (s32[1,4096]{1,0:T(1,128)S(1)}, s32[1,4096]{1,0:T(1,128)}, u32[]{:S(2)}) copy-start(s32[1,4096]{1,0:T(1,128)} %param.5) | copy-start | bytes 49156
  3.7 19.7 %copy-start.2 = (s32[1,3]{1,0:T(1,128)S(1)}, s32[1,3]{1,0:T(1,128)}, u32[]{:S(2)}) copy-start(s32[1,3]{1,0:T(1,128)} %lengths_ref.1) | copy-start | bytes 40
  3.8 79.5 %all-to-all-start = ((bf16[128,16,256]{2,1,0:T(8,128)(2,1)}), bf16[128,16,256]{2,1,0:T(8,128)(2,1)S(1)}, u32[]{:S(2)}, u32[]{:S(2)}) async-start(bf16[128,16,256]{2,1,0:T(8,128)(2,1)} %bitcast.9), calls=%async_computation | async-start | bytes 2097152 | tf_op jit(solution)/shard_map/all_to_all | solution.py:388
  24.6 56.6 %collective-permute-start = (bf16[144,128]{1,0:T(8,128)(2,1)S(1)}, bf16[144,128]{1,0:T(8,128)(2,1)S(1)}, u32[]{:S(2)}, u32[]{:S(2)}) collective-permute-start(bf16[144,128]{1,0:T(8,128)(2,1)S(1)} %get-tuple-element.26), channel_id=1, source_target_pairs={{0,2},{1,3},{2,0},{3,1},{4,6},{5,7},{6,4},{7,5},{8,10},{9,11},{10,... | collective-permute-start | bytes 110600 | tf_op jit(solution)/shard_map/ppermute | solution.py:399
  35.5 47.7 %collective-permute-start.1 = (bf16[144,128]{1,0:T(8,128)(2,1)S(1)}, bf16[144,128]{1,0:T(8,128)(2,1)S(1)}, u32[]{:S(2)}, u32[]{:S(2)}) collective-permute-start(bf16[144,128]{1,0:T(8,128)(2,1)S(1)} %get-tuple-element.27), channel_id=1, source_target_pairs={{0,3},{1,2},{2,1},{3,0},{4,7},{5,6},{6,5},{7,4},{8,11},{9,10},{10,... | collective-permute-start | bytes 110600 | tf_op jit(solution)/shard_map/ppermute | solution.py:399
  39.1 44.1 %collective-permute-start.2 = (bf16[144,128]{1,0:T(8,128)(2,1)S(1)}, bf16[144,128]{1,0:T(8,128)(2,1)S(1)}, u32[]{:S(2)}, u32[]{:S(2)}) collective-permute-start(bf16[144,128]{1,0:T(8,128)(2,1)S(1)} %get-tuple-element.28), channel_id=1, source_target_pairs={{0,1},{1,0},{2,3},{3,2},{4,5},{5,4},{6,7},{7,6},{8,9},{9,8},{10,11... | collective-permute-start | bytes 110600 | tf_op jit(solution)/shard_map/ppermute | solution.py:399
  83.9 11.6 %collective-permute-start.3 = (bf16[512,256]{1,0:T(8,128)(2,1)S(1)}, bf16[512,256]{1,0:T(8,128)(2,1)S(1)}, u32[]{:S(2)}, u32[]{:S(2)}) collective-permute-start(bf16[512,256]{1,0:T(8,128)(2,1)S(1)} %get-tuple-element.31.vk0_ref.vk_ref), channel_id=1, source_target_pairs={{0,4},{4,8},{8,12},{1,5},{5,9},{9,13},{2,6},{6,10},{10,14},{3,7},{... | collective-permute-start | bytes 786440 | tf_op jit(solution)/shard_map/ppermute | solution.py:394
  86.7 12.1 %collective-permute-start.4 = (bf16[512,256]{1,0:T(8,128)(2,1)S(1)}, bf16[512,256]{1,0:T(8,128)(2,1)S(1)}, u32[]{:S(2)}, u32[]{:S(2)}) collective-permute-start(bf16[512,256]{1,0:T(8,128)(2,1)S(1)} %get-tuple-element.31.vk0_ref.vk_ref), channel_id=1, source_target_pairs={{0,8},{4,12},{1,9},{5,13},{2,10},{6,14},{3,11},{7,15},{16,24},{20,... | collective-permute-start | bytes 786440 | tf_op jit(solution)/shard_map/ppermute | solution.py:394
  88.0 19.2 %collective-permute-start.8 = (bf16[512,128]{1,0:T(8,128)(2,1)S(1)}, bf16[512,128]{1,0:T(8,128)(2,1)S(1)}, u32[]{:S(2)}, u32[]{:S(2)}) collective-permute-start(bf16[512,128]{1,0:T(8,128)(2,1)S(1)} %get-tuple-element.30.query_ref), channel_id=1, source_target_pairs={{8,0},{12,4},{9,1},{13,5},{10,2},{14,6},{11,3},{15,7},{24,16},{28,... | collective-permute-start | bytes 393224 | tf_op jit(solution)/shard_map/ppermute | solution.py:394
  93.5 13.7 %collective-permute-start.9 = (bf16[512,128]{1,0:T(8,128)(2,1)S(1)}, bf16[512,128]{1,0:T(8,128)(2,1)S(1)}, u32[]{:S(2)}, u32[]{:S(2)}) collective-permute-start(bf16[512,128]{1,0:T(8,128)(2,1)S(1)} %get-tuple-element.30.query_ref), channel_id=1, source_target_pairs={{4,0},{8,4},{12,8},{5,1},{9,5},{13,9},{6,2},{10,6},{14,10},{7,3},{... | collective-permute-start | bytes 393224 | tf_op jit(solution)/shard_map/ppermute | solution.py:394
  100.5 6.7 %collective-permute-start.10 = (bf16[512,128]{1,0:T(8,128)(2,1)S(1)}, bf16[512,128]{1,0:T(8,128)(2,1)S(1)}, u32[]{:S(2)}, u32[]{:S(2)}) collective-permute-start(bf16[512,128]{1,0:T(8,128)(2,1)S(1)} %get-tuple-element.37.mixed_ref), channel_id=1, source_target_pairs={{8,0},{12,4},{9,1},{13,5},{10,2},{14,6},{11,3},{15,7},{24,16},{28,... | collective-permute-start | bytes 393224 | tf_op jit(solution)/shard_map/ppermute | solution.py:394
  101.8 5.7 %collective-permute-start.11 = (bf16[512,128]{1,0:T(8,128)(2,1)S(1)}, bf16[512,128]{1,0:T(8,128)(2,1)S(1)}, u32[]{:S(2)}, u32[]{:S(2)}) collective-permute-start(bf16[512,128]{1,0:T(8,128)(2,1)S(1)} %get-tuple-element.37.mixed_ref), channel_id=1, source_target_pairs={{4,0},{8,4},{12,8},{5,1},{9,5},{13,9},{6,2},{10,6},{14,10},{7,3},{... | collective-permute-start | bytes 393224 | tf_op jit(solution)/shard_map/ppermute | solution.py:394
  110.8 69.8 %all-to-all-start.1 = ((bf16[128,16,256]{2,1,0:T(8,128)(2,1)}), bf16[128,16,256]{2,1,0:T(8,128)(2,1)S(1)}, u32[]{:S(2)}, u32[]{:S(2)}) async-start(bf16[128,16,256]{2,1,0:T(8,128)(2,1)} %bitcast.3), calls=%async_computation.1 | async-start | bytes 2097152 | tf_op jit(solution)/shard_map/all_to_all | solution.py:388
  121.3 57.7 %collective-permute-start.5 = (bf16[128,128]{1,0:T(8,128)(2,1)S(1)}, bf16[128,128]{1,0:T(8,128)(2,1)S(1)}, u32[]{:S(2)}, u32[]{:S(2)}) collective-permute-start(bf16[128,128]{1,0:T(8,128)(2,1)S(1)} %get-tuple-element.33), channel_id=1, source_target_pairs={{0,2},{1,3},{2,0},{3,1},{4,6},{5,7},{6,4},{7,5},{8,10},{9,11},{10,... | collective-permute-start | bytes 98312 | tf_op jit(solution)/shard_map/ppermute | solution.py:399
  132.2 48.3 %collective-permute-start.6 = (bf16[128,128]{1,0:T(8,128)(2,1)S(1)}, bf16[128,128]{1,0:T(8,128)(2,1)S(1)}, u32[]{:S(2)}, u32[]{:S(2)}) collective-permute-start(bf16[128,128]{1,0:T(8,128)(2,1)S(1)} %get-tuple-element.34), channel_id=1, source_target_pairs={{0,3},{1,2},{2,1},{3,0},{4,7},{5,6},{6,5},{7,4},{8,11},{9,10},{10,... | collective-permute-start | bytes 98312 | tf_op jit(solution)/shard_map/ppermute | solution.py:399
  135.8 44.7 %collective-permute-start.7 = (bf16[128,128]{1,0:T(8,128)(2,1)S(1)}, bf16[128,128]{1,0:T(8,128)(2,1)S(1)}, u32[]{:S(2)}, u32[]{:S(2)}) collective-permute-start(bf16[128,128]{1,0:T(8,128)(2,1)S(1)} %get-tuple-element.35), channel_id=1, source_target_pairs={{0,1},{1,0},{2,3},{3,2},{4,5},{5,4},{6,7},{7,6},{8,9},{9,8},{10,11... | collective-permute-start | bytes 98312 | tf_op jit(solution)/shard_map/ppermute | solution.py:399

commit v5 on v4

--- a/solution.py
+++ b/solution.py
@@ -195,16 +195,9 @@
         vk_ref[rows, HEAD_DIM:] = moved[ROWS:, HEAD_DIM:]
 
 
-def half_scores(a, b):
-    return dot_nt(a, b) * (0.5 * SCALE)
-
-
-def silu_of(half, tanh):
-    return half + half * tanh
-
-
-def slope_of(half, tanh):
-    return (0.5 + 0.5 * tanh) * (1.0 + half * (1.0 - tanh))
+def gates(scores, allowed):
+    half = scores * (0.5 * SCALE)
+    return jnp.where(allowed, 0.5 + 0.5 * jnp.tanh(half), 0.0), half + half
 
 
 def low_down(low_ref):
@@ -233,9 +226,9 @@
     for vk_ref, rows, at in steps_of(
         (vk2_ref, vk1_ref, vk0_ref), (quarter - 2, quarter - 1, quarter)
     ):
-        half = half_scores(queries, vk_ref[rows, HEAD_DIM:])
         allowed = pairs_allowed(at + iota((1, STEP), 1), query_pos, low)
-        weights = jnp.where(allowed, silu_of(half, jnp.tanh(half)), 0.0).astype(BF16)
+        part, scores = gates(dot_nt(queries, vk_ref[rows, HEAD_DIM:]), allowed)
+        weights = (scores * part).astype(BF16)
         mixed_sum = mixed_sum + dot_nn(weights, vk_ref[rows, :HEAD_DIM])
     center = mixed_sum - jnp.mean(mixed_sum, axis=-1, keepdims=True)
     inverse = lax.rsqrt(jnp.mean(center * center, axis=-1, keepdims=True) + EPSILON)
@@ -261,19 +254,20 @@
         layer_ref[...] = held[block_rows(head ^ k), :HEAD_DIM]
 
 
-def key_grads(keys, values, key_pos, queries, grad_mixed, query_pos, low):
-    half = half_scores(keys, queries)
-    allowed = pairs_allowed(key_pos, query_pos, low)
-    tanh = jnp.tanh(half)
-    weights = jnp.where(allowed, silu_of(half, tanh), 0.0).astype(BF16)
-    slope = jnp.where(allowed, slope_of(half, tanh), 0.0)
+def key_gates(keys, key_pos, queries, query_pos, low):
+    part, scores = gates(dot_nt(keys, queries), pairs_allowed(key_pos, query_pos, low))
+    weights = scores * part
+    return weights.astype(BF16), part * (1.0 + scores - weights)
+
+
+def key_grads(weights, slope, values, queries, grad_mixed):
     grad_scores = (dot_nt(values, grad_mixed) * slope).astype(BF16)
     return dot_nn(weights, grad_mixed), dot_nn(grad_scores, queries)
 
 
 def query_grad_kernel(
-    low_ref, low_rows_ref, s0, s2, s3, s1, mixed_ref, gate_grad_ref, query_ref,
-    vk1_ref, vk2_ref, vk0_ref, out_ref, own_ref, picks_ref, done,
+    low_ref, low_rows_ref, s0, s2, s3, s1, mixed_ref, gate_grad_ref, query_ref, q1_ref,
+    vk1_ref, vk2_ref, vk0_ref, out_ref, own_ref, picks_ref, weights_ref, slope_ref, done,
 ):
     low = low_down(low_ref)
     quarter = lax.axis_index("x")
@@ -285,9 +279,9 @@
         (vk2_ref, vk1_ref, vk0_ref), (quarter - 2, quarter - 1, quarter)
     ):
         keys = vk_ref[rows, HEAD_DIM:]
-        half = half_scores(queries, keys)
         allowed = pairs_allowed(at + iota((1, STEP), 1), own_pos, low)
-        slope = jnp.where(allowed, slope_of(half, jnp.tanh(half)), 0.0)
+        part, scores = gates(dot_nt(queries, keys), allowed)
+        slope = part * (1.0 + scores - scores * part)
         grad_scores = (dot_nt(grad_mixed, vk_ref[rows, :HEAD_DIM]) * slope).astype(BF16)
         total = total + dot_nn(grad_scores, keys)
     done[0] = gate_grad_ref[...]
@@ -297,13 +291,19 @@
     values, keys = vk0_ref[:, :HEAD_DIM], vk0_ref[:, HEAD_DIM:]
     sums = (0.0, 0.0)
     for part, rows, at in steps_of((query_ref,), (quarter,)):
-        terms = key_grads(
-            keys, values, own_pos, part[rows], mixed_ref[rows], at + iota((1, STEP), 1),
-            low_rows_ref[0:1, rows],
+        weights, slope = key_gates(
+            keys, own_pos, part[rows], at + iota((1, STEP), 1), low_rows_ref[0:1, rows]
         )
+        terms = key_grads(weights, slope, values, part[rows], mixed_ref[rows])
         sums = tuple(a + b for a, b in zip(sums, terms))
     for n in range(2):
         own_ref[n] = sums[n]
+    for n, (part, rows, at) in enumerate(steps_of((q1_ref,), (quarter + 1,))):
+        along = PART + n * STEP
+        weights_ref[n], slope_ref[n] = key_gates(
+            keys, own_pos, part[rows], at + iota((1, STEP), 1),
+            low_rows_ref[0:1, along : along + STEP],
+        )
 
 
 def back_picks(sides, picks_ref):
@@ -325,7 +325,7 @@
 
 def backward_kernel(
     low_rows_ref, picks_ref, vk_ref, q2_ref, q1_ref, m2_ref, m1_ref,
-    own_ref, gq_ref, out_ref, done, packed, sems,
+    own_ref, weights_ref, slope_ref, gq_ref, out_ref, done, packed, sems,
 ):
     packed[:, :, :, :HEAD_DIM] = gq_ref[...]
     quarter = lax.axis_index("x")
@@ -335,10 +335,14 @@
     later = steps_of(((q1_ref, m1_ref), (q2_ref, m2_ref)), (quarter + 1, quarter + 2))
     for n, ((part, mixed), rows, at) in enumerate(later):
         along = PART + n * STEP
-        terms = key_grads(
-            keys, values, own_pos, part[rows], mixed[rows], at + iota((1, STEP), 1),
-            low_rows_ref[0:1, along : along + STEP],
-        )
+        if n < PART // STEP:
+            weights, slope = weights_ref[n], slope_ref[n]
+        else:
+            weights, slope = key_gates(
+                keys, own_pos, part[rows], at + iota((1, STEP), 1),
+                low_rows_ref[0:1, along : along + STEP],
+            )
+        terms = key_grads(weights, slope, values, part[rows], mixed[rows])
         sums = tuple(a + b for a, b in zip(sums, terms))
     done[0] = sums[0].astype(BF16)
     done[1] = (sums[1] * SCALE).astype(BF16)
@@ -441,15 +445,16 @@
     )
     mixed_parts = (from_quarter(mixed, 2), from_quarter(mixed, 1))
     layer_home = swap_heads(layer)
-    gq_back, own, picks = call(
+    gq_back, own, picks, weights, slopes = call(
         query_grad_kernel,
-        [half_chunked, shape(2, PART, HEAD_DIM, dtype=F32), shape(HEADS, N_DP * CHUNK, 2 * ROWS)],
-        (low, low_rows, *side, mixed, gate_grad, queries, *vk_parts),
+        [half_chunked, shape(2, PART, HEAD_DIM, dtype=F32), shape(HEADS, N_DP * CHUNK, 2 * ROWS),
+         shape(PART // STEP, PART, STEP), shape(PART // STEP, PART, STEP, dtype=F32)],
+        (low, low_rows, *side, mixed, gate_grad, queries, query_parts[1], *vk_parts),
         scratch=[done], flops=1 << 29, nbytes=2 << 20,
     )
     (back,) = call(
         backward_kernel, [chunked],
-        (low_rows, picks, vk, *query_parts, *mixed_parts, own, gq_back),
+        (low_rows, picks, vk, *query_parts, *mixed_parts, own, weights, slopes, gq_back),
         scratch=[done, pltpu.VMEM(chunked.shape, BF16), dma((HEADS,))],
         flops=1 << 30, nbytes=3 << 20, hbm_out=True,
     )

time: 183 us -> 182 us (level)
  transfers between devices with their start and end apart: 14 -> 14, of which waited for: 6 -> 5; matrix products, arithmetic and copies ran while one was open for 0% -> 0% of each run, Pallas kernels for 3% -> 4%
where the time goes in v5:
time: 182 us; the launch traced here: 181 us
  waiting for transfers between devices  89 us (49%)
  starting transfers between devices  77.1 us (42%)
  Pallas kernels  14.3 us (8%)
    ppermute x6, waiting for transfers between devices, swap_heads(): lax.ppermute(pieces[k], 'h', [(i, i ^ k) for i in range(HEADS)])  85 us
    ppermute x6, starting transfers between devices, swap_heads(): lax.ppermute(pieces[k], 'h', [(i, i ^ k) for i in range(HEADS)])  32.9 us
    all_to_all x2, starting transfers between devices, route(): moved = lax.all_to_all(flat, ('dp', 'h'), 0, 0, tiled=True)  30.1 us
    pallas_call x7, Pallas kernels, call(): pl.pallas_call(kernel, out_shape=outs, in_specs=[pl.BlockSpec(memory_spac...  14.3 us
    ppermute x6, starting transfers between devices, from_quarter(): return lax.ppermute(array, 'x', pairs)  14.1 us
    ppermute x6, waiting for transfers between devices, from_quarter(): return lax.ppermute(array, 'x', pairs)  4.02 us
  transfers between devices with their start and end apart: 14, of which 5 were waited for; matrix products, arithmetic and copies ran while one was open for 0% of the time, Pallas kernels for 4%

profile of v5, /device:TPU:37, one launch (start us, length us, event | category | flops | bytes accessed | tf_op | source)
XLA Modules:
  0.0 181.4 jit_solution(13449347073912845278)
XLA Ops:
  0.6 3.1 %pack_kernel.1 = bf16[32,4,16,256]{3,2,1,0:T(8,128)(2,1)} custom-call(s32[32,128]{1,0:T(8,128)} %bitcast.7, bf16[128,2048]{1,0:T(8,128)(2,1)} %proj_ref.1), custom_call_target="tpu_custom_call" | custom-call | flops 134217728 | bytes 1572864 | tf_op jit(solution)/shard_map/pack_kernel/pallas_call | solution.py:50
  3.8 19.6 %all-to-all-start = ((bf16[128,16,256]{2,1,0:T(8,128)(2,1)}), bf16[128,16,256]{2,1,0:T(8,128)(2,1)S(1)}, u32[]{:S(2)}, u32[]{:S(2)}) async-start(bf16[128,16,256]{2,1,0:T(8,128)(2,1)} %bitcast.9), calls=%async_computation | async-start | bytes 2097152 | tf_op jit(solution)/shard_map/all_to_all | solution.py:392
  24.6 10.9 %collective-permute-start = (bf16[144,128]{1,0:T(8,128)(2,1)S(1)}, bf16[144,128]{1,0:T(8,128)(2,1)S(1)}, u32[]{:S(2)}, u32[]{:S(2)}) collective-permute-start(bf16[144,128]{1,0:T(8,128)(2,1)S(1)} %get-tuple-element.28), channel_id=1, source_target_pairs={{0,2},{1,3},{2,0},{3,1},{4,6},{5,7},{6,4},{7,5},{8,10},{9,11},{10,... | collective-permute-start | bytes 110600 | tf_op jit(solution)/shard_map/ppermute | solution.py:403
  35.5 3.6 %collective-permute-start.1 = (bf16[144,128]{1,0:T(8,128)(2,1)S(1)}, bf16[144,128]{1,0:T(8,128)(2,1)S(1)}, u32[]{:S(2)}, u32[]{:S(2)}) collective-permute-start(bf16[144,128]{1,0:T(8,128)(2,1)S(1)} %get-tuple-element.29), channel_id=1, source_target_pairs={{0,3},{1,2},{2,1},{3,0},{4,7},{5,6},{6,5},{7,4},{8,11},{9,10},{10,... | collective-permute-start | bytes 110600 | tf_op jit(solution)/shard_map/ppermute | solution.py:403
  39.1 1.9 %collective-permute-start.2 = (bf16[144,128]{1,0:T(8,128)(2,1)S(1)}, bf16[144,128]{1,0:T(8,128)(2,1)S(1)}, u32[]{:S(2)}, u32[]{:S(2)}) collective-permute-start(bf16[144,128]{1,0:T(8,128)(2,1)S(1)} %get-tuple-element.30), channel_id=1, source_target_pairs={{0,1},{1,0},{2,3},{3,2},{4,5},{5,4},{6,7},{7,6},{8,9},{9,8},{10,11... | collective-permute-start | bytes 110600 | tf_op jit(solution)/shard_map/ppermute | solution.py:403
  41.1 40.2 %collective-permute-done.s2 = bf16[144,128]{1,0:T(8,128)(2,1)S(1)} collective-permute-done((bf16[144,128]{1,0:T(8,128)(2,1)S(1)}, bf16[144,128]{1,0:T(8,128)(2,1)S(1)}, u32[]{:S(2)}, u32[]{:S(2)}) %collective-permute-start) | collective-permute-done | bytes 36896 | tf_op jit(solution)/shard_map/ppermute | solution.py:403
  81.2 2.0 %collective-permute-done.1.s3 = bf16[144,128]{1,0:T(8,128)(2,1)S(1)} collective-permute-done((bf16[144,128]{1,0:T(8,128)(2,1)S(1)}, bf16[144,128]{1,0:T(8,128)(2,1)S(1)}, u32[]{:S(2)}, u32[]{:S(2)}) %collective-permute-start.1) | collective-permute-done | bytes 36896 | tf_op jit(solution)/shard_map/ppermute | solution.py:403
  83.9 2.8 %collective-permute-start.3 = (bf16[512,256]{1,0:T(8,128)(2,1)S(1)}, bf16[512,256]{1,0:T(8,128)(2,1)S(1)}, u32[]{:S(2)}, u32[]{:S(2)}) collective-permute-start(bf16[512,256]{1,0:T(8,128)(2,1)S(1)} %get-tuple-element.33.vk0_ref.vk_ref), channel_id=1, source_target_pairs={{0,4},{4,8},{8,12},{1,5},{5,9},{9,13},{2,6},{6,10},{10,14},{3,7},{... | collective-permute-start | bytes 786440 | tf_op jit(solution)/shard_map/ppermute | solution.py:398
  86.7 1.3 collective-permute-start.4
  88.0 3.1 %collective-permute-start.8 = (bf16[512,128]{1,0:T(8,128)(2,1)S(1)}, bf16[512,128]{1,0:T(8,128)(2,1)S(1)}, u32[]{:S(2)}, u32[]{:S(2)}) collective-permute-start(bf16[512,128]{1,0:T(8,128)(2,1)S(1)} %get-tuple-element.32.query_ref), channel_id=1, source_target_pairs={{4,0},{8,4},{12,8},{5,1},{9,5},{13,9},{6,2},{10,6},{14,10},{7,3},{... | collective-permute-start | bytes 393224 | tf_op jit(solution)/shard_map/ppermute | solution.py:398
  91.1 3.7 %collective-permute-start.9 = (bf16[512,128]{1,0:T(8,128)(2,1)S(1)}, bf16[512,128]{1,0:T(8,128)(2,1)S(1)}, u32[]{:S(2)}, u32[]{:S(2)}) collective-permute-start(bf16[512,128]{1,0:T(8,128)(2,1)S(1)} %get-tuple-element.32.query_ref), channel_id=1, source_target_pairs={{8,0},{12,4},{9,1},{13,5},{10,2},{14,6},{11,3},{15,7},{24,16},{28,... | collective-permute-start | bytes 393224 | tf_op jit(solution)/shard_map/ppermute | solution.py:398
  94.9 4.0 %collective-permute-done.4.vk2_ref = bf16[512,256]{1,0:T(8,128)(2,1)S(1)} collective-permute-done((bf16[512,256]{1,0:T(8,128)(2,1)S(1)}, bf16[512,256]{1,0:T(8,128)(2,1)S(1)}, u32[]{:S(2)}, u32[]{:S(2)}) %collective-permute-start.4) | collective-permute-done | bytes 262176 | tf_op jit(solution)/shard_map/ppermute | solution.py:398
  98.9 1.8 forward_kernel.1
  100.6 1.3 collective-permute-start.10
  101.9 1.9 %collective-permute-start.11 = (bf16[512,128]{1,0:T(8,128)(2,1)S(1)}, bf16[512,128]{1,0:T(8,128)(2,1)S(1)}, u32[]{:S(2)}, u32[]{:S(2)}) collective-permute-start(bf16[512,128]{1,0:T(8,128)(2,1)S(1)} %get-tuple-element.39.mixed_ref), channel_id=1, source_target_pairs={{4,0},{8,4},{12,8},{5,1},{9,5},{13,9},{6,2},{10,6},{14,10},{7,3},{... | collective-permute-start | bytes 393224 | tf_op jit(solution)/shard_map/ppermute | solution.py:398
  103.9 3.8 %query_grad_kernel.1 = (bf16[32,4,16,128]{3,2,1,0:T(8,128)(2,1)S(1)}, f32[2,512,128]{2,1,0:T(8,128)S(1)}, bf16[4,512,256]{2,1,0:T(8,128)(2,1)S(1)}, bf16[2,512,256]{2,1,0:T(8,128)(2,1)S(1)}, f32[2,512,256]{2,1,0:T(8,128)S(1)}) custom-call(s32[512,128]{1,0:T(8,128)S(1)} %get-tuple-element.26.low_ref, s32[8,1536]{1,0:T(8,128)S(1)} %get-tuple-element.38.low_rows_ref, ...), custom_call_target="tpu_custom_call" | custom-call | flops 536870912 | bytes 2097152 | tf_op jit(solution)/shard_map/query_grad_kernel/pallas_call | solution.py:50
  107.7 2.6 %backward_kernel.1 = bf16[32,4,16,256]{3,2,1,0:T(8,128)(2,1)} custom-call(s32[8,1536]{1,0:T(8,128)S(1)} %get-tuple-element.38.low_rows_ref, bf16[4,512,256]{2,1,0:T(8,128)(2,1)S(1)} %get-tuple-element.41.picks_ref, bf16[512,256]{1,0:T(8,128)(2,1)S(1)} %get-tuple-element.33.vk0_ref.vk_ref, bf16[512,128]{1,0:T(8,128)(2,1)S(1)} %collective-permute-done.9.q2_ref, ...), custom_call_target="tpu_custom_call" | custom-call | flops 1073741824 | bytes 3145728 | tf_op jit(solution)/shard_map/backward_kernel/pallas_call | solution.py:50
  110.3 10.5 %all-to-all-start.1 = ((bf16[128,16,256]{2,1,0:T(8,128)(2,1)}), bf16[128,16,256]{2,1,0:T(8,128)(2,1)S(1)}, u32[]{:S(2)}, u32[]{:S(2)}) async-start(bf16[128,16,256]{2,1,0:T(8,128)(2,1)} %bitcast.3), calls=%async_computation.1 | async-start | bytes 2097152 | tf_op jit(solution)/shard_map/all_to_all | solution.py:392
  120.8 10.9 %collective-permute-start.5 = (bf16[128,128]{1,0:T(8,128)(2,1)S(1)}, bf16[128,128]{1,0:T(8,128)(2,1)S(1)}, u32[]{:S(2)}, u32[]{:S(2)}) collective-permute-start(bf16[128,128]{1,0:T(8,128)(2,1)S(1)} %get-tuple-element.35), channel_id=1, source_target_pairs={{0,2},{1,3},{2,0},{3,1},{4,6},{5,7},{6,4},{7,5},{8,10},{9,11},{10,... | collective-permute-start | bytes 98312 | tf_op jit(solution)/shard_map/ppermute | solution.py:403
  131.7 3.6 %collective-permute-start.6 = (bf16[128,128]{1,0:T(8,128)(2,1)S(1)}, bf16[128,128]{1,0:T(8,128)(2,1)S(1)}, u32[]{:S(2)}, u32[]{:S(2)}) collective-permute-start(bf16[128,128]{1,0:T(8,128)(2,1)S(1)} %get-tuple-element.36), channel_id=1, source_target_pairs={{0,3},{1,2},{2,1},{3,0},{4,7},{5,6},{6,5},{7,4},{8,11},{9,10},{10,... | collective-permute-start | bytes 98312 | tf_op jit(solution)/shard_map/ppermute | solution.py:403
  135.3 1.9 %collective-permute-start.7 = (bf16[128,128]{1,0:T(8,128)(2,1)S(1)}, bf16[128,128]{1,0:T(8,128)(2,1)S(1)}, u32[]{:S(2)}, u32[]{:S(2)}) collective-permute-start(bf16[128,128]{1,0:T(8,128)(2,1)S(1)} %get-tuple-element.37), channel_id=1, source_target_pairs={{0,1},{1,0},{2,3},{3,2},{4,5},{5,4},{6,7},{7,6},{8,9},{9,8},{10,11... | collective-permute-start | bytes 98312 | tf_op jit(solution)/shard_map/ppermute | solution.py:403
  137.3 41.2 %collective-permute-done.5.l2 = bf16[128,128]{1,0:T(8,128)(2,1)S(1)} collective-permute-done((bf16[128,128]{1,0:T(8,128)(2,1)S(1)}, bf16[128,128]{1,0:T(8,128)(2,1)S(1)}, u32[]{:S(2)}, u32[]{:S(2)}) %collective-permute-start.5) | collective-permute-done | bytes 32800 | tf_op jit(solution)/shard_map/ppermute | solution.py:403
  178.5 1.6 collective-permute-done.6.l3
  180.1 1.3 finish_kernel.1
  (17 shorter events, 1.8 us)
Async XLA Ops:
  3.7 19.7 %copy-start = (bf16[128,512]{1,0:T(8,128)(2,1)S(1)}, bf16[128,512]{1,0:T(8,128)(2,1)}, u32[]{:S(2)}) copy-start(bf16[128,512]{1,0:T(8,128)(2,1)} %grad_ref.1) | copy-start | bytes 393220
  3.7 19.7 %copy-start.1 = (s32[1,4096]{1,0:T(1,128)S(1)}, s32[1,4096]{1,0:T(1,128)}, u32[]{:S(2)}) copy-start(s32[1,4096]{1,0:T(1,128)} %param.5) | copy-start | bytes 49156
  3.7 19.7 %copy-start.2 = (s32[1,3]{1,0:T(1,128)S(1)}, s32[1,3]{1,0:T(1,128)}, u32[]{:S(2)}) copy-start(s32[1,3]{1,0:T(1,128)} %lengths_ref.1) | copy-start | bytes 40
  3.8 79.5 %all-to-all-start = ((bf16[128,16,256]{2,1,0:T(8,128)(2,1)}), bf16[128,16,256]{2,1,0:T(8,128)(2,1)S(1)}, u32[]{:S(2)}, u32[]{:S(2)}) async-start(bf16[128,16,256]{2,1,0:T(8,128)(2,1)} %bitcast.9), calls=%async_computation | async-start | bytes 2097152 | tf_op jit(solution)/shard_map/all_to_all | solution.py:392
  24.6 56.6 %collective-permute-start = (bf16[144,128]{1,0:T(8,128)(2,1)S(1)}, bf16[144,128]{1,0:T(8,128)(2,1)S(1)}, u32[]{:S(2)}, u32[]{:S(2)}) collective-permute-start(bf16[144,128]{1,0:T(8,128)(2,1)S(1)} %get-tuple-element.28), channel_id=1, source_target_pairs={{0,2},{1,3},{2,0},{3,1},{4,6},{5,7},{6,4},{7,5},{8,10},{9,11},{10,... | collective-permute-start | bytes 110600 | tf_op jit(solution)/shard_map/ppermute | solution.py:403
  35.5 47.7 %collective-permute-start.1 = (bf16[144,128]{1,0:T(8,128)(2,1)S(1)}, bf16[144,128]{1,0:T(8,128)(2,1)S(1)}, u32[]{:S(2)}, u32[]{:S(2)}) collective-permute-start(bf16[144,128]{1,0:T(8,128)(2,1)S(1)} %get-tuple-element.29), channel_id=1, source_target_pairs={{0,3},{1,2},{2,1},{3,0},{4,7},{5,6},{6,5},{7,4},{8,11},{9,10},{10,... | collective-permute-start | bytes 110600 | tf_op jit(solution)/shard_map/ppermute | solution.py:403
  39.1 44.1 %collective-permute-start.2 = (bf16[144,128]{1,0:T(8,128)(2,1)S(1)}, bf16[144,128]{1,0:T(8,128)(2,1)S(1)}, u32[]{:S(2)}, u32[]{:S(2)}) collective-permute-start(bf16[144,128]{1,0:T(8,128)(2,1)S(1)} %get-tuple-element.30), channel_id=1, source_target_pairs={{0,1},{1,0},{2,3},{3,2},{4,5},{5,4},{6,7},{7,6},{8,9},{9,8},{10,11... | collective-permute-start | bytes 110600 | tf_op jit(solution)/shard_map/ppermute | solution.py:403
  83.9 11.0 %collective-permute-start.3 = (bf16[512,256]{1,0:T(8,128)(2,1)S(1)}, bf16[512,256]{1,0:T(8,128)(2,1)S(1)}, u32[]{:S(2)}, u32[]{:S(2)}) collective-permute-start(bf16[512,256]{1,0:T(8,128)(2,1)S(1)} %get-tuple-element.33.vk0_ref.vk_ref), channel_id=1, source_target_pairs={{0,4},{4,8},{8,12},{1,5},{5,9},{9,13},{2,6},{6,10},{10,14},{3,7},{... | collective-permute-start | bytes 786440 | tf_op jit(solution)/shard_map/ppermute | solution.py:398
  86.7 12.1 %collective-permute-start.4 = (bf16[512,256]{1,0:T(8,128)(2,1)S(1)}, bf16[512,256]{1,0:T(8,128)(2,1)S(1)}, u32[]{:S(2)}, u32[]{:S(2)}) collective-permute-start(bf16[512,256]{1,0:T(8,128)(2,1)S(1)} %get-tuple-element.33.vk0_ref.vk_ref), channel_id=1, source_target_pairs={{0,8},{4,12},{1,9},{5,13},{2,10},{6,14},{3,11},{7,15},{16,24},{20,... | collective-permute-start | bytes 786440 | tf_op jit(solution)/shard_map/ppermute | solution.py:398
  88.0 15.8 %collective-permute-start.8 = (bf16[512,128]{1,0:T(8,128)(2,1)S(1)}, bf16[512,128]{1,0:T(8,128)(2,1)S(1)}, u32[]{:S(2)}, u32[]{:S(2)}) collective-permute-start(bf16[512,128]{1,0:T(8,128)(2,1)S(1)} %get-tuple-element.32.query_ref), channel_id=1, source_target_pairs={{4,0},{8,4},{12,8},{5,1},{9,5},{13,9},{6,2},{10,6},{14,10},{7,3},{... | collective-permute-start | bytes 393224 | tf_op jit(solution)/shard_map/ppermute | solution.py:398
  91.1 16.5 %collective-permute-start.9 = (bf16[512,128]{1,0:T(8,128)(2,1)S(1)}, bf16[512,128]{1,0:T(8,128)(2,1)S(1)}, u32[]{:S(2)}, u32[]{:S(2)}) collective-permute-start(bf16[512,128]{1,0:T(8,128)(2,1)S(1)} %get-tuple-element.32.query_ref), channel_id=1, source_target_pairs={{8,0},{12,4},{9,1},{13,5},{10,2},{14,6},{11,3},{15,7},{24,16},{28,... | collective-permute-start | bytes 393224 | tf_op jit(solution)/shard_map/ppermute | solution.py:398
  100.6 7.0 %collective-permute-start.10 = (bf16[512,128]{1,0:T(8,128)(2,1)S(1)}, bf16[512,128]{1,0:T(8,128)(2,1)S(1)}, u32[]{:S(2)}, u32[]{:S(2)}) collective-permute-start(bf16[512,128]{1,0:T(8,128)(2,1)S(1)} %get-tuple-element.39.mixed_ref), channel_id=1, source_target_pairs={{8,0},{12,4},{9,1},{13,5},{10,2},{14,6},{11,3},{15,7},{24,16},{28,... | collective-permute-start | bytes 393224 | tf_op jit(solution)/shard_map/ppermute | solution.py:398
  101.9 5.7 %collective-permute-start.11 = (bf16[512,128]{1,0:T(8,128)(2,1)S(1)}, bf16[512,128]{1,0:T(8,128)(2,1)S(1)}, u32[]{:S(2)}, u32[]{:S(2)}) collective-permute-start(bf16[512,128]{1,0:T(8,128)(2,1)S(1)} %get-tuple-element.39.mixed_ref), channel_id=1, source_target_pairs={{4,0},{8,4},{12,8},{5,1},{9,5},{13,9},{6,2},{10,6},{14,10},{7,3},{... | collective-permute-start | bytes 393224 | tf_op jit(solution)/shard_map/ppermute | solution.py:398
  110.3 69.8 %all-to-all-start.1 = ((bf16[128,16,256]{2,1,0:T(8,128)(2,1)}), bf16[128,16,256]{2,1,0:T(8,128)(2,1)S(1)}, u32[]{:S(2)}, u32[]{:S(2)}) async-start(bf16[128,16,256]{2,1,0:T(8,128)(2,1)} %bitcast.3), calls=%async_computation.1 | async-start | bytes 2097152 | tf_op jit(solution)/shard_map/all_to_all | solution.py:392
  120.8 57.7 %collective-permute-start.5 = (bf16[128,128]{1,0:T(8,128)(2,1)S(1)}, bf16[128,128]{1,0:T(8,128)(2,1)S(1)}, u32[]{:S(2)}, u32[]{:S(2)}) collective-permute-start(bf16[128,128]{1,0:T(8,128)(2,1)S(1)} %get-tuple-element.35), channel_id=1, source_target_pairs={{0,2},{1,3},{2,0},{3,1},{4,6},{5,7},{6,4},{7,5},{8,10},{9,11},{10,... | collective-permute-start | bytes 98312 | tf_op jit(solution)/shard_map/ppermute | solution.py:403
  131.7 48.3 %collective-permute-start.6 = (bf16[128,128]{1,0:T(8,128)(2,1)S(1)}, bf16[128,128]{1,0:T(8,128)(2,1)S(1)}, u32[]{:S(2)}, u32[]{:S(2)}) collective-permute-start(bf16[128,128]{1,0:T(8,128)(2,1)S(1)} %get-tuple-element.36), channel_id=1, source_target_pairs={{0,3},{1,2},{2,1},{3,0},{4,7},{5,6},{6,5},{7,4},{8,11},{9,10},{10,... | collective-permute-start | bytes 98312 | tf_op jit(solution)/shard_map/ppermute | solution.py:403
  135.3 44.7 %collective-permute-start.7 = (bf16[128,128]{1,0:T(8,128)(2,1)S(1)}, bf16[128,128]{1,0:T(8,128)(2,1)S(1)}, u32[]{:S(2)}, u32[]{:S(2)}) collective-permute-start(bf16[128,128]{1,0:T(8,128)(2,1)S(1)} %get-tuple-element.37), channel_id=1, source_target_pairs={{0,1},{1,0},{2,3},{3,2},{4,5},{5,4},{6,7},{7,6},{8,9},{9,8},{10,11... | collective-permute-start | bytes 98312 | tf_op jit(solution)/shard_map/ppermute | solution.py:403

commit v6 on v5

--- a/solution.py
+++ b/solution.py
@@ -128,7 +128,7 @@
 
 
 def side_kernel(lengths_ref, dest_ref, grad_ref, *out_refs):
-    *out_refs, home_ref, low_ref, low_rows_ref = out_refs
+    *out_refs, code_ref, home_ref, low_ref, low_rows_ref = out_refs
     bounds = user_bounds(lengths_ref)
     base = lax.axis_index("x") * PART
     low_ref[...] = first_key(base + iota(low_ref.shape, 0), bounds)
@@ -152,16 +152,12 @@
         total = total + jnp.where(row_of == place[i : i + 1], code[i : i + 1], 0.0)
     codes = jnp.broadcast_to(jnp.sum(total, axis=1, keepdims=True), square).T
     for k, out_ref in enumerate(out_refs):
-        out_ref[:ROWS] = grad_ref[:, head_columns(lax.axis_index("h") ^ k)]
-        out_ref[ROWS:] = codes[:CHUNK].astype(BF16)
+        out_ref[...] = grad_ref[:, head_columns(lax.axis_index("h") ^ k)]
+    code_ref[...] = codes[0:1]
 
 
 def chunk_row(code, half):
     return (code >> 3) * CHUNK + half * CAP + (code & (CAP - 1))
-
-
-def code_across(side_ref):
-    return side_ref[ROWS : ROWS + CHUNK].astype(F32)[0:1]
 
 
 def both_halves(code, axis):
@@ -176,13 +172,14 @@
 def code_of_block(c, head, sides):
     code = jnp.zeros((1, ROWS), F32)
     for k, side_ref in enumerate(sides):
-        code = jnp.where((head ^ k) == c, code_across(side_ref), code)
+        code = jnp.where((head ^ k) == c, side_ref[...], code)
     return code
 
 
 def unpack_kernel(
-    s0, s2, s3, s1, arrived_ref, gate_ref, query_ref, vk_ref,
+    g0, g2, g3, g1, s0, s2, s3, s1, arrived_ref, gate_ref, query_ref, vk_ref,
 ):
+    del g0, g2, g3, g1
     for c in range(HEADS):
         rows = slice(c * ROWS, (c + 1) * ROWS)
         code = code_of_block(c, lax.axis_index("h"), (s0, s1, s2, s3))
@@ -236,7 +233,7 @@
     gating = gate_ref[...].astype(F32)
     head = lax.axis_index("h")
     for k, part in enumerate((s0, s1, s2, s3)):
-        held[block_rows(head ^ k), HEAD_DIM:] = part[:ROWS]
+        held[block_rows(head ^ k), HEAD_DIM:] = part[...]
     upstream = held[:, HEAD_DIM:].astype(F32)
     layer = (normed * gating).astype(BF16)
     grad_normed = upstream * gating
@@ -309,7 +306,7 @@
 def back_picks(sides, picks_ref):
     sublane = iota((N_DP * CHUNK, 2 * ROWS), 0)
     for k, side_ref in enumerate(sides):
-        at = both_halves(code_across(side_ref).astype(jnp.int32), 1)
+        at = both_halves(side_ref[...].astype(jnp.int32), 1)
         picks_ref[lax.axis_index("h") ^ k] = jnp.where(sublane == at, 1.0, 0.0).astype(BF16)
 
 
@@ -419,19 +416,22 @@
         flops=2 * 256 * 128 * 2048, nbytes=3 << 19,
         hbm_in=(1,), hbm_out=True, limit=62 * 1024 * 1024,
     )
-    *side_out, home, low, low_rows = call(
+    *side_out, code, home, low, low_rows = call(
         side_kernel,
-        [shape(ROWS + CHUNK, HEAD_DIM)] * HEADS
+        pieces
         + [
+            shape(1, ROWS, dtype=F32),
             shape(2 * ROWS, N_DP * CHUNK), shape(PART, ROWS, dtype=jnp.int32),
             shape(8, (REACH + 1) * PART, dtype=jnp.int32),
         ],
         (lengths, mapping, grad_out), smem=(0,), nbytes=3 << 17,
     )
     side = swap_heads(side_out)
+    codes = swap_heads([code] * HEADS)
     arrived = route(packed)
     gate, queries, vk = call(
-        unpack_kernel, [head_part, head_part, shape(PART, 2 * HEAD_DIM)], (*side, arrived),
+        unpack_kernel, [head_part, head_part, shape(PART, 2 * HEAD_DIM)], (*side, *codes, arrived),
+        hbm_in=(0, 1, 2, 3),
         flops=1 << 28, nbytes=2 << 20,
     )
     vk_parts = (from_quarter(vk, -1), from_quarter(vk, -2), vk)
@@ -449,7 +449,7 @@
         query_grad_kernel,
         [half_chunked, shape(2, PART, HEAD_DIM, dtype=F32), shape(HEADS, N_DP * CHUNK, 2 * ROWS),
          shape(PART // STEP, PART, STEP), shape(PART // STEP, PART, STEP, dtype=F32)],
-        (low, low_rows, *side, mixed, gate_grad, queries, query_parts[1], *vk_parts),
+        (low, low_rows, *codes, mixed, gate_grad, queries, query_parts[1], *vk_parts),
         scratch=[done], flops=1 << 29, nbytes=2 << 20,
     )
     (back,) = call(

time: 182 us -> 185 us (1.016)
  starting transfers between devices: 77.1 us -> 94 us
  waiting for transfers between devices: 89 us -> 74.6 us
    ppermute x6 -> x9, starting transfers between devices: 32.9 us -> 50 us  [swap_heads(): lax.ppermute(pieces[k], 'h', [(i, i ^ k) for i in range(HEADS)])]
    ppermute x6 -> x9, waiting for transfers between devices: 85 us -> 70.5 us  [swap_heads(): lax.ppermute(pieces[k], 'h', [(i, i ^ k) for i in range(HEADS)])]
  transfers between devices with their start and end apart: 14 -> 17, of which waited for: 5 -> 5; matrix products, arithmetic and copies ran while one was open for 0% -> 0% of each run, Pallas kernels for 4% -> 4%
where the time goes in v6:
time: 185 us; the launch traced here: 184 us
  starting transfers between devices  94 us (51%)
  waiting for transfers between devices  74.6 us (40%)
  Pallas kernels  14.3 us (8%)
    ppermute x9, waiting for transfers between devices, swap_heads(): lax.ppermute(pieces[k], 'h', [(i, i ^ k) for i in range(HEADS)])  70.5 us
    ppermute x9, starting transfers between devices, swap_heads(): lax.ppermute(pieces[k], 'h', [(i, i ^ k) for i in range(HEADS)])  50 us
    all_to_all x2, starting transfers between devices, route(): moved = lax.all_to_all(flat, ('dp', 'h'), 0, 0, tiled=True)  29.9 us
    pallas_call x7, Pallas kernels, call(): pl.pallas_call(kernel, out_shape=outs, in_specs=[pl.BlockSpec(memory_spac...  14.3 us
    ppermute x6, starting transfers between devices, from_quarter(): return lax.ppermute(array, 'x', pairs)  14.1 us
    ppermute x6, waiting for transfers between devices, from_quarter(): return lax.ppermute(array, 'x', pairs)  4.14 us
  transfers between devices with their start and end apart: 17, of which 5 were waited for; matrix products, arithmetic and copies ran while one was open for 0% of the time, Pallas kernels for 4%

profile of v6, /device:TPU:37, one launch (start us, length us, event | category | flops | bytes accessed | tf_op | source)
XLA Modules:
  0.0 184.0 jit_solution(13784817269610401094)
XLA Ops:
  0.6 3.1 %pack_kernel.1 = bf16[32,4,16,256]{3,2,1,0:T(8,128)(2,1)} custom-call(s32[32,128]{1,0:T(8,128)} %bitcast.7, bf16[128,2048]{1,0:T(8,128)(2,1)} %proj_ref.1), custom_call_target="tpu_custom_call" | custom-call | flops 134217728 | bytes 1572864 | tf_op jit(solution)/shard_map/pack_kernel/pallas_call | solution.py:50
  3.8 19.6 %all-to-all-start = ((bf16[128,16,256]{2,1,0:T(8,128)(2,1)}), bf16[128,16,256]{2,1,0:T(8,128)(2,1)S(1)}, u32[]{:S(2)}, u32[]{:S(2)}) async-start(bf16[128,16,256]{2,1,0:T(8,128)(2,1)} %bitcast.9), calls=%async_computation | async-start | bytes 2097152 | tf_op jit(solution)/shard_map/all_to_all | solution.py:389
  24.6 10.9 %collective-permute-start = (bf16[128,128]{1,0:T(8,128)(2,1)S(1)}, bf16[128,128]{1,0:T(8,128)(2,1)S(1)}, u32[]{:S(2)}, u32[]{:S(2)}) collective-permute-start(bf16[128,128]{1,0:T(8,128)(2,1)S(1)} %get-tuple-element.29), channel_id=1, source_target_pairs={{0,2},{1,3},{2,0},{3,1},{4,6},{5,7},{6,4},{7,5},{8,10},{9,11},{10,... | collective-permute-start | bytes 98312 | tf_op jit(solution)/shard_map/ppermute | solution.py:400
  35.5 3.6 %collective-permute-start.1 = (bf16[128,128]{1,0:T(8,128)(2,1)S(1)}, bf16[128,128]{1,0:T(8,128)(2,1)S(1)}, u32[]{:S(2)}, u32[]{:S(2)}) collective-permute-start(bf16[128,128]{1,0:T(8,128)(2,1)S(1)} %get-tuple-element.30), channel_id=1, source_target_pairs={{0,3},{1,2},{2,1},{3,0},{4,7},{5,6},{6,5},{7,4},{8,11},{9,10},{10,... | collective-permute-start | bytes 98312 | tf_op jit(solution)/shard_map/ppermute | solution.py:400
  39.1 1.9 %collective-permute-start.2 = (bf16[128,128]{1,0:T(8,128)(2,1)S(1)}, bf16[128,128]{1,0:T(8,128)(2,1)S(1)}, u32[]{:S(2)}, u32[]{:S(2)}) collective-permute-start(bf16[128,128]{1,0:T(8,128)(2,1)S(1)} %get-tuple-element.31), channel_id=1, source_target_pairs={{0,1},{1,0},{2,3},{3,2},{4,5},{5,4},{6,7},{7,6},{8,9},{9,8},{10,11... | collective-permute-start | bytes 98312 | tf_op jit(solution)/shard_map/ppermute | solution.py:400
  41.1 10.9 %collective-permute-start.3 = (f32[1,128]{1,0:T(1,128)S(1)}, f32[1,128]{1,0:T(1,128)S(1)}, u32[]{:S(2)}, u32[]{:S(2)}) collective-permute-start(f32[1,128]{1,0:T(1,128)S(1)} %get-tuple-element.32.s0), channel_id=1, source_target_pairs={{0,2},{1,3},{2,0},{3,1},{4,6},{5,7},{6,4},{7,5},{8,10},{9,11},{10,... | collective-permute-start | bytes 1544 | tf_op jit(solution)/shard_map/ppermute | solution.py:400
  52.0 3.8 %collective-permute-start.4 = (f32[1,128]{1,0:T(1,128)S(1)}, f32[1,128]{1,0:T(1,128)S(1)}, u32[]{:S(2)}, u32[]{:S(2)}) collective-permute-start(f32[1,128]{1,0:T(1,128)S(1)} %get-tuple-element.32.s0), channel_id=1, source_target_pairs={{0,3},{1,2},{2,1},{3,0},{4,7},{5,6},{6,5},{7,4},{8,11},{9,10},{10,... | collective-permute-start | bytes 1544 | tf_op jit(solution)/shard_map/ppermute | solution.py:400
  55.7 26.9 %collective-permute-done.3.s2 = f32[1,128]{1,0:T(1,128)S(1)} collective-permute-done((f32[1,128]{1,0:T(1,128)S(1)}, f32[1,128]{1,0:T(1,128)S(1)}, u32[]{:S(2)}, u32[]{:S(2)}) %collective-permute-start.3) | collective-permute-done | bytes 544 | tf_op jit(solution)/shard_map/ppermute | solution.py:400
  82.7 2.4 %collective-permute-start.5 = (f32[1,128]{1,0:T(1,128)S(1)}, f32[1,128]{1,0:T(1,128)S(1)}, u32[]{:S(2)}, u32[]{:S(2)}) collective-permute-start(f32[1,128]{1,0:T(1,128)S(1)} %get-tuple-element.32.s0), channel_id=1, source_target_pairs={{0,1},{1,0},{2,3},{3,2},{4,5},{5,4},{6,7},{7,6},{8,9},{9,8},{10,11... | collective-permute-start | bytes 1544 | tf_op jit(solution)/shard_map/ppermute | solution.py:400
  86.6 2.8 %collective-permute-start.6 = (bf16[512,256]{1,0:T(8,128)(2,1)S(1)}, bf16[512,256]{1,0:T(8,128)(2,1)S(1)}, u32[]{:S(2)}, u32[]{:S(2)}) collective-permute-start(bf16[512,256]{1,0:T(8,128)(2,1)S(1)} %get-tuple-element.35.vk0_ref.vk_ref), channel_id=1, source_target_pairs={{0,4},{4,8},{8,12},{1,5},{5,9},{9,13},{2,6},{6,10},{10,14},{3,7},{... | collective-permute-start | bytes 786440 | tf_op jit(solution)/shard_map/ppermute | solution.py:395
  90.7 3.1 %collective-permute-start.11 = (bf16[512,128]{1,0:T(8,128)(2,1)S(1)}, bf16[512,128]{1,0:T(8,128)(2,1)S(1)}, u32[]{:S(2)}, u32[]{:S(2)}) collective-permute-start(bf16[512,128]{1,0:T(8,128)(2,1)S(1)} %get-tuple-element.34.query_ref), channel_id=1, source_target_pairs={{4,0},{8,4},{12,8},{5,1},{9,5},{13,9},{6,2},{10,6},{14,10},{7,3},{... | collective-permute-start | bytes 393224 | tf_op jit(solution)/shard_map/ppermute | solution.py:395
  93.8 3.7 %collective-permute-start.12 = (bf16[512,128]{1,0:T(8,128)(2,1)S(1)}, bf16[512,128]{1,0:T(8,128)(2,1)S(1)}, u32[]{:S(2)}, u32[]{:S(2)}) collective-permute-start(bf16[512,128]{1,0:T(8,128)(2,1)S(1)} %get-tuple-element.34.query_ref), channel_id=1, source_target_pairs={{8,0},{12,4},{9,1},{13,5},{10,2},{14,6},{11,3},{15,7},{24,16},{28,... | collective-permute-start | bytes 393224 | tf_op jit(solution)/shard_map/ppermute | solution.py:395
  97.5 4.1 %collective-permute-done.7.vk2_ref = bf16[512,256]{1,0:T(8,128)(2,1)S(1)} collective-permute-done((bf16[512,256]{1,0:T(8,128)(2,1)S(1)}, bf16[512,256]{1,0:T(8,128)(2,1)S(1)}, u32[]{:S(2)}, u32[]{:S(2)}) %collective-permute-start.7) | collective-permute-done | bytes 262176 | tf_op jit(solution)/shard_map/ppermute | solution.py:395
  101.7 1.8 forward_kernel.1
  104.7 1.9 %collective-permute-start.14 = (bf16[512,128]{1,0:T(8,128)(2,1)S(1)}, bf16[512,128]{1,0:T(8,128)(2,1)S(1)}, u32[]{:S(2)}, u32[]{:S(2)}) collective-permute-start(bf16[512,128]{1,0:T(8,128)(2,1)S(1)} %get-tuple-element.41.mixed_ref), channel_id=1, source_target_pairs={{4,0},{8,4},{12,8},{5,1},{9,5},{13,9},{6,2},{10,6},{14,10},{7,3},{... | collective-permute-start | bytes 393224 | tf_op jit(solution)/shard_map/ppermute | solution.py:395
  106.7 3.8 %query_grad_kernel.1 = (bf16[32,4,16,128]{3,2,1,0:T(8,128)(2,1)S(1)}, f32[2,512,128]{2,1,0:T(8,128)S(1)}, bf16[4,512,256]{2,1,0:T(8,128)(2,1)S(1)}, bf16[2,512,256]{2,1,0:T(8,128)(2,1)S(1)}, f32[2,512,256]{2,1,0:T(8,128)S(1)}) custom-call(s32[512,128]{1,0:T(8,128)S(1)} %get-tuple-element.27.low_ref, s32[8,1536]{1,0:T(8,128)S(1)} %get-tuple-element.40.low_rows_ref, ...), custom_call_target="tpu_custom_call" | custom-call | flops 536870912 | bytes 2097152 | tf_op jit(solution)/shard_map/query_grad_kernel/pallas_call | solution.py:50
  110.4 2.6 %backward_kernel.1 = bf16[32,4,16,256]{3,2,1,0:T(8,128)(2,1)} custom-call(s32[8,1536]{1,0:T(8,128)S(1)} %get-tuple-element.40.low_rows_ref, bf16[4,512,256]{2,1,0:T(8,128)(2,1)S(1)} %get-tuple-element.43.picks_ref, bf16[512,256]{1,0:T(8,128)(2,1)S(1)} %get-tuple-element.35.vk0_ref.vk_ref, bf16[512,128]{1,0:T(8,128)(2,1)S(1)} %collective-permute-done.12.q2_ref, ...), custom_call_target="tpu_custom_call" | custom-call | flops 1073741824 | bytes 3145728 | tf_op jit(solution)/shard_map/backward_kernel/pallas_call | solution.py:50
  113.1 10.3 %all-to-all-start.1 = ((bf16[128,16,256]{2,1,0:T(8,128)(2,1)}), bf16[128,16,256]{2,1,0:T(8,128)(2,1)S(1)}, u32[]{:S(2)}, u32[]{:S(2)}) async-start(bf16[128,16,256]{2,1,0:T(8,128)(2,1)} %bitcast.3), calls=%async_computation.1 | async-start | bytes 2097152 | tf_op jit(solution)/shard_map/all_to_all | solution.py:389
  123.4 10.9 %collective-permute-start.8 = (bf16[128,128]{1,0:T(8,128)(2,1)S(1)}, bf16[128,128]{1,0:T(8,128)(2,1)S(1)}, u32[]{:S(2)}, u32[]{:S(2)}) collective-permute-start(bf16[128,128]{1,0:T(8,128)(2,1)S(1)} %get-tuple-element.37), channel_id=1, source_target_pairs={{0,2},{1,3},{2,0},{3,1},{4,6},{5,7},{6,4},{7,5},{8,10},{9,11},{10,... | collective-permute-start | bytes 98312 | tf_op jit(solution)/shard_map/ppermute | solution.py:400
  134.3 3.6 %collective-permute-start.9 = (bf16[128,128]{1,0:T(8,128)(2,1)S(1)}, bf16[128,128]{1,0:T(8,128)(2,1)S(1)}, u32[]{:S(2)}, u32[]{:S(2)}) collective-permute-start(bf16[128,128]{1,0:T(8,128)(2,1)S(1)} %get-tuple-element.38), channel_id=1, source_target_pairs={{0,3},{1,2},{2,1},{3,0},{4,7},{5,6},{6,5},{7,4},{8,11},{9,10},{10,... | collective-permute-start | bytes 98312 | tf_op jit(solution)/shard_map/ppermute | solution.py:400
  137.9 1.9 %collective-permute-start.10 = (bf16[128,128]{1,0:T(8,128)(2,1)S(1)}, bf16[128,128]{1,0:T(8,128)(2,1)S(1)}, u32[]{:S(2)}, u32[]{:S(2)}) collective-permute-start(bf16[128,128]{1,0:T(8,128)(2,1)S(1)} %get-tuple-element.39), channel_id=1, source_target_pairs={{0,1},{1,0},{2,3},{3,2},{4,5},{5,4},{6,7},{7,6},{8,9},{9,8},{10,11... | collective-permute-start | bytes 98312 | tf_op jit(solution)/shard_map/ppermute | solution.py:400
  139.9 41.2 %collective-permute-done.8.l2 = bf16[128,128]{1,0:T(8,128)(2,1)S(1)} collective-permute-done((bf16[128,128]{1,0:T(8,128)(2,1)S(1)}, bf16[128,128]{1,0:T(8,128)(2,1)S(1)}, u32[]{:S(2)}, u32[]{:S(2)}) %collective-permute-start.8) | collective-permute-done | bytes 32800 | tf_op jit(solution)/shard_map/ppermute | solution.py:400
  181.1 1.6 collective-permute-done.9.l3
  182.7 1.3 finish_kernel.1
  (23 shorter events, 5.2 us)
Async XLA Ops:
  3.7 19.7 %copy-start = (bf16[128,512]{1,0:T(8,128)(2,1)S(1)}, bf16[128,512]{1,0:T(8,128)(2,1)}, u32[]{:S(2)}) copy-start(bf16[128,512]{1,0:T(8,128)(2,1)} %grad_ref.1) | copy-start | bytes 393220
  3.7 19.7 %copy-start.1 = (s32[1,4096]{1,0:T(1,128)S(1)}, s32[1,4096]{1,0:T(1,128)}, u32[]{:S(2)}) copy-start(s32[1,4096]{1,0:T(1,128)} %param.5) | copy-start | bytes 49156
  3.7 19.7 %copy-start.2 = (s32[1,3]{1,0:T(1,128)S(1)}, s32[1,3]{1,0:T(1,128)}, u32[]{:S(2)}) copy-start(s32[1,3]{1,0:T(1,128)} %lengths_ref.1) | copy-start | bytes 40
  3.8 82.1 %all-to-all-start = ((bf16[128,16,256]{2,1,0:T(8,128)(2,1)}), bf16[128,16,256]{2,1,0:T(8,128)(2,1)S(1)}, u32[]{:S(2)}, u32[]{:S(2)}) async-start(bf16[128,16,256]{2,1,0:T(8,128)(2,1)} %bitcast.9), calls=%async_computation | async-start | bytes 2097152 | tf_op jit(solution)/shard_map/all_to_all | solution.py:389
  24.6 61.3 %collective-permute-start = (bf16[128,128]{1,0:T(8,128)(2,1)S(1)}, bf16[128,128]{1,0:T(8,128)(2,1)S(1)}, u32[]{:S(2)}, u32[]{:S(2)}) collective-permute-start(bf16[128,128]{1,0:T(8,128)(2,1)S(1)} %get-tuple-element.29), channel_id=1, source_target_pairs={{0,2},{1,3},{2,0},{3,1},{4,6},{5,7},{6,4},{7,5},{8,10},{9,11},{10,... | collective-permute-start | bytes 98312 | tf_op jit(solution)/shard_map/ppermute | solution.py:400
  35.5 50.4 %collective-permute-start.1 = (bf16[128,128]{1,0:T(8,128)(2,1)S(1)}, bf16[128,128]{1,0:T(8,128)(2,1)S(1)}, u32[]{:S(2)}, u32[]{:S(2)}) collective-permute-start(bf16[128,128]{1,0:T(8,128)(2,1)S(1)} %get-tuple-element.30), channel_id=1, source_target_pairs={{0,3},{1,2},{2,1},{3,0},{4,7},{5,6},{6,5},{7,4},{8,11},{9,10},{10,... | collective-permute-start | bytes 98312 | tf_op jit(solution)/shard_map/ppermute | solution.py:400
  39.1 46.8 %collective-permute-start.2 = (bf16[128,128]{1,0:T(8,128)(2,1)S(1)}, bf16[128,128]{1,0:T(8,128)(2,1)S(1)}, u32[]{:S(2)}, u32[]{:S(2)}) collective-permute-start(bf16[128,128]{1,0:T(8,128)(2,1)S(1)} %get-tuple-element.31), channel_id=1, source_target_pairs={{0,1},{1,0},{2,3},{3,2},{4,5},{5,4},{6,7},{7,6},{8,9},{9,8},{10,11... | collective-permute-start | bytes 98312 | tf_op jit(solution)/shard_map/ppermute | solution.py:400
  41.1 41.6 %collective-permute-start.3 = (f32[1,128]{1,0:T(1,128)S(1)}, f32[1,128]{1,0:T(1,128)S(1)}, u32[]{:S(2)}, u32[]{:S(2)}) collective-permute-start(f32[1,128]{1,0:T(1,128)S(1)} %get-tuple-element.32.s0), channel_id=1, source_target_pairs={{0,2},{1,3},{2,0},{3,1},{4,6},{5,7},{6,4},{7,5},{8,10},{9,11},{10,... | collective-permute-start | bytes 1544 | tf_op jit(solution)/shard_map/ppermute | solution.py:400
  52.0 33.1 %collective-permute-start.4 = (f32[1,128]{1,0:T(1,128)S(1)}, f32[1,128]{1,0:T(1,128)S(1)}, u32[]{:S(2)}, u32[]{:S(2)}) collective-permute-start(f32[1,128]{1,0:T(1,128)S(1)} %get-tuple-element.32.s0), channel_id=1, source_target_pairs={{0,3},{1,2},{2,1},{3,0},{4,7},{5,6},{6,5},{7,4},{8,11},{9,10},{10,... | collective-permute-start | bytes 1544 | tf_op jit(solution)/shard_map/ppermute | solution.py:400
  82.7 3.2 %collective-permute-start.5 = (f32[1,128]{1,0:T(1,128)S(1)}, f32[1,128]{1,0:T(1,128)S(1)}, u32[]{:S(2)}, u32[]{:S(2)}) collective-permute-start(f32[1,128]{1,0:T(1,128)S(1)} %get-tuple-element.32.s0), channel_id=1, source_target_pairs={{0,1},{1,0},{2,3},{3,2},{4,5},{5,4},{6,7},{7,6},{8,9},{9,8},{10,11... | collective-permute-start | bytes 1544 | tf_op jit(solution)/shard_map/ppermute | solution.py:400
  86.6 11.0 %collective-permute-start.6 = (bf16[512,256]{1,0:T(8,128)(2,1)S(1)}, bf16[512,256]{1,0:T(8,128)(2,1)S(1)}, u32[]{:S(2)}, u32[]{:S(2)}) collective-permute-start(bf16[512,256]{1,0:T(8,128)(2,1)S(1)} %get-tuple-element.35.vk0_ref.vk_ref), channel_id=1, source_target_pairs={{0,4},{4,8},{8,12},{1,5},{5,9},{9,13},{2,6},{6,10},{10,14},{3,7},{... | collective-permute-start | bytes 786440 | tf_op jit(solution)/shard_map/ppermute | solution.py:395
  89.4 12.3 %collective-permute-start.7 = (bf16[512,256]{1,0:T(8,128)(2,1)S(1)}, bf16[512,256]{1,0:T(8,128)(2,1)S(1)}, u32[]{:S(2)}, u32[]{:S(2)}) collective-permute-start(bf16[512,256]{1,0:T(8,128)(2,1)S(1)} %get-tuple-element.35.vk0_ref.vk_ref), channel_id=1, source_target_pairs={{0,8},{4,12},{1,9},{5,13},{2,10},{6,14},{3,11},{7,15},{16,24},{20,... | collective-permute-start | bytes 786440 | tf_op jit(solution)/shard_map/ppermute | solution.py:395
  90.7 16.0 %collective-permute-start.11 = (bf16[512,128]{1,0:T(8,128)(2,1)S(1)}, bf16[512,128]{1,0:T(8,128)(2,1)S(1)}, u32[]{:S(2)}, u32[]{:S(2)}) collective-permute-start(bf16[512,128]{1,0:T(8,128)(2,1)S(1)} %get-tuple-element.34.query_ref), channel_id=1, source_target_pairs={{4,0},{8,4},{12,8},{5,1},{9,5},{13,9},{6,2},{10,6},{14,10},{7,3},{... | collective-permute-start | bytes 393224 | tf_op jit(solution)/shard_map/ppermute | solution.py:395
  93.8 16.6 %collective-permute-start.12 = (bf16[512,128]{1,0:T(8,128)(2,1)S(1)}, bf16[512,128]{1,0:T(8,128)(2,1)S(1)}, u32[]{:S(2)}, u32[]{:S(2)}) collective-permute-start(bf16[512,128]{1,0:T(8,128)(2,1)S(1)} %get-tuple-element.34.query_ref), channel_id=1, source_target_pairs={{8,0},{12,4},{9,1},{13,5},{10,2},{14,6},{11,3},{15,7},{24,16},{28,... | collective-permute-start | bytes 393224 | tf_op jit(solution)/shard_map/ppermute | solution.py:395
  103.4 7.0 %collective-permute-start.13 = (bf16[512,128]{1,0:T(8,128)(2,1)S(1)}, bf16[512,128]{1,0:T(8,128)(2,1)S(1)}, u32[]{:S(2)}, u32[]{:S(2)}) collective-permute-start(bf16[512,128]{1,0:T(8,128)(2,1)S(1)} %get-tuple-element.41.mixed_ref), channel_id=1, source_target_pairs={{8,0},{12,4},{9,1},{13,5},{10,2},{14,6},{11,3},{15,7},{24,16},{28,... | collective-permute-start | bytes 393224 | tf_op jit(solution)/shard_map/ppermute | solution.py:395
  104.7 5.7 %collective-permute-start.14 = (bf16[512,128]{1,0:T(8,128)(2,1)S(1)}, bf16[512,128]{1,0:T(8,128)(2,1)S(1)}, u32[]{:S(2)}, u32[]{:S(2)}) collective-permute-start(bf16[512,128]{1,0:T(8,128)(2,1)S(1)} %get-tuple-element.41.mixed_ref), channel_id=1, source_target_pairs={{4,0},{8,4},{12,8},{5,1},{9,5},{13,9},{6,2},{10,6},{14,10},{7,3},{... | collective-permute-start | bytes 393224 | tf_op jit(solution)/shard_map/ppermute | solution.py:395
  113.1 69.6 %all-to-all-start.1 = ((bf16[128,16,256]{2,1,0:T(8,128)(2,1)}), bf16[128,16,256]{2,1,0:T(8,128)(2,1)S(1)}, u32[]{:S(2)}, u32[]{:S(2)}) async-start(bf16[128,16,256]{2,1,0:T(8,128)(2,1)} %bitcast.3), calls=%async_computation.1 | async-start | bytes 2097152 | tf_op jit(solution)/shard_map/all_to_all | solution.py:389
  123.4 57.7 %collective-permute-start.8 = (bf16[128,128]{1,0:T(8,128)(2,1)S(1)}, bf16[128,128]{1,0:T(8,128)(2,1)S(1)}, u32[]{:S(2)}, u32[]{:S(2)}) collective-permute-start(bf16[128,128]{1,0:T(8,128)(2,1)S(1)} %get-tuple-element.37), channel_id=1, source_target_pairs={{0,2},{1,3},{2,0},{3,1},{4,6},{5,7},{6,4},{7,5},{8,10},{9,11},{10,... | collective-permute-start | bytes 98312 | tf_op jit(solution)/shard_map/ppermute | solution.py:400
  134.3 48.3 %collective-permute-start.9 = (bf16[128,128]{1,0:T(8,128)(2,1)S(1)}, bf16[128,128]{1,0:T(8,128)(2,1)S(1)}, u32[]{:S(2)}, u32[]{:S(2)}) collective-permute-start(bf16[128,128]{1,0:T(8,128)(2,1)S(1)} %get-tuple-element.38), channel_id=1, source_target_pairs={{0,3},{1,2},{2,1},{3,0},{4,7},{5,6},{6,5},{7,4},{8,11},{9,10},{10,... | collective-permute-start | bytes 98312 | tf_op jit(solution)/shard_map/ppermute | solution.py:400
  137.9 44.7 %collective-permute-start.10 = (bf16[128,128]{1,0:T(8,128)(2,1)S(1)}, bf16[128,128]{1,0:T(8,128)(2,1)S(1)}, u32[]{:S(2)}, u32[]{:S(2)}) collective-permute-start(bf16[128,128]{1,0:T(8,128)(2,1)S(1)} %get-tuple-element.39), channel_id=1, source_target_pairs={{0,1},{1,0},{2,3},{3,2},{4,5},{5,4},{6,7},{7,6},{8,9},{9,8},{10,11... | collective-permute-start | bytes 98312 | tf_op jit(solution)/shard_map/ppermute | solution.py:400

commit v7 on v5

--- a/solution.py
+++ b/solution.py
@@ -127,8 +127,8 @@
     return low
 
 
-def side_kernel(lengths_ref, dest_ref, grad_ref, *out_refs):
-    *out_refs, home_ref, low_ref, low_rows_ref = out_refs
+def plan_kernel(lengths_ref, dest_ref, side_ref, home_ref, low_ref, low_rows_ref):
+    del side_ref
     bounds = user_bounds(lengths_ref)
     base = lax.axis_index("x") * PART
     low_ref[...] = first_key(base + iota(low_ref.shape, 0), bounds)
@@ -137,6 +137,9 @@
     earlier = (across == down) & (iota((ROWS, ROWS), 1) < iota((ROWS, ROWS), 0))
     rank = jnp.sum(jnp.where(earlier, 1.0, 0.0), axis=1, keepdims=True)
     home_ref[...] = pick_down((down[:, 0:1] * CAP + rank).astype(jnp.int32))
+
+
+def side_kernel(dest_ref, grad_ref, *out_refs):
     group = lax.axis_index("dp")
     mapping = dest_ref[...]
     landing = lax.shift_right_logical(mapping, 7) == group
@@ -419,14 +422,17 @@
         flops=2 * 256 * 128 * 2048, nbytes=3 << 19,
         hbm_in=(1,), hbm_out=True, limit=62 * 1024 * 1024,
     )
-    *side_out, home, low, low_rows = call(
-        side_kernel,
-        [shape(ROWS + CHUNK, HEAD_DIM)] * HEADS
-        + [
+    side_out = call(
+        side_kernel, [shape(ROWS + CHUNK, HEAD_DIM)] * HEADS, (mapping, grad_out),
+        nbytes=3 << 17,
+    )
+    home, low, low_rows = call(
+        plan_kernel,
+        [
             shape(2 * ROWS, N_DP * CHUNK), shape(PART, ROWS, dtype=jnp.int32),
             shape(8, (REACH + 1) * PART, dtype=jnp.int32),
         ],
-        (lengths, mapping, grad_out), smem=(0,), nbytes=3 << 17,
+        (lengths, mapping, side_out[0]), smem=(0,), nbytes=3 << 17,
     )
     side = swap_heads(side_out)
     arrived = route(packed)

time: 182 us -> 182 us (level)
    pallas_call x7 -> x8, Pallas kernels: 14.3 us -> 14.6 us  [call(): pl.pallas_call(kernel, out_shape=outs, in_specs=[pl.BlockSpec(memory_spac...]
where the time goes in v7:
time: 182 us; the launch traced here: 181 us
  waiting for transfers between devices  88.7 us (49%)
  starting transfers between devices  77.1 us (42%)
  Pallas kernels  14.6 us (8%)
    ppermute x6, waiting for transfers between devices, swap_heads(): lax.ppermute(pieces[k], 'h', [(i, i ^ k) for i in range(HEADS)])  85.6 us
    ppermute x6, starting transfers between devices, swap_heads(): lax.ppermute(pieces[k], 'h', [(i, i ^ k) for i in range(HEADS)])  32.9 us
    all_to_all x2, starting transfers between devices, route(): moved = lax.all_to_all(flat, ('dp', 'h'), 0, 0, tiled=True)  30.1 us
    pallas_call x8, Pallas kernels, call(): pl.pallas_call(kernel, out_shape=outs, in_specs=[pl.BlockSpec(memory_spac...  14.6 us
    ppermute x6, starting transfers between devices, from_quarter(): return lax.ppermute(array, 'x', pairs)  14.1 us
  transfers between devices with their start and end apart: 14, of which 5 were waited for; matrix products, arithmetic and copies ran while one was open for 0% of the time, Pallas kernels for 4%

profile of v7, /device:TPU:37, one launch (start us, length us, event | category | flops | bytes accessed | tf_op | source)
XLA Modules:
  0.0 181.3 jit_solution(10677596961468823124)
XLA Ops:
  0.6 3.1 %pack_kernel.1 = bf16[32,4,16,256]{3,2,1,0:T(8,128)(2,1)} custom-call(s32[32,128]{1,0:T(8,128)} %bitcast.7, bf16[128,2048]{1,0:T(8,128)(2,1)} %proj_ref.1), custom_call_target="tpu_custom_call" | custom-call | flops 134217728 | bytes 1572864 | tf_op jit(solution)/shard_map/pack_kernel/pallas_call | solution.py:50
  3.7 19.6 %all-to-all-start = ((bf16[128,16,256]{2,1,0:T(8,128)(2,1)}), bf16[128,16,256]{2,1,0:T(8,128)(2,1)S(1)}, u32[]{:S(2)}, u32[]{:S(2)}) async-start(bf16[128,16,256]{2,1,0:T(8,128)(2,1)} %bitcast.10), calls=%async_computation | async-start | bytes 2097152 | tf_op jit(solution)/shard_map/all_to_all | solution.py:395
  23.9 10.9 %collective-permute-start = (bf16[144,128]{1,0:T(8,128)(2,1)S(1)}, bf16[144,128]{1,0:T(8,128)(2,1)S(1)}, u32[]{:S(2)}, u32[]{:S(2)}) collective-permute-start(bf16[144,128]{1,0:T(8,128)(2,1)S(1)} %get-tuple-element.28), channel_id=1, source_target_pairs={{0,2},{1,3},{2,0},{3,1},{4,6},{5,7},{6,4},{7,5},{8,10},{9,11},{10,... | collective-permute-start | bytes 110600 | tf_op jit(solution)/shard_map/ppermute | solution.py:406
  34.8 3.6 %collective-permute-start.1 = (bf16[144,128]{1,0:T(8,128)(2,1)S(1)}, bf16[144,128]{1,0:T(8,128)(2,1)S(1)}, u32[]{:S(2)}, u32[]{:S(2)}) collective-permute-start(bf16[144,128]{1,0:T(8,128)(2,1)S(1)} %get-tuple-element.29), channel_id=1, source_target_pairs={{0,3},{1,2},{2,1},{3,0},{4,7},{5,6},{6,5},{7,4},{8,11},{9,10},{10,... | collective-permute-start | bytes 110600 | tf_op jit(solution)/shard_map/ppermute | solution.py:406
  38.5 1.9 %collective-permute-start.2 = (bf16[144,128]{1,0:T(8,128)(2,1)S(1)}, bf16[144,128]{1,0:T(8,128)(2,1)S(1)}, u32[]{:S(2)}, u32[]{:S(2)}) collective-permute-start(bf16[144,128]{1,0:T(8,128)(2,1)S(1)} %get-tuple-element.30), channel_id=1, source_target_pairs={{0,1},{1,0},{2,3},{3,2},{4,5},{5,4},{6,7},{7,6},{8,9},{9,8},{10,11... | collective-permute-start | bytes 110600 | tf_op jit(solution)/shard_map/ppermute | solution.py:406
  40.4 40.8 %collective-permute-done.s2 = bf16[144,128]{1,0:T(8,128)(2,1)S(1)} collective-permute-done((bf16[144,128]{1,0:T(8,128)(2,1)S(1)}, bf16[144,128]{1,0:T(8,128)(2,1)S(1)}, u32[]{:S(2)}, u32[]{:S(2)}) %collective-permute-start) | collective-permute-done | bytes 36896 | tf_op jit(solution)/shard_map/ppermute | solution.py:406
  81.2 2.0 %collective-permute-done.1.s3 = bf16[144,128]{1,0:T(8,128)(2,1)S(1)} collective-permute-done((bf16[144,128]{1,0:T(8,128)(2,1)S(1)}, bf16[144,128]{1,0:T(8,128)(2,1)S(1)}, u32[]{:S(2)}, u32[]{:S(2)}) %collective-permute-start.1) | collective-permute-done | bytes 36896 | tf_op jit(solution)/shard_map/ppermute | solution.py:406
  83.9 2.8 %collective-permute-start.3 = (bf16[512,256]{1,0:T(8,128)(2,1)S(1)}, bf16[512,256]{1,0:T(8,128)(2,1)S(1)}, u32[]{:S(2)}, u32[]{:S(2)}) collective-permute-start(bf16[512,256]{1,0:T(8,128)(2,1)S(1)} %get-tuple-element.33.vk0_ref.vk_ref), channel_id=1, source_target_pairs={{0,4},{4,8},{8,12},{1,5},{5,9},{9,13},{2,6},{6,10},{10,14},{3,7},{... | collective-permute-start | bytes 786440 | tf_op jit(solution)/shard_map/ppermute | solution.py:401
  86.7 1.3 collective-permute-start.4
  88.9 3.1 %collective-permute-start.8 = (bf16[512,128]{1,0:T(8,128)(2,1)S(1)}, bf16[512,128]{1,0:T(8,128)(2,1)S(1)}, u32[]{:S(2)}, u32[]{:S(2)}) collective-permute-start(bf16[512,128]{1,0:T(8,128)(2,1)S(1)} %get-tuple-element.32.query_ref), channel_id=1, source_target_pairs={{4,0},{8,4},{12,8},{5,1},{9,5},{13,9},{6,2},{10,6},{14,10},{7,3},{... | collective-permute-start | bytes 393224 | tf_op jit(solution)/shard_map/ppermute | solution.py:401
  92.1 3.7 %collective-permute-start.9 = (bf16[512,128]{1,0:T(8,128)(2,1)S(1)}, bf16[512,128]{1,0:T(8,128)(2,1)S(1)}, u32[]{:S(2)}, u32[]{:S(2)}) collective-permute-start(bf16[512,128]{1,0:T(8,128)(2,1)S(1)} %get-tuple-element.32.query_ref), channel_id=1, source_target_pairs={{8,0},{12,4},{9,1},{13,5},{10,2},{14,6},{11,3},{15,7},{24,16},{28,... | collective-permute-start | bytes 393224 | tf_op jit(solution)/shard_map/ppermute | solution.py:401
  95.8 3.1 %collective-permute-done.4.vk2_ref = bf16[512,256]{1,0:T(8,128)(2,1)S(1)} collective-permute-done((bf16[512,256]{1,0:T(8,128)(2,1)S(1)}, bf16[512,256]{1,0:T(8,128)(2,1)S(1)}, u32[]{:S(2)}, u32[]{:S(2)}) %collective-permute-start.4) | collective-permute-done | bytes 262176 | tf_op jit(solution)/shard_map/ppermute | solution.py:401
  98.8 1.8 forward_kernel.1
  100.6 1.3 collective-permute-start.10
  101.9 1.9 %collective-permute-start.11 = (bf16[512,128]{1,0:T(8,128)(2,1)S(1)}, bf16[512,128]{1,0:T(8,128)(2,1)S(1)}, u32[]{:S(2)}, u32[]{:S(2)}) collective-permute-start(bf16[512,128]{1,0:T(8,128)(2,1)S(1)} %get-tuple-element.39.mixed_ref), channel_id=1, source_target_pairs={{4,0},{8,4},{12,8},{5,1},{9,5},{13,9},{6,2},{10,6},{14,10},{7,3},{... | collective-permute-start | bytes 393224 | tf_op jit(solution)/shard_map/ppermute | solution.py:401
  103.9 3.8 %query_grad_kernel.1 = (bf16[32,4,16,128]{3,2,1,0:T(8,128)(2,1)S(1)}, f32[2,512,128]{2,1,0:T(8,128)S(1)}, bf16[4,512,256]{2,1,0:T(8,128)(2,1)S(1)}, bf16[2,512,256]{2,1,0:T(8,128)(2,1)S(1)}, f32[2,512,256]{2,1,0:T(8,128)S(1)}) custom-call(s32[512,128]{1,0:T(8,128)S(1)} %get-tuple-element.27.low_ref, s32[8,1536]{1,0:T(8,128)S(1)} %get-tuple-element.38.low_rows_ref, ...), custom_call_target="tpu_custom_call" | custom-call | flops 536870912 | bytes 2097152 | tf_op jit(solution)/shard_map/query_grad_kernel/pallas_call | solution.py:50
  107.6 2.6 %backward_kernel.1 = bf16[32,4,16,256]{3,2,1,0:T(8,128)(2,1)} custom-call(s32[8,1536]{1,0:T(8,128)S(1)} %get-tuple-element.38.low_rows_ref, bf16[4,512,256]{2,1,0:T(8,128)(2,1)S(1)} %get-tuple-element.41.picks_ref, bf16[512,256]{1,0:T(8,128)(2,1)S(1)} %get-tuple-element.33.vk0_ref.vk_ref, bf16[512,128]{1,0:T(8,128)(2,1)S(1)} %collective-permute-done.9.q2_ref, ...), custom_call_target="tpu_custom_call" | custom-call | flops 1073741824 | bytes 3145728 | tf_op jit(solution)/shard_map/backward_kernel/pallas_call | solution.py:50
  110.3 10.5 %all-to-all-start.1 = ((bf16[128,16,256]{2,1,0:T(8,128)(2,1)}), bf16[128,16,256]{2,1,0:T(8,128)(2,1)S(1)}, u32[]{:S(2)}, u32[]{:S(2)}) async-start(bf16[128,16,256]{2,1,0:T(8,128)(2,1)} %bitcast.3), calls=%async_computation.1 | async-start | bytes 2097152 | tf_op jit(solution)/shard_map/all_to_all | solution.py:395
  120.8 10.9 %collective-permute-start.5 = (bf16[128,128]{1,0:T(8,128)(2,1)S(1)}, bf16[128,128]{1,0:T(8,128)(2,1)S(1)}, u32[]{:S(2)}, u32[]{:S(2)}) collective-permute-start(bf16[128,128]{1,0:T(8,128)(2,1)S(1)} %get-tuple-element.35), channel_id=1, source_target_pairs={{0,2},{1,3},{2,0},{3,1},{4,6},{5,7},{6,4},{7,5},{8,10},{9,11},{10,... | collective-permute-start | bytes 98312 | tf_op jit(solution)/shard_map/ppermute | solution.py:406
  131.7 3.6 %collective-permute-start.6 = (bf16[128,128]{1,0:T(8,128)(2,1)S(1)}, bf16[128,128]{1,0:T(8,128)(2,1)S(1)}, u32[]{:S(2)}, u32[]{:S(2)}) collective-permute-start(bf16[128,128]{1,0:T(8,128)(2,1)S(1)} %get-tuple-element.36), channel_id=1, source_target_pairs={{0,3},{1,2},{2,1},{3,0},{4,7},{5,6},{6,5},{7,4},{8,11},{9,10},{10,... | collective-permute-start | bytes 98312 | tf_op jit(solution)/shard_map/ppermute | solution.py:406
  135.3 1.9 %collective-permute-start.7 = (bf16[128,128]{1,0:T(8,128)(2,1)S(1)}, bf16[128,128]{1,0:T(8,128)(2,1)S(1)}, u32[]{:S(2)}, u32[]{:S(2)}) collective-permute-start(bf16[128,128]{1,0:T(8,128)(2,1)S(1)} %get-tuple-element.37), channel_id=1, source_target_pairs={{0,1},{1,0},{2,3},{3,2},{4,5},{5,4},{6,7},{7,6},{8,9},{9,8},{10,11... | collective-permute-start | bytes 98312 | tf_op jit(solution)/shard_map/ppermute | solution.py:406
  137.2 41.2 %collective-permute-done.5.l2 = bf16[128,128]{1,0:T(8,128)(2,1)S(1)} collective-permute-done((bf16[128,128]{1,0:T(8,128)(2,1)S(1)}, bf16[128,128]{1,0:T(8,128)(2,1)S(1)}, u32[]{:S(2)}, u32[]{:S(2)}) %collective-permute-start.5) | collective-permute-done | bytes 32800 | tf_op jit(solution)/shard_map/ppermute | solution.py:406
  178.4 1.6 collective-permute-done.6.l3
  180.0 1.3 finish_kernel.1
  (18 shorter events, 2.1 us)
Async XLA Ops:
  3.7 19.7 %copy-start = (s32[1,4096]{1,0:T(1,128)S(1)}, s32[1,4096]{1,0:T(1,128)}, u32[]{:S(2)}) copy-start(s32[1,4096]{1,0:T(1,128)} %param.5) | copy-start | bytes 49156
  3.7 19.7 %copy-start.1 = (bf16[128,512]{1,0:T(8,128)(2,1)S(1)}, bf16[128,512]{1,0:T(8,128)(2,1)}, u32[]{:S(2)}) copy-start(bf16[128,512]{1,0:T(8,128)(2,1)} %grad_ref.1) | copy-start | bytes 393220
  3.7 79.5 %all-to-all-start = ((bf16[128,16,256]{2,1,0:T(8,128)(2,1)}), bf16[128,16,256]{2,1,0:T(8,128)(2,1)S(1)}, u32[]{:S(2)}, u32[]{:S(2)}) async-start(bf16[128,16,256]{2,1,0:T(8,128)(2,1)} %bitcast.10), calls=%async_computation | async-start | bytes 2097152 | tf_op jit(solution)/shard_map/all_to_all | solution.py:395
  23.9 57.3 %collective-permute-start = (bf16[144,128]{1,0:T(8,128)(2,1)S(1)}, bf16[144,128]{1,0:T(8,128)(2,1)S(1)}, u32[]{:S(2)}, u32[]{:S(2)}) collective-permute-start(bf16[144,128]{1,0:T(8,128)(2,1)S(1)} %get-tuple-element.28), channel_id=1, source_target_pairs={{0,2},{1,3},{2,0},{3,1},{4,6},{5,7},{6,4},{7,5},{8,10},{9,11},{10,... | collective-permute-start | bytes 110600 | tf_op jit(solution)/shard_map/ppermute | solution.py:406
  34.8 48.4 %collective-permute-start.1 = (bf16[144,128]{1,0:T(8,128)(2,1)S(1)}, bf16[144,128]{1,0:T(8,128)(2,1)S(1)}, u32[]{:S(2)}, u32[]{:S(2)}) collective-permute-start(bf16[144,128]{1,0:T(8,128)(2,1)S(1)} %get-tuple-element.29), channel_id=1, source_target_pairs={{0,3},{1,2},{2,1},{3,0},{4,7},{5,6},{6,5},{7,4},{8,11},{9,10},{10,... | collective-permute-start | bytes 110600 | tf_op jit(solution)/shard_map/ppermute | solution.py:406
  38.5 44.7 %collective-permute-start.2 = (bf16[144,128]{1,0:T(8,128)(2,1)S(1)}, bf16[144,128]{1,0:T(8,128)(2,1)S(1)}, u32[]{:S(2)}, u32[]{:S(2)}) collective-permute-start(bf16[144,128]{1,0:T(8,128)(2,1)S(1)} %get-tuple-element.30), channel_id=1, source_target_pairs={{0,1},{1,0},{2,3},{3,2},{4,5},{5,4},{6,7},{7,6},{8,9},{9,8},{10,11... | collective-permute-start | bytes 110600 | tf_op jit(solution)/shard_map/ppermute | solution.py:406
  83.9 4.1 %copy-start.2 = (s32[1,3]{1,0:T(1,128)S(1)}, s32[1,3]{1,0:T(1,128)}, u32[]{:S(2)}) copy-start(s32[1,3]{1,0:T(1,128)} %lengths_ref.1) | copy-start | bytes 40
  83.9 11.9 %collective-permute-start.3 = (bf16[512,256]{1,0:T(8,128)(2,1)S(1)}, bf16[512,256]{1,0:T(8,128)(2,1)S(1)}, u32[]{:S(2)}, u32[]{:S(2)}) collective-permute-start(bf16[512,256]{1,0:T(8,128)(2,1)S(1)} %get-tuple-element.33.vk0_ref.vk_ref), channel_id=1, source_target_pairs={{0,4},{4,8},{8,12},{1,5},{5,9},{9,13},{2,6},{6,10},{10,14},{3,7},{... | collective-permute-start | bytes 786440 | tf_op jit(solution)/shard_map/ppermute | solution.py:401
  86.7 12.1 %collective-permute-start.4 = (bf16[512,256]{1,0:T(8,128)(2,1)S(1)}, bf16[512,256]{1,0:T(8,128)(2,1)S(1)}, u32[]{:S(2)}, u32[]{:S(2)}) collective-permute-start(bf16[512,256]{1,0:T(8,128)(2,1)S(1)} %get-tuple-element.33.vk0_ref.vk_ref), channel_id=1, source_target_pairs={{0,8},{4,12},{1,9},{5,13},{2,10},{6,14},{3,11},{7,15},{16,24},{20,... | collective-permute-start | bytes 786440 | tf_op jit(solution)/shard_map/ppermute | solution.py:401
  88.9 14.9 %collective-permute-start.8 = (bf16[512,128]{1,0:T(8,128)(2,1)S(1)}, bf16[512,128]{1,0:T(8,128)(2,1)S(1)}, u32[]{:S(2)}, u32[]{:S(2)}) collective-permute-start(bf16[512,128]{1,0:T(8,128)(2,1)S(1)} %get-tuple-element.32.query_ref), channel_id=1, source_target_pairs={{4,0},{8,4},{12,8},{5,1},{9,5},{13,9},{6,2},{10,6},{14,10},{7,3},{... | collective-permute-start | bytes 393224 | tf_op jit(solution)/shard_map/ppermute | solution.py:401
  92.1 15.6 %collective-permute-start.9 = (bf16[512,128]{1,0:T(8,128)(2,1)S(1)}, bf16[512,128]{1,0:T(8,128)(2,1)S(1)}, u32[]{:S(2)}, u32[]{:S(2)}) collective-permute-start(bf16[512,128]{1,0:T(8,128)(2,1)S(1)} %get-tuple-element.32.query_ref), channel_id=1, source_target_pairs={{8,0},{12,4},{9,1},{13,5},{10,2},{14,6},{11,3},{15,7},{24,16},{28,... | collective-permute-start | bytes 393224 | tf_op jit(solution)/shard_map/ppermute | solution.py:401
  100.6 7.0 %collective-permute-start.10 = (bf16[512,128]{1,0:T(8,128)(2,1)S(1)}, bf16[512,128]{1,0:T(8,128)(2,1)S(1)}, u32[]{:S(2)}, u32[]{:S(2)}) collective-permute-start(bf16[512,128]{1,0:T(8,128)(2,1)S(1)} %get-tuple-element.39.mixed_ref), channel_id=1, source_target_pairs={{8,0},{12,4},{9,1},{13,5},{10,2},{14,6},{11,3},{15,7},{24,16},{28,... | collective-permute-start | bytes 393224 | tf_op jit(solution)/shard_map/ppermute | solution.py:401
  101.9 5.7 %collective-permute-start.11 = (bf16[512,128]{1,0:T(8,128)(2,1)S(1)}, bf16[512,128]{1,0:T(8,128)(2,1)S(1)}, u32[]{:S(2)}, u32[]{:S(2)}) collective-permute-start(bf16[512,128]{1,0:T(8,128)(2,1)S(1)} %get-tuple-element.39.mixed_ref), channel_id=1, source_target_pairs={{4,0},{8,4},{12,8},{5,1},{9,5},{13,9},{6,2},{10,6},{14,10},{7,3},{... | collective-permute-start | bytes 393224 | tf_op jit(solution)/shard_map/ppermute | solution.py:401
  110.3 69.8 %all-to-all-start.1 = ((bf16[128,16,256]{2,1,0:T(8,128)(2,1)}), bf16[128,16,256]{2,1,0:T(8,128)(2,1)S(1)}, u32[]{:S(2)}, u32[]{:S(2)}) async-start(bf16[128,16,256]{2,1,0:T(8,128)(2,1)} %bitcast.3), calls=%async_computation.1 | async-start | bytes 2097152 | tf_op jit(solution)/shard_map/all_to_all | solution.py:395
  120.8 57.7 %collective-permute-start.5 = (bf16[128,128]{1,0:T(8,128)(2,1)S(1)}, bf16[128,128]{1,0:T(8,128)(2,1)S(1)}, u32[]{:S(2)}, u32[]{:S(2)}) collective-permute-start(bf16[128,128]{1,0:T(8,128)(2,1)S(1)} %get-tuple-element.35), channel_id=1, source_target_pairs={{0,2},{1,3},{2,0},{3,1},{4,6},{5,7},{6,4},{7,5},{8,10},{9,11},{10,... | collective-permute-start | bytes 98312 | tf_op jit(solution)/shard_map/ppermute | solution.py:406
  131.7 48.3 %collective-permute-start.6 = (bf16[128,128]{1,0:T(8,128)(2,1)S(1)}, bf16[128,128]{1,0:T(8,128)(2,1)S(1)}, u32[]{:S(2)}, u32[]{:S(2)}) collective-permute-start(bf16[128,128]{1,0:T(8,128)(2,1)S(1)} %get-tuple-element.36), channel_id=1, source_target_pairs={{0,3},{1,2},{2,1},{3,0},{4,7},{5,6},{6,5},{7,4},{8,11},{9,10},{10,... | collective-permute-start | bytes 98312 | tf_op jit(solution)/shard_map/ppermute | solution.py:406
  135.3 44.7 %collective-permute-start.7 = (bf16[128,128]{1,0:T(8,128)(2,1)S(1)}, bf16[128,128]{1,0:T(8,128)(2,1)S(1)}, u32[]{:S(2)}, u32[]{:S(2)}) collective-permute-start(bf16[128,128]{1,0:T(8,128)(2,1)S(1)} %get-tuple-element.37), channel_id=1, source_target_pairs={{0,1},{1,0},{2,3},{3,2},{4,5},{5,4},{6,7},{7,6},{8,9},{9,8},{10,11... | collective-permute-start | bytes 98312 | tf_op jit(solution)/shard_map/ppermute | solution.py:406
